TPU v7x, 256 devices: a whole 4x4x8 slice. The times are simulated.
256 devices in a mesh: wa: 16 (over x, z_hi, core), tu: 4 (over y), tv: 4 (over z_lo).
Axes of the slice: x: 4, y: 4, z: 8 (z_hi: 2, z_lo: 4; z = z_hi * 4 + z_lo), core: 2. Of those that a mesh axis runs over, the one named last changes fastest.
Arguments:
- kernel_u: bfloat16 [4096, 256, 128], P(('wa', 'tu', 'tv')), may hold values from -0.5 to 0.5
- kernel_v: bfloat16 [4096, 256, 128], P(('wa', 'tu', 'tv')), may hold values from -0.5 to 0.5
- visibilities: bfloat16 [4096, 2, 256], P(('wa', 'tu', 'tv')), may hold values from -6 to 6
- vis_count: int32 [4096], P(('wa', 'tu', 'tv')), may hold values from 1 to 256
- tile_route: int32 [4096, 1], P(('wa', 'tu', 'tv')), may hold values from 0 to 15; in each aligned block of 16 rows (0 to 15, 16 to 31, ...) at most 2 rows name the same one
- block_offset: int32 [4096, 2], P(('wa', 'tu', 'tv')), may hold values from 0 to 896
- plane_w: float32 [16], P('wa'), may hold values from -300 to 300
Outputs:
- image: float32 [4096, 4096], P('wa', ('tu', 'tv'))
Inputs may be any that keep to these rules, and one draw needn't show every extreme that they name: `tile_route`: of the 16 blocks entering one device (aligned blocks of rows), at most 2 go to the same uv tile, and exactly 2 go to one tile from some device. `block_offset`: A block's subgrid lies inside its tile.
All inputs are finite; a program needn't handle non-finite values.
Results may differ from a plain program's by a relative error of at most 0.025.
Values may be sent and summed in bfloat16 or wider, within the bound.
No kernel may reach another device: no remote copies, remote signals or barrier semaphores. Data moves between devices by JAX's collectives and lax.ppermute only.
A program may use at most 64 MiB of HBM per device.

v0:
```python
import math

import jax
import jax.numpy as jnp
from jax import lax
from jax.sharding import PartitionSpec as P

N = 8192
P_SIZE = 64


field_half = 0.25


def first_table(q_len, r_len):
    q_idx = jnp.arange(q_len, dtype=jnp.int32)
    c_idx = jnp.arange(r_len, dtype=jnp.int32)
    angles = (q_idx[:, None] * c_idx[None, :] % r_len).astype(jnp.float32) * (2.0 * math.pi / r_len)
    cosine = jnp.cos(angles)
    sine_part = jnp.sin(angles)
    real_in = jnp.stack([cosine, sine_part], axis=1)
    imag_in = jnp.stack([-sine_part, cosine], axis=1)
    return jnp.stack([real_in, imag_in], axis=0).astype(jnp.bfloat16)


def twiddle_parts(p_len, r_len):
    p_idx = jnp.arange(p_len, dtype=jnp.int32)
    c_idx = jnp.arange(r_len, dtype=jnp.int32)
    angles = (p_idx[:, None] * c_idx[None, :]).astype(jnp.float32) * (2.0 * math.pi / N)
    return (jnp.cos(angles), jnp.sin(angles))


def last_table(p_len, e_vals):
    p_idx = jnp.arange(p_len, dtype=jnp.int32)
    angles = (p_idx[:, None] * e_vals[None, :] % p_len).astype(jnp.float32) * (
        2.0 * math.pi / p_len
    )
    cosine = jnp.cos(angles)
    sine_part = jnp.sin(angles)
    real_in = jnp.stack([cosine, sine_part], axis=2)
    imag_in = jnp.stack([-sine_part, cosine], axis=2)
    return jnp.stack([real_in, imag_in], axis=1).astype(jnp.bfloat16)


def rotate(values, cos_t, sin_t, axis):
    real_part = lax.index_in_dim(values, 0, axis, keepdims=False).astype(jnp.float32)
    imag_part = lax.index_in_dim(values, 1, axis, keepdims=False).astype(jnp.float32)
    rotated = jnp.stack(
        [real_part * cos_t - imag_part * sin_t, real_part * sin_t + imag_part * cos_t], axis=axis
    )
    return rotated.astype(jnp.bfloat16)


def screen_parts(row_ids, col_ids, w_value):
    half_n = N // 2
    cell_size = 2.0 * field_half / N
    dir_l = ((row_ids + half_n) % N - half_n).astype(jnp.float32) * cell_size
    dir_m = ((col_ids + half_n) % N - half_n).astype(jnp.float32) * cell_size
    n_lift = jnp.sqrt(1.0 - dir_l[:, None] ** 2 - dir_m[None, :] ** 2) - 1.0
    quarter = ((row_ids[:, None] + col_ids[None, :]) % 4).astype(jnp.float32)
    angles = 2.0 * math.pi * w_value * n_lift - 0.5 * math.pi * quarter
    return (jnp.cos(angles), jnp.sin(angles))


def weighted_subgrids(vis_masked, ku_slots, kv_slots):
    weighted = (
        vis_masked.astype(jnp.float32)[:, :, :, None] * ku_slots.astype(jnp.float32)[:, None, :, :]
    ).astype(jnp.bfloat16)
    sub_grids = jnp.einsum("nxcs,nct->nxst", weighted, kv_slots, preferred_element_type=jnp.float32)
    return sub_grids.astype(jnp.bfloat16)


def body(kernel_u, kernel_v, visibilities, vis_count, tile_route, block_offset, plane_w):
    tile_count = lax.axis_size("tu") * lax.axis_size("tv")
    block_count = kernel_u.shape[0]
    slot_count = kernel_u.shape[1]
    capacity = max(2, 2 * block_count // tile_count)
    tile_u = N // 2 // lax.axis_size("tu")
    tile_v = N // 2 // lax.axis_size("tv")
    q_len = N // 2 // P_SIZE
    r_len = N // P_SIZE
    target = tile_route[:, 0]
    tile_hits = (target[:, None] == jnp.arange(tile_count, dtype=jnp.int32)[None, :]).astype(
        jnp.int32
    )
    earlier = jnp.cumsum(tile_hits, axis=0) - tile_hits
    slot_rank = jnp.sum(earlier * tile_hits, axis=1)
    slot_of = target * capacity + slot_rank
    slot_match = slot_of[None, :] == jnp.arange(tile_count * capacity, dtype=jnp.int32)[:, None]
    source = jnp.sum(
        slot_match.astype(jnp.int32) * jnp.arange(block_count, dtype=jnp.int32)[None, :], axis=1
    )
    filled = jnp.any(slot_match, axis=1)
    live_mask = jnp.arange(slot_count, dtype=jnp.int32)[None, :] < vis_count[:, None]
    masked = jnp.where(live_mask[:, None, :], visibilities, jnp.zeros_like(visibilities))
    offsets = jnp.where(
        filled[:, None], jnp.take(block_offset, source, axis=0), jnp.zeros((), jnp.int32)
    )
    slot_vis = jnp.take(masked, source, axis=0)
    slot_vis = jnp.where(filled[:, None, None], slot_vis, jnp.zeros_like(slot_vis))
    slot_ku = jnp.take(kernel_u, source, axis=0)
    slot_kv = jnp.take(kernel_v, source, axis=0)
    got_ku, got_kv, got_vis, got_off = (
        lax.all_to_all(slot_ku, ("tu", "tv"), split_axis=0, concat_axis=0, tiled=True),
        lax.all_to_all(slot_kv, ("tu", "tv"), split_axis=0, concat_axis=0, tiled=True),
        lax.all_to_all(slot_vis, ("tu", "tv"), split_axis=0, concat_axis=0, tiled=True),
        lax.all_to_all(offsets, ("tu", "tv"), split_axis=0, concat_axis=0, tiled=True),
    )
    sub_grids = weighted_subgrids(got_vis, got_ku, got_kv)
    numbers = lax.ScatterDimensionNumbers(
        update_window_dims=(1, 2, 3), inserted_window_dims=(), scatter_dims_to_operand_dims=(1, 2)
    )
    uv_grid = lax.scatter_add(
        jnp.zeros((2, tile_u, tile_v), jnp.float32),
        got_off.astype(jnp.int32),
        sub_grids.astype(jnp.float32),
        numbers,
        indices_are_sorted=False,
        unique_indices=False,
        mode=lax.GatherScatterMode.PROMISE_IN_BOUNDS,
    )
    tile_grid = uv_grid.astype(jnp.bfloat16)
    grid_rows = lax.all_to_all(tile_grid, "tv", split_axis=1, concat_axis=2, tiled=True)
    pencil_rows = grid_rows.shape[1]
    table_one = first_table(q_len, r_len)
    tw_cos, tw_sin = twiddle_parts(P_SIZE, r_len)
    table_two = last_table(P_SIZE, jnp.arange(P_SIZE // 2, dtype=jnp.int32))
    spread = grid_rows.reshape(2, pencil_rows, q_len, P_SIZE)
    first_pass = jnp.einsum(
        "xuqp,xqyc->upyc", spread, table_one, preferred_element_type=jnp.float32
    ).astype(jnp.bfloat16)
    turned = rotate(first_pass, tw_cos, tw_sin, 2)
    spectrum = jnp.einsum(
        "upyc,pyez->uezc", turned, table_two, preferred_element_type=jnp.float32
    ).astype(jnp.bfloat16)
    columns = lax.all_to_all(spectrum, ("tu", "tv"), split_axis=1, concat_axis=0, tiled=True)
    e_loc = columns.shape[1]
    width_loc = e_loc * r_len
    stacked = columns.reshape(q_len, P_SIZE, e_loc, 2, r_len)
    second_pass = jnp.einsum(
        "qpexc,xqyd->pdeyc", stacked, table_one, preferred_element_type=jnp.float32
    ).astype(jnp.bfloat16)
    turned_two = rotate(second_pass, tw_cos[:, :, None, None], tw_sin[:, :, None, None], 3)
    w_value = plane_w[0]
    device = lax.axis_index(("tu", "tv"))
    col_ids = device * width_loc + jnp.arange(width_loc, dtype=jnp.int32)
    norm_scale = 1.0 / math.sqrt(slot_count * block_count * lax.axis_size("wa") * tile_count)
    row_count = lax.axis_size("wa") * (N // 2 // lax.axis_size("wa"))
    f_count = max(row_count // r_len, 1)
    e_vals = jnp.arange(f_count, dtype=jnp.int32)
    table_part = last_table(P_SIZE, e_vals)
    planar = jnp.einsum(
        "pdeyc,pyfz->fdezc", turned_two, table_part, preferred_element_type=jnp.float32
    )
    flat_rows = planar.reshape(f_count * r_len, e_loc, 2, r_len)
    row_ids = jnp.arange(row_count, dtype=jnp.int32)
    s_re, s_im = screen_parts(row_ids, col_ids, w_value)
    x_re = flat_rows[:, :, 0, :].reshape(row_count, width_loc)
    x_im = flat_rows[:, :, 1, :].reshape(row_count, width_loc)
    return lax.psum_scatter(
        ((x_re * s_re - x_im * s_im) * norm_scale).astype(jnp.bfloat16),
        "wa",
        scatter_dimension=0,
        tiled=True,
    ).astype(jnp.float32)


def solution(mesh):
    placed = (
        P(("wa", "tu", "tv"), None, None),
        P(("wa", "tu", "tv"), None, None),
        P(("wa", "tu", "tv"), None, None),
        P(("wa", "tu", "tv")),
        P(("wa", "tu", "tv"), None),
        P(("wa", "tu", "tv"), None),
        P("wa"),
    )
    return jax.shard_map(
        body, mesh=mesh, in_specs=placed, out_specs=P("wa", ("tu", "tv")), check_vma=False
    )
```

profile of v0, /device:TPU:2, one launch (start us, length us, event | category | flops | bytes accessed | tf_op | source)
XLA Modules:
  0.0 1543.6 jit_solution(14474218148248976425)
XLA Ops:
  11.4 8.6 all-to-all-start
  42.9 52.9 %all_to_all.54 = bf16[32,256,128]{2,1,0:T(8,128)(2,1)} all-to-all(bf16[32,256,128]{2,1,0:T(8,128)(2,1)} %get-tuple-element.34), channel_id=1, replica_groups=mesh['wa'=16,'tu'=4,'tv'=4] {'tu','tv'}, dimensions={0} | all-to-all | bytes 4194304 | tf_op jit(solution)/shard_map/all_to_all | solution.py:104
  104.0 44.6 %all-to-all-done.3 = bf16[32,256,128]{2,1,0:T(8,128)(2,1)S(1)} async-done(((bf16[32,256,128]{2,1,0:T(8,128)(2,1)}), bf16[32,256,128]{2,1,0:T(8,128)(2,1)S(1)}, u32[]{:S(2)}, u32[]{:S(2)}) %all-to-all-start.3) | async-done | bytes 2097184 | tf_op jit(solution)/shard_map/all_to_all | solution.py:105
  159.4 625.4 %while.1 = (s32[]{:T(128)}, f32[2,1024,1024]{2,0,1:T(2,128)}, s32[32,2]{0,1:T(2,128)S(1)}, f32[32,2,128,128]{3,2,1,0:T(8,128)}, s32[]{:T(128)}, /*index=5*/s32[3]{0:T(128)S(1)}, s32[1]{0:T(128)}, s32[]{:T(128)}) while((s32[]{:T(128)}, f32[2,1024,1024]{2,0,1:T(2,128)}, s32[32,2]{0,1:T(2,128)S(1)}, f32[32,2,128,128]{3,2,1,0:T(8,128)}, s32[]{:T(128)}, ...), condition=%wide.while_cond, body=%wide.while_body.sunk | while | flops 65555 | bytes 1179811 | solution.py:113
  165.9 23.8 %dynamic-update-slice.3 = f32[2,1024,1024]{2,0,1:T(2,128)} dynamic-update-slice(f32[2,1024,1024]{2,0,1:T(2,128)} %get-tuple-element.80, f32[2,128,128]{2,0,1:T(2,128)S(1)} %copy.137, s32[]{:T(128)} %constant.126.clone.1..sunk, s32[]{:T(128)} %bitcast.117, s32[]{:T(128)} %bitcast.118) | dynamic-update-slice | bytes 262148 | tf_op jit(solution)/shard_map/scatter-add
  209.3 23.8 %dynamic-update-slice.3 = f32[2,1024,1024]{2,0,1:T(2,128)} dynamic-update-slice(f32[2,1024,1024]{2,0,1:T(2,128)} %get-tuple-element.80, f32[2,128,128]{2,0,1:T(2,128)S(1)} %copy.137, s32[]{:T(128)} %constant.126.clone.1..sunk, s32[]{:T(128)} %bitcast.117, s32[]{:T(128)} %bitcast.118) | dynamic-update-slice | bytes 262148 | tf_op jit(solution)/shard_map/scatter-add
  305.0 23.8 %dynamic-update-slice.3 = f32[2,1024,1024]{2,0,1:T(2,128)} dynamic-update-slice(f32[2,1024,1024]{2,0,1:T(2,128)} %get-tuple-element.80, f32[2,128,128]{2,0,1:T(2,128)S(1)} %copy.137, s32[]{:T(128)} %constant.126.clone.1..sunk, s32[]{:T(128)} %bitcast.117, s32[]{:T(128)} %bitcast.118) | dynamic-update-slice | bytes 262148 | tf_op jit(solution)/shard_map/scatter-add
  348.4 23.8 %dynamic-update-slice.3 = f32[2,1024,1024]{2,0,1:T(2,128)} dynamic-update-slice(f32[2,1024,1024]{2,0,1:T(2,128)} %get-tuple-element.80, f32[2,128,128]{2,0,1:T(2,128)S(1)} %copy.137, s32[]{:T(128)} %constant.126.clone.1..sunk, s32[]{:T(128)} %bitcast.117, s32[]{:T(128)} %bitcast.118) | dynamic-update-slice | bytes 262148 | tf_op jit(solution)/shard_map/scatter-add
  391.8 23.8 %dynamic-update-slice.3 = f32[2,1024,1024]{2,0,1:T(2,128)} dynamic-update-slice(f32[2,1024,1024]{2,0,1:T(2,128)} %get-tuple-element.80, f32[2,128,128]{2,0,1:T(2,128)S(1)} %copy.137, s32[]{:T(128)} %constant.126.clone.1..sunk, s32[]{:T(128)} %bitcast.117, s32[]{:T(128)} %bitcast.118) | dynamic-update-slice | bytes 262148 | tf_op jit(solution)/shard_map/scatter-add
  435.1 23.8 %dynamic-update-slice.3 = f32[2,1024,1024]{2,0,1:T(2,128)} dynamic-update-slice(f32[2,1024,1024]{2,0,1:T(2,128)} %get-tuple-element.80, f32[2,128,128]{2,0,1:T(2,128)S(1)} %copy.137, s32[]{:T(128)} %constant.126.clone.1..sunk, s32[]{:T(128)} %bitcast.117, s32[]{:T(128)} %bitcast.118) | dynamic-update-slice | bytes 262148 | tf_op jit(solution)/shard_map/scatter-add
  478.5 23.8 %dynamic-update-slice.3 = f32[2,1024,1024]{2,0,1:T(2,128)} dynamic-update-slice(f32[2,1024,1024]{2,0,1:T(2,128)} %get-tuple-element.80, f32[2,128,128]{2,0,1:T(2,128)S(1)} %copy.137, s32[]{:T(128)} %constant.126.clone.1..sunk, s32[]{:T(128)} %bitcast.117, s32[]{:T(128)} %bitcast.118) | dynamic-update-slice | bytes 262148 | tf_op jit(solution)/shard_map/scatter-add
  521.9 23.8 %dynamic-update-slice.3 = f32[2,1024,1024]{2,0,1:T(2,128)} dynamic-update-slice(f32[2,1024,1024]{2,0,1:T(2,128)} %get-tuple-element.80, f32[2,128,128]{2,0,1:T(2,128)S(1)} %copy.137, s32[]{:T(128)} %constant.126.clone.1..sunk, s32[]{:T(128)} %bitcast.117, s32[]{:T(128)} %bitcast.118) | dynamic-update-slice | bytes 262148 | tf_op jit(solution)/shard_map/scatter-add
  565.3 23.8 %dynamic-update-slice.3 = f32[2,1024,1024]{2,0,1:T(2,128)} dynamic-update-slice(f32[2,1024,1024]{2,0,1:T(2,128)} %get-tuple-element.80, f32[2,128,128]{2,0,1:T(2,128)S(1)} %copy.137, s32[]{:T(128)} %constant.126.clone.1..sunk, s32[]{:T(128)} %bitcast.117, s32[]{:T(128)} %bitcast.118) | dynamic-update-slice | bytes 262148 | tf_op jit(solution)/shard_map/scatter-add
  634.9 23.8 %dynamic-update-slice.3 = f32[2,1024,1024]{2,0,1:T(2,128)} dynamic-update-slice(f32[2,1024,1024]{2,0,1:T(2,128)} %get-tuple-element.80, f32[2,128,128]{2,0,1:T(2,128)S(1)} %copy.137, s32[]{:T(128)} %constant.126.clone.1..sunk, s32[]{:T(128)} %bitcast.117, s32[]{:T(128)} %bitcast.118) | dynamic-update-slice | bytes 262148 | tf_op jit(solution)/shard_map/scatter-add
  678.3 23.8 %dynamic-update-slice.3 = f32[2,1024,1024]{2,0,1:T(2,128)} dynamic-update-slice(f32[2,1024,1024]{2,0,1:T(2,128)} %get-tuple-element.80, f32[2,128,128]{2,0,1:T(2,128)S(1)} %copy.137, s32[]{:T(128)} %constant.126.clone.1..sunk, s32[]{:T(128)} %bitcast.117, s32[]{:T(128)} %bitcast.118) | dynamic-update-slice | bytes 262148 | tf_op jit(solution)/shard_map/scatter-add
  747.9 23.8 %dynamic-update-slice.3 = f32[2,1024,1024]{2,0,1:T(2,128)} dynamic-update-slice(f32[2,1024,1024]{2,0,1:T(2,128)} %get-tuple-element.80, f32[2,128,128]{2,0,1:T(2,128)S(1)} %copy.137, s32[]{:T(128)} %constant.126.clone.1..sunk, s32[]{:T(128)} %bitcast.117, s32[]{:T(128)} %bitcast.118) | dynamic-update-slice | bytes 262148 | tf_op jit(solution)/shard_map/scatter-add
  793.0 52.5 %all-to-all-start.4 = ((bf16[2,1024,1024]{2,0,1:T(2,128)(2,1)}), bf16[2,1024,1024]{2,0,1:T(2,128)(2,1)}, u32[]{:S(2)}, u32[]{:S(2)}) async-start(bf16[2,1024,1024]{2,0,1:T(2,128)(2,1)} %convert_element_type.173), calls=%async_computation.4 | async-start | bytes 8388608 | tf_op jit(solution)/shard_map/all_to_all | solution.py:123
  846.1 92.9 %all-to-all-done.4 = bf16[2,1024,1024]{2,0,1:T(2,128)(2,1)} async-done(((bf16[2,1024,1024]{2,0,1:T(2,128)(2,1)}), bf16[2,1024,1024]{2,0,1:T(2,128)(2,1)}, u32[]{:S(2)}, u32[]{:S(2)}) %all-to-all-start.4) | async-done | bytes 4194336 | tf_op jit(solution)/shard_map/all_to_all | solution.py:123
  970.0 9.2 fusion.20
  982.8 281.6 %all-to-all-start.5 = ((bf16[256,32,2,128]{3,0,2,1:T(8,128)(2,1)}), bf16[256,32,2,128]{3,0,2,1:T(8,128)(2,1)}, u32[]{:S(2)}, u32[]{:S(2)}) async-start(bf16[256,32,2,128]{3,0,2,1:T(8,128)(2,1)} %copy.92), calls=%async_computation.5 | async-start | bytes 8388608 | tf_op jit(solution)/shard_map/all_to_all | solution.py:136
  1265.1 91.8 %all-to-all-done.5 = bf16[256,32,2,128]{3,0,2,1:T(8,128)(2,1)} async-done(((bf16[256,32,2,128]{3,0,2,1:T(8,128)(2,1)}), bf16[256,32,2,128]{3,0,2,1:T(8,128)(2,1)}, u32[]{:S(2)}, u32[]{:S(2)}) %all-to-all-start.5) | async-done | bytes 4194336 | tf_op jit(solution)/shard_map/all_to_all | solution.py:136
  1376.7 12.1 fusion.32
  1408.9 21.8 %fusion.23 = bf16[4096,256]{0,1:T(8,128)(2,1)} fusion(f32[4096,2,1,128]{0,3,1,2:T(8,128)} %copy.98, f32[4096,2,1,128]{0,3,1,2:T(8,128)} %copy.97, s32[256]{0:T(256)S(1)} %iota_add_fusion, f32[256]{0:T(256)S(1)} %fusion.76, f32[4096]{0:T(1024)S(1)} %fusion.60, f32[]{:T(128)} %bitcast.42), kind=kLoop, calls=%fused_computation.49 | loop fusion | flops 24117248 | bytes 10504196 | tf_op jit(solution)/shard_map/convert_element_type | solution.py:161
  1430.8 104.1 %reduce-scatter.2.cloned.1.call-done = bf16[256,256]{0,1:T(8,128)(2,1)} async-done(((bf16[4096,256]{0,1:T(8,128)(2,1)}), bf16[256,256]{0,1:T(8,128)(2,1)}) %reduce-scatter.2.cloned.1.call-update) | async-done | bytes 131088 | tf_op jit(solution)/shard_map/reduce_scatter | solution.py:160
  (282 shorter events, 471.1 us)
Async XLA Ops:
  6.5 16.5 %copy-start = (bf16[16,256,128]{2,1,0:T(8,128)(2,1)S(1)}, bf16[16,256,128]{2,1,0:T(8,128)(2,1)}, u32[]{:S(2)}) copy-start(bf16[16,256,128]{2,1,0:T(8,128)(2,1)} %param.9) | copy-start | bytes 3145732
  11.4 16.6 %all-to-all-start = ((s32[16,2,2]{1,2,0:T(2,128)}), s32[16,2,2]{1,2,0:T(2,128)S(1)}, u32[]{:S(2)}, u32[]{:S(2)}) async-start(s32[16,2,2]{1,2,0:T(2,128)} %copy.84), calls=%async_computation | async-start | bytes 32768 | tf_op jit(solution)/shard_map/all_to_all | solution.py:107
  28.0 14.8 all-to-all-start.1
  95.8 52.8 %all-to-all-start.3 = ((bf16[32,256,128]{2,1,0:T(8,128)(2,1)}), bf16[32,256,128]{2,1,0:T(8,128)(2,1)S(1)}, u32[]{:S(2)}, u32[]{:S(2)}) async-start(bf16[32,256,128]{2,1,0:T(8,128)(2,1)} %get-tuple-element.35), calls=%async_computation.3 | async-start | bytes 4194304 | tf_op jit(solution)/shard_map/all_to_all | solution.py:105
  154.0 5.4 copy-start.2
  793.0 146.1 %all-to-all-start.4 = ((bf16[2,1024,1024]{2,0,1:T(2,128)(2,1)}), bf16[2,1024,1024]{2,0,1:T(2,128)(2,1)}, u32[]{:S(2)}, u32[]{:S(2)}) async-start(bf16[2,1024,1024]{2,0,1:T(2,128)(2,1)} %convert_element_type.173), calls=%async_computation.4 | async-start | bytes 8388608 | tf_op jit(solution)/shard_map/all_to_all | solution.py:123
  982.8 374.1 %all-to-all-start.5 = ((bf16[256,32,2,128]{3,0,2,1:T(8,128)(2,1)}), bf16[256,32,2,128]{3,0,2,1:T(8,128)(2,1)}, u32[]{:S(2)}, u32[]{:S(2)}) async-start(bf16[256,32,2,128]{3,0,2,1:T(8,128)(2,1)} %copy.92), calls=%async_computation.5 | async-start | bytes 8388608 | tf_op jit(solution)/shard_map/all_to_all | solution.py:136
  1264.4 270.5 %reduce-scatter.2.cloned.1.call-start = ((), (), s32[]{:S(2)}) async-start(), calls=%async_computation.7 | async-start | bytes 2228224 | tf_op jit(solution)/shard_map/reduce_scatter | solution.py:160
  1408.9 127.7 %copy-start.1 = (bf16[16,256,128]{2,1,0:T(8,128)(2,1)S(1)}, bf16[16,256,128]{2,1,0:T(8,128)(2,1)}, u32[]{:S(2)}) copy-start(bf16[16,256,128]{2,1,0:T(8,128)(2,1)} %param.9) | copy-start | bytes 3145732
Sparse Core Ops, SparseCore 0:
  1430.9 103.9 reduce-scatter.1
where the time goes:
time: 1560 us; the launch traced here: 1540 us
  local copies, waits for them, and re-layouts  572 us (37%)
  starting transfers between devices  353 us (23%)
  waiting for transfers between devices  338 us (22%)
  other arithmetic  172 us (11%)
  blocking collectives  52.9 us (3%)
  matrix products  40.5 us (3%)
    scatter-add x160, local copies, waits for them, and re-layouts  515 us
    all_to_all x1, starting transfers between devices, body(): lax.all_to_all(spectrum, ('tu', 'tv'), split_axis=1, concat_axis=0, tiled...  282 us
    scatter-add x64, other arithmetic  110 us
    reduce_scatter x1, waiting for transfers between devices, body(): lax.psum_scatter(((x_re * s_re - x_im * s_im) * norm_scale).astype(jnp.bf...  104 us
    all_to_all x1, waiting for transfers between devices, body(): lax.all_to_all(tile_grid, 'tv', split_axis=1, concat_axis=2, tiled=True)  92.9 us
    all_to_all x1, waiting for transfers between devices, body(): lax.all_to_all(spectrum, ('tu', 'tv'), split_axis=1, concat_axis=0, tiled...  91.8 us
    all_to_all x1, blocking collectives, body(): lax.all_to_all(slot_ku, ('tu', 'tv'), split_axis=0, concat_axis=0, tiled=...  52.9 us
    all_to_all x1, starting transfers between devices, body(): lax.all_to_all(tile_grid, 'tv', split_axis=1, concat_axis=2, tiled=True)  52.5 us
  transfers between devices with their start and end apart: 6, of which 6 were waited for; matrix products, arithmetic and copies ran while one was open for 1% of the time, Pallas kernels for 0%

commit v1 on v0

v1 whole, which is shorter than its diff:
```python
import functools
import math

import jax
import jax.numpy as jnp
import ml_dtypes
import numpy as np
from jax import lax
from jax.experimental import pallas as pl
from jax.experimental.pallas import tpu as pltpu
from jax.sharding import PartitionSpec as P

N = 8192
HALF = 4096
S = 128
RANK = 8
COLS = 256
U0 = 64
U1 = 64
D_LEN = 128
F_LEN = 32
TILE = 1024
CHUNKS = 2
FIELD = 0.25
MIB = 1 << 20


def factor_tables(owners):
    t = np.arange(S) - (S - 1) / 2
    mu = np.arange(COLS) - (COLS - 1) / 2
    angle = 2.0 * np.pi * np.outer(t, mu) / N
    left, right = [], []
    for part in (np.cos(angle), np.sin(angle)):
        u, sv, vh = np.linalg.svd(part, full_matrices=False)
        left.append(u[:, :RANK])
        right.append(sv[:RANK, None] * vh[:RANK])
    basis = np.concatenate(left, axis=1)
    rows = []
    for j in range(owners):
        centre = COLS * j + (COLS - 1) / 2
        turn = np.exp(2j * np.pi * np.arange(S) * centre / N)
        proj = (basis * turn[:, None]).T
        rows.append(np.concatenate([proj.real, -proj.imag], axis=1))
        rows.append(np.concatenate([proj.imag, proj.real], axis=1))
    project = np.concatenate(rows, axis=0).astype(ml_dtypes.bfloat16)
    even, odd = right
    expand = np.concatenate(
        [
            np.concatenate([even, even], axis=1),
            np.concatenate([-odd, odd], axis=1),
            np.concatenate([-even, even], axis=1),
            np.concatenate([-odd, -odd], axis=1),
        ],
        axis=0,
    ).astype(np.float32)
    return project, expand


def row_tables():
    u0 = np.arange(U0)[:, None, None]
    u1 = np.arange(U1)[None, None, :]
    d = np.arange(D_LEN)[None, :, None]
    a = 2.0 * np.pi * (((u0 + U0 * u1) * d) % N) / N
    c, s = np.cos(a), np.sin(a)
    first = np.concatenate(
        [np.concatenate([c, -s], axis=2), np.concatenate([s, c], axis=2)], axis=1
    )
    b = 2.0 * np.pi * ((np.arange(F_LEN)[:, None] * np.arange(U0)[None, :]) % U0) / U0
    c, s = np.cos(b), np.sin(b)
    last = np.concatenate([np.concatenate([c, -s], axis=1), np.concatenate([s, c], axis=1)], axis=0)
    return first.astype(ml_dtypes.bfloat16), last.astype(ml_dtypes.bfloat16)


def project_kernel(count_ref, ku_ref, kv_ref, vis_ref, table_ref, out_ref, *, first_block):
    b = pl.program_id(0)
    live = count_ref[first_block + b]
    slots = lax.broadcasted_iota(jnp.int32, (2, ku_ref.shape[1]), 1)
    vis = jnp.where(slots < live, vis_ref[0].astype(jnp.float32), 0.0)
    kv_t = kv_ref[0].astype(jnp.float32).T
    weighted = jnp.concatenate([kv_t * vis[0:1, :], kv_t * vis[1:2, :]], axis=0)
    sub = jnp.dot(
        weighted.astype(jnp.bfloat16), ku_ref[0], preferred_element_type=jnp.float32
    ).astype(jnp.bfloat16)
    out = jnp.dot(table_ref[...], sub, preferred_element_type=jnp.float32)
    out_ref[...] = out.astype(jnp.bfloat16).reshape(out_ref.shape)


def project_chunk(count, ku, kv, vis, table, owners, chunk, size):
    slots = ku.shape[1]
    first = chunk * size
    return pl.pallas_call(
        functools.partial(project_kernel, first_block=first),
        out_shape=jax.ShapeDtypeStruct((owners, 4 * RANK, size * S), jnp.bfloat16),
        grid_spec=pltpu.PrefetchScalarGridSpec(
            num_scalar_prefetch=1,
            grid=(size,),
            in_specs=[
                pl.BlockSpec((1, slots, S), lambda b, _: (first + b, 0, 0)),
                pl.BlockSpec((1, slots, S), lambda b, _: (first + b, 0, 0)),
                pl.BlockSpec((1, 2, slots), lambda b, _: (first + b, 0, 0)),
                pl.BlockSpec(table.shape, lambda b, _: (0, 0)),
            ],
            out_specs=pl.BlockSpec((owners, 4 * RANK, S), lambda b, _: (0, 0, b)),
        ),
        compiler_params=pltpu.CompilerParams(vmem_limit_bytes=32 * MIB),
        cost_estimate=pl.CostEstimate(
            flops=size * 2 * (256 * 256 * 128 + 512 * 256 * 128),
            bytes_accessed=size * 4 * 65536,
            transcendentals=0,
        ),
    )(count, ku, kv, vis, table)


def add_blocks(row_ref, got_ref, phase_ref, expand_ref, acc_ref, chunk, size, per_src):
    table = expand_ref[...]
    r = RANK

    def per_source(src, carry):
        for b in range(size):
            g = src * per_src + chunk * size + b
            row = row_ref[g]
            ph = phase_ref[pl.ds(g, 1), :]
            swapped = jnp.concatenate([ph[:, COLS:], ph[:, :COLS]], axis=1)
            weights = jnp.concatenate(
                [
                    table[0:r] * ph,
                    table[r : 2 * r] * swapped,
                    table[2 * r : 3 * r] * swapped,
                    table[3 * r : 4 * r] * ph,
                ],
                axis=0,
            ).astype(jnp.bfloat16)
            coeffs = got_ref[src, :, b * S : (b + 1) * S]
            rows = lax.dot_general(
                coeffs, weights, (((0,), (0,)), ((), ())), preferred_element_type=jnp.float32
            )
            for c in range(4):
                acc_ref[c, pl.ds(row, S), :] += rows[:, c * 128 : (c + 1) * 128]
        return carry

    lax.fori_loop(0, got_ref.shape[0], per_source, 0)


def grid_kernel(row_ref, got_ref, phase_ref, expand_ref, *rest, chunk, size, per_src):
    if chunk == 0:
        (out_ref,) = rest
        out_ref[...] = jnp.zeros_like(out_ref)
    else:
        old_ref, out_ref, sem = rest
        copy = pltpu.make_async_copy(old_ref, out_ref, sem)
        copy.start()
        copy.wait()
    add_blocks(row_ref, got_ref, phase_ref, expand_ref, out_ref, chunk, size, per_src)


def grid_chunk(rows, got, phase, expand, old, chunk, size, per_src):
    vmem = pl.BlockSpec(memory_space=pltpu.VMEM)
    operands = [rows, got, phase, expand]
    specs = [pl.BlockSpec(memory_space=pltpu.SMEM), vmem, vmem, vmem]
    scratch = []
    if chunk:
        operands.append(old)
        specs.append(pl.BlockSpec(memory_space=pl.ANY))
        scratch.append(pltpu.SemaphoreType.DMA)
    return pl.pallas_call(
        functools.partial(grid_kernel, chunk=chunk, size=size, per_src=per_src),
        out_shape=jax.ShapeDtypeStruct((4, HALF, 128), jnp.float32),
        in_specs=specs,
        out_specs=vmem,
        scratch_shapes=scratch,
        compiler_params=pltpu.CompilerParams(vmem_limit_bytes=32 * MIB),
        cost_estimate=pl.CostEstimate(
            flops=got.shape[0] * size * 2 * 128 * 256 * 512,
            bytes_accessed=12 * MIB,
            transcendentals=0,
        ),
    )(*operands)


def image_kernel(
    row_ref, place_ref, got_ref, phase_ref, expand_ref, old_ref, first_hbm, last_ref, screen_hbm,
    keep_ref, send_ref, acc_ref, first_ref, mid_ref, screen_ref, full_ref, sems,
    *, chunk, size, per_src,
):
    load_old = pltpu.make_async_copy(old_ref, acc_ref, sems.at[0])
    load_first = pltpu.make_async_copy(first_hbm, first_ref, sems.at[1])
    load_screen = pltpu.make_async_copy(screen_hbm, screen_ref, sems.at[2])
    load_old.start()
    load_first.start()
    load_screen.start()
    load_old.wait()
    add_blocks(row_ref, got_ref, phase_ref, expand_ref, acc_ref, chunk, size, per_src)
    load_first.wait()

    def first_step(u0, carry):
        parts = [acc_ref[c, pl.ds(u0, U1, stride=U0), :] for c in range(4)]
        x = jnp.concatenate(
            [
                jnp.concatenate([parts[0], parts[1]], axis=1),
                jnp.concatenate([parts[2], parts[3]], axis=1),
            ],
            axis=0,
        ).astype(jnp.bfloat16)
        y = jnp.dot(first_ref[u0], x, preferred_element_type=jnp.float32)
        base = pl.multiple_of(u0 * (2 * D_LEN), 2 * D_LEN)
        mid_ref[0, pl.ds(base, 2 * D_LEN), :] = y[:, :128]
        mid_ref[1, pl.ds(base, 2 * D_LEN), :] = y[:, 128:]
        return carry

    lax.fori_loop(0, U0, first_step, 0, unroll=2)
    load_screen.wait()
    last = last_ref[...]

    def last_step(d, carry):
        parts = [
            [mid_ref[c, pl.ds(x * D_LEN + d, U0, stride=2 * D_LEN), :] for c in range(2)]
            for x in range(2)
        ]
        y = jnp.concatenate([jnp.concatenate(p, axis=1) for p in parts], axis=0)
        planar = jnp.dot(last, y.astype(jnp.bfloat16), preferred_element_type=jnp.float32)
        value = planar[:F_LEN] * screen_ref[0, d] - planar[F_LEN:] * screen_ref[1, d]
        for c in range(2):
            full_ref[c, pl.ds(d, F_LEN, stride=D_LEN), :] = value[:, c * 128 : (c + 1) * 128]
        return carry

    lax.fori_loop(0, D_LEN, last_step, 0, unroll=2)
    for out_ref, which in ((keep_ref, 0), (send_ref, 1)):
        for i in range(out_ref.shape[0]):
            base = pl.multiple_of(place_ref[which, i] * COLS, COLS)
            for c in range(2):
                out_ref[i, :, c * 128 : (c + 1) * 128] = full_ref[
                    c, pl.ds(base, COLS), :
                ].astype(jnp.bfloat16)


def make_image(rows, place, got, phase, expand, old, first, last, screen, chunk, size, per_src):
    vmem = pl.BlockSpec(memory_space=pltpu.VMEM)
    smem = pl.BlockSpec(memory_space=pltpu.SMEM)
    hbm = pl.BlockSpec(memory_space=pl.ANY)
    piece = jax.ShapeDtypeStruct((place.shape[1], COLS, COLS), jnp.bfloat16)
    return pl.pallas_call(
        functools.partial(image_kernel, chunk=chunk, size=size, per_src=per_src),
        out_shape=(piece, piece),
        in_specs=[smem, smem, vmem, vmem, vmem, hbm, hbm, vmem, hbm],
        out_specs=(vmem, vmem),
        scratch_shapes=[
            pltpu.VMEM((4, HALF, 128), jnp.float32),
            pltpu.VMEM(first.shape, jnp.bfloat16),
            pltpu.VMEM((2, U0 * 2 * D_LEN, 128), jnp.float32),
            pltpu.VMEM(screen.shape, jnp.float32),
            pltpu.VMEM((2, HALF, 128), jnp.float32),
            pltpu.SemaphoreType.DMA((3,)),
        ],
        compiler_params=pltpu.CompilerParams(vmem_limit_bytes=56 * MIB),
        cost_estimate=pl.CostEstimate(
            flops=4 * 1024**3, bytes_accessed=24 * MIB, transcendentals=0
        ),
    )(rows, place, got, phase, expand, old, first, last, screen)


def screen_parts(col_base, w_value, scale):
    d = jnp.arange(D_LEN, dtype=jnp.int32)[:, None, None]
    f = jnp.arange(F_LEN, dtype=jnp.int32)[None, :, None]
    row = f * D_LEN + d
    col = col_base + jnp.arange(COLS, dtype=jnp.int32)[None, None, :]
    half = N // 2
    cell = 2.0 * FIELD / N
    dl = ((row + half) % N - half).astype(jnp.float32) * cell
    dm = ((col + half) % N - half).astype(jnp.float32) * cell
    lift = jnp.sqrt(1.0 - dl**2 - dm**2) - 1.0
    quarter = ((row + col) % 4).astype(jnp.float32)
    angle = 2.0 * math.pi * w_value * lift - 0.5 * math.pi * quarter
    return jnp.stack([jnp.cos(angle), jnp.sin(angle)]) * scale


def sum_planes(keep, send, planes):
    def shifted(values, target):
        pairs = [(i, target(i)) for i in range(planes)]
        return lax.ppermute(values, "wa", pairs).astype(jnp.float32)

    total = keep.astype(jnp.float32) + shifted(send, lambda i: i ^ 1)
    total = total.astype(jnp.bfloat16).reshape(4, 2, COLS, COLS)
    got = [
        shifted(total[step], lambda i, step=step: (i + 4 * step) % planes) for step in (1, 2, 3)
    ]
    total = (total[0].astype(jnp.float32) + got[0] + got[1] + got[2]).astype(jnp.bfloat16)
    return total[0].astype(jnp.float32) + shifted(total[1], lambda i: i ^ 2)


def body(kernel_u, kernel_v, visibilities, vis_count, tile_route, block_offset, plane_w):
    n_tu, n_tv, planes = lax.axis_size("tu"), lax.axis_size("tv"), lax.axis_size("wa")
    owners = n_tu * n_tv
    blocks, slots = kernel_u.shape[0], kernel_u.shape[1]
    size = blocks // CHUNKS
    project, expand = factor_tables(owners)
    first, last = row_tables()

    target = tile_route[:, 0]
    corner = jnp.stack(
        [target // n_tv * TILE + block_offset[:, 0], target % n_tv * TILE + block_offset[:, 1]],
        axis=0,
    )
    corners = lax.all_gather(corner, ("tu", "tv"), axis=0)
    rows = corners[:, 0, :].reshape(-1)
    cols = corners[:, 1, :].reshape(-1)

    owner = lax.axis_index(("tu", "tv"))
    col_base = owner * COLS
    lane = jnp.arange(COLS, dtype=jnp.int32)
    turns = (cols[:, None] * (col_base + lane)[None, :]) % N
    shift = (S - 1) / 2 * (lane.astype(jnp.float32) - (COLS - 1) / 2)
    angle = (turns.astype(jnp.float32) + shift[None, :]) * (2.0 * math.pi / N)
    phase = jnp.concatenate([jnp.cos(angle), jnp.sin(angle)], axis=1)

    scale = 1.0 / math.sqrt(slots * blocks * owners * 16)
    screen = screen_parts(col_base, plane_w[0], scale)

    got = []
    for chunk in range(CHUNKS):
        coeffs = project_chunk(
            vis_count, kernel_u, kernel_v, visibilities, project, owners, chunk, size
        )
        got.append(
            lax.all_to_all(coeffs, ("tu", "tv"), split_axis=0, concat_axis=0, tiled=True)
        )
    me = lax.axis_index("wa")
    core, z_hi, x = me % 2, me // 2 % 2, me // 4
    step = jnp.arange(8, dtype=jnp.int32)
    pair = ((x + step // 2) % 4) * 4 + (z_hi ^ (step % 2)) * 2
    place = jnp.stack([pair + core, pair + (1 - core)])

    acc = None
    for chunk in range(CHUNKS - 1):
        acc = grid_chunk(rows, got[chunk], phase, expand, acc, chunk, size, blocks)
    keep, send = make_image(
        rows, place, got[-1], phase, expand, acc, first, last, screen, CHUNKS - 1, size, blocks
    )
    if planes != 16:
        return keep, send
    return sum_planes(keep, send, planes)


def solution(mesh):
    split = ("wa", "tu", "tv")
    placed = (
        P(split, None, None),
        P(split, None, None),
        P(split, None, None),
        P(split),
        P(split, None),
        P(split, None),
        P("wa"),
    )
    return jax.shard_map(
        body, mesh=mesh, in_specs=placed, out_specs=P("wa", ("tu", "tv")), check_vma=False
    )
```

time: 1560 us -> 200 us (0.13)
  local copies, waits for them, and re-layouts: 572 us -> 10.2 us
  starting transfers between devices: 353 us -> 21.8 us
  waiting for transfers between devices: 338 us -> 18.5 us
  other arithmetic: 172 us -> 27.6 us
  Pallas kernels: 0 us -> 64.7 us
  matrix products: 40.5 us -> 0 us
    scatter-add x160 -> x0, local copies, waits for them, and re-layouts: 515 us -> none
    all_to_all x5 -> x2, starting transfers between devices: 353 us -> 12.3 us  [body(): lax.all_to_all(coeffs, ('tu', 'tv'), split_axis=0, concat_axis=0, tiled=T...]
    all_to_all x5 -> x2, waiting for transfers between devices: 234 us -> 0.01 us  [body(): lax.all_to_all(coeffs, ('tu', 'tv'), split_axis=0, concat_axis=0, tiled=T...]
    scatter-add x64 -> x0, other arithmetic: 110 us -> none
    reduce_scatter x1 -> x0, waiting for transfers between devices: 104 us -> none  [body(): lax.psum_scatter(((x_re * s_re - x_im * s_im) * norm_scale).astype(jnp.bf...]
    pallas_call x0 -> x4, Pallas kernels: none -> 64.7 us  [the longest x1 44.9 us: make_image(): pl.pallas_call(functools.partial(image_kernel, chunk=chunk, size=size, pe...]
    all_gather x0 -> x1, blocking collectives: none -> 53.2 us  [body(): corners = lax.all_gather(corner, ('tu', 'tv'), axis=0)]
    all_to_all x1 -> x0, blocking collectives: 52.9 us -> none  [body(): lax.all_to_all(slot_ku, ('tu', 'tv'), split_axis=0, concat_axis=0, tiled=...]
  transfers between devices with their start and end apart: 6 -> 7, of which waited for: 6 -> 5; matrix products, arithmetic and copies ran while one was open for 1% -> 13% of each run, Pallas kernels for 0% -> 7%
where the time goes in v1:
time: 200 us; the launch traced here: 197 us
  Pallas kernels  64.7 us (32%)
  blocking collectives  53.2 us (27%)
  other arithmetic  27.6 us (14%)
  starting transfers between devices  21.8 us (11%)
  waiting for transfers between devices  18.5 us (9%)
  local copies, waits for them, and re-layouts  10.2 us (5%)
    all_gather x1, blocking collectives, body(): corners = lax.all_gather(corner, ('tu', 'tv'), axis=0)  53.2 us
    pallas_call x1, Pallas kernels, make_image(): pl.pallas_call(functools.partial(image_kernel, chunk=chunk, size=size, pe...  44.9 us
    cos x1, other arithmetic, screen_parts(): return jnp.stack([jnp.cos(angle), jnp.sin(angle)]) * scale  19 us
    ppermute x5, waiting for transfers between devices, shifted(): return lax.ppermute(values, 'wa', pairs).astype(jnp.float32)  18.5 us
    all_to_all x2, starting transfers between devices, body(): lax.all_to_all(coeffs, ('tu', 'tv'), split_axis=0, concat_axis=0, tiled=T...  12.3 us
    pallas_call x2, Pallas kernels, project_chunk(): pl.pallas_call(functools.partial(project_kernel, first_block=first), out_...  11.4 us
    ppermute x5, starting transfers between devices, shifted(): return lax.ppermute(values, 'wa', pairs).astype(jnp.float32)  9.54 us
    unnamed x34, local copies, waits for them, and re-layouts  9.08 us
  transfers between devices with their start and end apart: 7, of which 5 were waited for; matrix products, arithmetic and copies ran while one was open for 13% of the time, Pallas kernels for 7%

profile of v1, /device:TPU:2, one launch (start us, length us, event | category | flops | bytes accessed | tf_op | source)
XLA Modules:
  0.0 196.9 jit_solution(2036599021406610007)
XLA Ops:
  0.0 1.2 copy-done.1
  1.2 1.2 copy-done.3
  4.8 5.7 %shard_map.110 = bf16[16,32,1024]{2,1,0:T(8,128)(2,1)} custom-call(s32[16]{0:T(128)S(1)} %copy-done.12, bf16[16,256,128]{2,1,0:T(8,128)(2,1)S(1)} %copy-done.1, bf16[16,256,128]{2,1,0:T(8,128)(2,1)S(1)} %copy-done.3, bf16[16,2,256]{2,1,0:T(2,128)(2,1)S(1)} %copy-done.9, bf16[512,256]{1,0:T(8,128)(2,1)S(1)} %copy-done.6), custom_call_target="tpu_custom_call" | custom-call | flops 402653184 | bytes 2097152 | tf_op jit(solution)/shard_map/pallas_call | solution.py:91
  10.5 8.6 %all-to-all-start.1 = ((bf16[16,32,1024]{2,1,0:T(8,128)(2,1)}), bf16[16,32,1024]{2,1,0:T(8,128)(2,1)S(1)}, u32[]{:S(2)}, u32[]{:S(2)}) async-start(bf16[16,32,1024]{2,1,0:T(8,128)(2,1)} %shard_map.110), calls=%async_computation.1 | async-start | bytes 2097152 | tf_op jit(solution)/shard_map/all_to_all | solution.py:324
  20.9 53.2 %all-gather.1 = s32[16,2,16]{2,1,0:T(2,128)S(1)} all-gather(s32[1,2,16]{2,1,0:T(2,128)S(1)} %add_bitcast_fusion), channel_id=2, replica_groups=mesh['wa'=16,'tu'=4,'tv'=4] {'tu','tv'}, dimensions={0}, use_global_device_ids=true | all-gather | bytes 2176 | tf_op jit(solution)/shard_map/all_gather | solution.py:303
  74.3 5.7 %shard_map.109 = bf16[16,32,1024]{2,1,0:T(8,128)(2,1)} custom-call(s32[16]{0:T(128)S(1)} %copy-done.13, bf16[16,256,128]{2,1,0:T(8,128)(2,1)S(1)} %copy-done.2, bf16[16,256,128]{2,1,0:T(8,128)(2,1)S(1)} %copy-done.4, bf16[16,2,256]{2,1,0:T(2,128)(2,1)S(1)} %copy-done.10, bf16[512,256]{1,0:T(8,128)(2,1)S(1)} %copy-done.7), custom_call_target="tpu_custom_call" | custom-call | flops 402653184 | bytes 2097152 | tf_op jit(solution)/shard_map/pallas_call | solution.py:91
  80.0 3.7 %all-to-all-start = ((bf16[16,32,1024]{2,1,0:T(8,128)(2,1)}), bf16[16,32,1024]{2,1,0:T(8,128)(2,1)S(1)}, u32[]{:S(2)}, u32[]{:S(2)}) async-start(bf16[16,32,1024]{2,1,0:T(8,128)(2,1)} %shard_map.109), calls=%async_computation | async-start | bytes 2097152 | tf_op jit(solution)/shard_map/all_to_all | solution.py:324
  84.3 1.1 fusion.11
  85.5 19.0 %fusion.5 = (f32[1,128,32,256]{3,2,1,0:T(8,128)S(1)}, f32[1,128,32,256]{3,2,1,0:T(8,128)S(1)}) fusion(s32[256]{0:T(256)S(1)} %iota_add_fusion.1, s32[128,32]{1,0:T(8,128)} %copy.13, f32[256]{0:T(256)S(1)} %fusion.21, f32[128,32]{1,0:T(8,128)S(1)} %copy.12, f32[]{:T(128)} %bitcast.4), kind=kLoop, calls=%fused_computation.12 | loop fusion | flops 18874368 | bytes 8423428 | tf_op jit(solution)/shard_map/cos | solution.py:273
  104.6 4.2 %maximum_multiply_fusion.screen_hbm = f32[2,128,32,256]{3,2,1,0:T(8,128)} fusion(f32[1,128,32,256]{3,2,1,0:T(8,128)S(1)} %get-tuple-element.15, f32[1,128,32,256]{3,2,1,0:T(8,128)S(1)} %get-tuple-element.14), kind=kLoop, calls=%fused_computation | loop fusion | flops 4194304 | bytes 16777216 | tf_op jit(solution)/shard_map/mul | solution.py:273
  108.8 8.5 %shard_map.111.old_ref = f32[4,4096,128]{2,1,0:T(8,128)S(1)} custom-call(s32[256]{0:T(256)S(1)} %reshape_squeeze.3.row_ref, bf16[16,32,1024]{2,1,0:T(8,128)(2,1)S(1)} %all-to-all-done.1.got_ref, f32[256,512]{1,0:T(8,128)S(1)} %pad_maximum_fusion.phase_ref, f32[32,512]{1,0:T(8,128)S(1)} %copy-done.8), custom_call_target="tpu_custom_call" | custom-call | flops 4294967296 | bytes 12582912 | tf_op jit(solution)/shard_map/pallas_call | solution.py:165
  117.3 3.3 %copy-done = f32[4,4096,128]{2,1,0:T(8,128)} copy-done((f32[4,4096,128]{2,1,0:T(8,128)}, f32[4,4096,128]{2,1,0:T(8,128)S(1)}, u32[]{:S(2)}) %copy-start) | copy-done | bytes 8388632
  120.5 1.0 copy-done.14
  121.5 44.9 %shard_map.112 = (bf16[8,256,256]{2,1,0:T(8,128)(2,1)}, bf16[8,256,256]{2,1,0:T(8,128)(2,1)}) custom-call(s32[256]{0:T(256)} %copy-done.11, s32[2,8]{1,0:T(2,128)} %pad_add_fusion.place_ref, bf16[16,32,1024]{2,1,0:T(8,128)(2,1)} %copy-done.14, f32[256,512]{1,0:T(8,128)} %copy-done.5, f32[32,512]{1,0:T(8,128)} %constant.182.clone.expand_ref, ...), custom_call_target="tpu_custom_call" | custom-call | flops 4294967296 | bytes 25165824 | tf_op jit(solution)/shard_map/pallas_call | solution.py:241
  166.5 2.9 %collective-permute-done = bf16[8,256,256]{2,1,0:T(8,128)(2,1)S(1)} collective-permute-done((bf16[8,256,256]{2,1,0:T(8,128)(2,1)}, bf16[8,256,256]{2,1,0:T(8,128)(2,1)S(1)}, u32[]{:S(2)}, u32[]{:S(2)}) %collective-permute-start) | collective-permute-done | bytes 1048608 | tf_op jit(solution)/shard_map/ppermute | solution.py:279
  169.4 1.5 add_convert_fusion
  170.9 1.6 collective-permute-start.1
  172.5 1.1 collective-permute-start.2
  173.6 2.1 %collective-permute-start.3 = (bf16[2,256,256]{2,1,0:T(8,128)(2,1)S(1)}, bf16[2,256,256]{2,1,0:T(8,128)(2,1)S(1)}, u32[]{:S(2)}, u32[]{:S(2)}) collective-permute-start(bf16[2,256,256]{2,1,0:T(8,128)(2,1)S(1)} %get-tuple-element.12), channel_id=1, source_target_pairs={{0,192},{16,208},{32,224},{48,240},{64,0},{80,16},{96,32},{112,48}... | collective-permute-start | bytes 786440 | tf_op jit(solution)/shard_map/ppermute | solution.py:279
  175.8 4.4 %collective-permute-done.1 = bf16[2,256,256]{2,1,0:T(8,128)(2,1)S(1)} collective-permute-done((bf16[2,256,256]{2,1,0:T(8,128)(2,1)S(1)}, bf16[2,256,256]{2,1,0:T(8,128)(2,1)S(1)}, u32[]{:S(2)}, u32[]{:S(2)}) %collective-permute-start.1) | collective-permute-done | bytes 262176 | tf_op jit(solution)/shard_map/ppermute | solution.py:279
  180.1 3.1 %collective-permute-done.2 = bf16[2,256,256]{2,1,0:T(8,128)(2,1)S(1)} collective-permute-done((bf16[2,256,256]{2,1,0:T(8,128)(2,1)S(1)}, bf16[2,256,256]{2,1,0:T(8,128)(2,1)S(1)}, u32[]{:S(2)}, u32[]{:S(2)}) %collective-permute-start.2) | collective-permute-done | bytes 262176 | tf_op jit(solution)/shard_map/ppermute | solution.py:279
  183.2 3.8 %collective-permute-done.3 = bf16[2,256,256]{2,1,0:T(8,128)(2,1)S(1)} collective-permute-done((bf16[2,256,256]{2,1,0:T(8,128)(2,1)S(1)}, bf16[2,256,256]{2,1,0:T(8,128)(2,1)S(1)}, u32[]{:S(2)}, u32[]{:S(2)}) %collective-permute-start.3) | collective-permute-done | bytes 262176 | tf_op jit(solution)/shard_map/ppermute | solution.py:279
  187.2 4.6 %collective-permute-start.4 = (bf16[256,256]{1,0:T(8,128)(2,1)S(1)}, bf16[256,256]{1,0:T(8,128)(2,1)S(1)}, u32[]{:S(2)}, u32[]{:S(2)}) collective-permute-start(bf16[256,256]{1,0:T(8,128)(2,1)S(1)} %slice_bitcast_fusion), channel_id=1, source_target_pairs={{0,32},{16,48},{32,0},{48,16},{64,96},{80,112},{96,64},{112,80},{1... | collective-permute-start | bytes 393224 | tf_op jit(solution)/shard_map/ppermute | solution.py:279
  191.8 4.4 %collective-permute-done.4 = bf16[256,256]{1,0:T(8,128)(2,1)S(1)} collective-permute-done((bf16[256,256]{1,0:T(8,128)(2,1)S(1)}, bf16[256,256]{1,0:T(8,128)(2,1)S(1)}, u32[]{:S(2)}, u32[]{:S(2)}) %collective-permute-start.4) | collective-permute-done | bytes 131104 | tf_op jit(solution)/shard_map/ppermute | solution.py:279
  (53 shorter events, 5.3 us)
Async XLA Ops:
  0.0 1.2 copy-start.1
  1.2 1.2 copy-start.3
  2.5 0.9 copy-start.6
  3.4 0.7 copy-start.9
  4.1 0.7 copy-start.12
  4.8 16.1 %copy-start.15 = (s32[16,2]{0,1:T(2,128)S(1)}, s32[16,2]{0,1:T(2,128)}, u32[]{:S(2)}) copy-start(s32[16,2]{0,1:T(2,128)} %param.16) | copy-start | bytes 388
  4.8 16.1 %copy-start.16 = (s32[16,1]{0,1:T(1,128)S(1)}, s32[16,1]{0,1:T(1,128)}, u32[]{:S(2)}) copy-start(s32[16,1]{0,1:T(1,128)} %param.15) | copy-start | bytes 196
  4.8 69.5 %copy-start.2 = (bf16[16,256,128]{2,1,0:T(8,128)(2,1)S(1)}, bf16[16,256,128]{2,1,0:T(8,128)(2,1)}, u32[]{:S(2)}) copy-start(bf16[16,256,128]{2,1,0:T(8,128)(2,1)} %ku_ref.3) | copy-start | bytes 3145732
  4.8 69.5 %copy-start.4 = (bf16[16,256,128]{2,1,0:T(8,128)(2,1)S(1)}, bf16[16,256,128]{2,1,0:T(8,128)(2,1)}, u32[]{:S(2)}) copy-start(bf16[16,256,128]{2,1,0:T(8,128)(2,1)} %kv_ref.3) | copy-start | bytes 3145732
  4.8 69.5 %copy-start.7 = (bf16[512,256]{1,0:T(8,128)(2,1)S(1)}, bf16[512,256]{1,0:T(8,128)(2,1)}, u32[]{:S(2)}) copy-start(bf16[512,256]{1,0:T(8,128)(2,1)} %constant.181.clone.table_ref) | copy-start | bytes 786436
  4.8 69.5 %copy-start.10 = (bf16[16,2,256]{2,1,0:T(2,128)(2,1)S(1)}, bf16[16,2,256]{2,1,0:T(2,128)(2,1)}, u32[]{:S(2)}) copy-start(bf16[16,2,256]{2,1,0:T(2,128)(2,1)} %vis_ref.3) | copy-start | bytes 49156
  4.8 69.5 %copy-start.13 = (s32[16]{0:T(128)S(1)}, s32[16]{0:T(128)}, u32[]{:S(2)}) copy-start(s32[16]{0:T(128)} %count_ref.3) | copy-start | bytes 196
  10.5 69.5 %all-to-all-start.1 = ((bf16[16,32,1024]{2,1,0:T(8,128)(2,1)}), bf16[16,32,1024]{2,1,0:T(8,128)(2,1)S(1)}, u32[]{:S(2)}, u32[]{:S(2)}) async-start(bf16[16,32,1024]{2,1,0:T(8,128)(2,1)} %shard_map.110), calls=%async_computation.1 | async-start | bytes 2097152 | tf_op jit(solution)/shard_map/all_to_all | solution.py:324
  74.2 34.5 %copy-start.11 = (s32[256]{0:T(256)}, s32[256]{0:T(256)S(1)}, u32[]{:S(2)}) copy-start(s32[256]{0:T(256)S(1)} %reshape_squeeze.3.row_ref) | copy-start | bytes 3076
  80.0 40.5 %all-to-all-start = ((bf16[16,32,1024]{2,1,0:T(8,128)(2,1)}), bf16[16,32,1024]{2,1,0:T(8,128)(2,1)S(1)}, u32[]{:S(2)}, u32[]{:S(2)}) async-start(bf16[16,32,1024]{2,1,0:T(8,128)(2,1)} %shard_map.109), calls=%async_computation | async-start | bytes 2097152 | tf_op jit(solution)/shard_map/all_to_all | solution.py:324
  85.5 23.3 %copy-start.5 = (f32[256,512]{1,0:T(8,128)}, f32[256,512]{1,0:T(8,128)S(1)}, u32[]{:S(2)}) copy-start(f32[256,512]{1,0:T(8,128)S(1)} %pad_maximum_fusion.phase_ref) | copy-start | bytes 1572868
  104.6 4.2 %copy-start.8 = (f32[32,512]{1,0:T(8,128)S(1)}, f32[32,512]{1,0:T(8,128)}, u32[]{:S(2)}) copy-start(f32[32,512]{1,0:T(8,128)} %constant.182.clone.expand_ref) | copy-start | bytes 196612
  117.3 3.3 %copy-start = (f32[4,4096,128]{2,1,0:T(8,128)}, f32[4,4096,128]{2,1,0:T(8,128)S(1)}, u32[]{:S(2)}) copy-start(f32[4,4096,128]{2,1,0:T(8,128)S(1)} %shard_map.111.old_ref) | copy-start | bytes 25165828
  120.5 1.0 copy-start.14
  166.4 3.0 %collective-permute-start = (bf16[8,256,256]{2,1,0:T(8,128)(2,1)}, bf16[8,256,256]{2,1,0:T(8,128)(2,1)S(1)}, u32[]{:S(2)}, u32[]{:S(2)}) collective-permute-start(bf16[8,256,256]{2,1,0:T(8,128)(2,1)} %get-tuple-element.8), channel_id=1, source_target_pairs={{0,16},{16,0},{32,48},{48,32},{64,80},{80,64},{96,112},{112,96},{1... | collective-permute-start | bytes 3145736 | tf_op jit(solution)/shard_map/ppermute | solution.py:279
  170.9 9.2 %collective-permute-start.1 = (bf16[2,256,256]{2,1,0:T(8,128)(2,1)S(1)}, bf16[2,256,256]{2,1,0:T(8,128)(2,1)S(1)}, u32[]{:S(2)}, u32[]{:S(2)}) collective-permute-start(bf16[2,256,256]{2,1,0:T(8,128)(2,1)S(1)} %get-tuple-element.11), channel_id=1, source_target_pairs={{0,64},{16,80},{32,96},{48,112},{64,128},{80,144},{96,160},{112,17... | collective-permute-start | bytes 786440 | tf_op jit(solution)/shard_map/ppermute | solution.py:279
  172.5 10.7 %collective-permute-start.2 = (bf16[2,256,256]{2,1,0:T(8,128)(2,1)S(1)}, bf16[2,256,256]{2,1,0:T(8,128)(2,1)S(1)}, u32[]{:S(2)}, u32[]{:S(2)}) collective-permute-start(bf16[2,256,256]{2,1,0:T(8,128)(2,1)S(1)} %get-tuple-element.13), channel_id=1, source_target_pairs={{0,128},{16,144},{32,160},{48,176},{64,192},{80,208},{96,224},{112... | collective-permute-start | bytes 786440 | tf_op jit(solution)/shard_map/ppermute | solution.py:279
  173.6 13.4 %collective-permute-start.3 = (bf16[2,256,256]{2,1,0:T(8,128)(2,1)S(1)}, bf16[2,256,256]{2,1,0:T(8,128)(2,1)S(1)}, u32[]{:S(2)}, u32[]{:S(2)}) collective-permute-start(bf16[2,256,256]{2,1,0:T(8,128)(2,1)S(1)} %get-tuple-element.12), channel_id=1, source_target_pairs={{0,192},{16,208},{32,224},{48,240},{64,0},{80,16},{96,32},{112,48}... | collective-permute-start | bytes 786440 | tf_op jit(solution)/shard_map/ppermute | solution.py:279
  187.2 9.0 %collective-permute-start.4 = (bf16[256,256]{1,0:T(8,128)(2,1)S(1)}, bf16[256,256]{1,0:T(8,128)(2,1)S(1)}, u32[]{:S(2)}, u32[]{:S(2)}) collective-permute-start(bf16[256,256]{1,0:T(8,128)(2,1)S(1)} %slice_bitcast_fusion), channel_id=1, source_target_pairs={{0,32},{16,48},{32,0},{48,16},{64,96},{80,112},{96,64},{112,80},{1... | collective-permute-start | bytes 393224 | tf_op jit(solution)/shard_map/ppermute | solution.py:279

commit v2 on v1

v2 whole, which is shorter than its diff:
```python
import functools
import math

import jax
import jax.numpy as jnp
import ml_dtypes
import numpy as np
from jax import lax
from jax.experimental import pallas as pl
from jax.experimental.pallas import tpu as pltpu
from jax.sharding import PartitionSpec as P

N = 8192
HALF = 4096
S = 128
EVEN, ODD = 8, 7
RANK = 8
MARK = 15
COLS = 256
U0 = 512
U1 = 8
L0 = 16
L1 = 256
TILE = 1024
CHUNKS = 2
STEP = 4
FIELD = 0.25
MIB = 1 << 20


def factor_tables(owners):
    t = np.arange(S) - (S - 1) / 2
    mu = np.arange(COLS) - (COLS - 1) / 2
    angle = 2.0 * np.pi * np.outer(t, mu) / N
    left, right = [], []
    for part, rank in ((np.cos(angle), EVEN), (np.sin(angle), ODD)):
        u, sv, vh = np.linalg.svd(part, full_matrices=False)
        pad = ((0, RANK - rank), (0, 0))
        left.append(np.pad(u[:, :rank].T, pad))
        right.append(np.pad(sv[:rank, None] * vh[:rank], pad))
    basis = np.concatenate(left, axis=0)
    rows = []
    for j in range(owners):
        centre = COLS * j + (COLS - 1) / 2
        turn = np.exp(2j * np.pi * np.arange(S) * centre / N)
        proj = basis * turn[None, :]
        rows.append(np.concatenate([proj.real, -proj.imag], axis=1))
        rows.append(np.concatenate([proj.imag, proj.real], axis=1))
    project = np.concatenate(rows, axis=0).astype(ml_dtypes.bfloat16)
    even, odd = right
    expand = np.concatenate(
        [
            np.concatenate([even, even], axis=1),
            np.concatenate([-odd, odd], axis=1),
            np.concatenate([-even, even], axis=1),
            np.concatenate([-odd, -odd], axis=1),
        ],
        axis=0,
    ).astype(np.float32)
    return project, expand


def row_table():
    u0 = np.arange(U0)[None, None, :]
    l0 = np.arange(L0)[:, None, None]
    l1 = np.arange(L1)[None, :, None]
    a = 2.0 * np.pi * ((u0 * (l0 + L0 * l1)) % N) / N
    c, s = np.cos(a).astype(ml_dtypes.bfloat16), np.sin(a).astype(ml_dtypes.bfloat16)
    table = np.concatenate(
        [np.concatenate([c, -s], axis=2), np.concatenate([s, c], axis=2)], axis=1
    )
    return np.stack([table[0::2], table[1::2]])


def project_kernel(count_ref, ku_ref, kv_ref, vis_ref, table_ref, mark_ref, out_ref, *, first):
    step = pl.program_id(0)
    slots = lax.broadcasted_iota(jnp.int32, (2, ku_ref.shape[1]), 1)
    owners, rows, _ = out_ref.shape
    table = table_ref[...]
    mark = jnp.concatenate([mark_ref[...], mark_ref[...]], axis=1)
    line = lax.broadcasted_iota(jnp.int32, (rows, 2 * S), 0)
    for pair in range(STEP // 2):
        subs = []
        for b in (2 * pair, 2 * pair + 1):
            live = count_ref[first + step * STEP + b]
            vis = jnp.where(slots < live, vis_ref[b].astype(jnp.float32), 0.0)
            kv_t = kv_ref[b].astype(jnp.float32).T
            weighted = jnp.concatenate([kv_t * vis[0:1, :], kv_t * vis[1:2, :]], axis=0)
            subs.append(
                jnp.dot(
                    weighted.astype(jnp.bfloat16), ku_ref[b], preferred_element_type=jnp.float32
                ).astype(jnp.bfloat16)
            )
        out = jnp.dot(
            table, jnp.concatenate(subs, axis=1), preferred_element_type=jnp.float32
        ).reshape(owners, rows, 2 * S)
        out = jnp.where((line == MARK)[None], mark[None], out)
        out_ref[:, :, pair * 2 * S : (pair + 1) * 2 * S] = out.astype(jnp.bfloat16)


def project_chunk(count, ku, kv, vis, table, mark, owners, chunk, size):
    slots = ku.shape[1]
    at = chunk * size // STEP
    return pl.pallas_call(
        functools.partial(project_kernel, first=chunk * size),
        out_shape=jax.ShapeDtypeStruct((owners, 4 * RANK, size * S), jnp.bfloat16),
        grid_spec=pltpu.PrefetchScalarGridSpec(
            num_scalar_prefetch=1,
            grid=(size // STEP,),
            in_specs=[
                pl.BlockSpec((STEP, slots, S), lambda b, _: (at + b, 0, 0)),
                pl.BlockSpec((STEP, slots, S), lambda b, _: (at + b, 0, 0)),
                pl.BlockSpec((STEP, 2, slots), lambda b, _: (at + b, 0, 0)),
                pl.BlockSpec(table.shape, lambda b, _: (0, 0)),
                pl.BlockSpec(mark.shape, lambda b, _: (0, 0)),
            ],
            out_specs=pl.BlockSpec((owners, 4 * RANK, STEP * S), lambda b, _: (0, 0, b)),
        ),
        compiler_params=pltpu.CompilerParams(vmem_limit_bytes=60 * MIB),
        cost_estimate=pl.CostEstimate(
            flops=size * 2 * (256 * 256 * 128 + 512 * 256 * 128),
            bytes_accessed=size * 4 * 65536,
            transcendentals=0,
        ),
    )(count, ku, kv, vis, table, mark)


def add_blocks(row_ref, got_ref, phase_ref, expand_ref, acc_ref, chunk, size, per_src):
    table = expand_ref[...]
    r = RANK

    def per_source(src, carry):
        for b in range(size):
            g = src * per_src + chunk * size + b
            row = row_ref[g]
            ph = phase_ref[pl.ds(g, 1), :]
            swapped = jnp.concatenate([ph[:, COLS:], ph[:, :COLS]], axis=1)
            weights = jnp.concatenate(
                [
                    table[0:r] * ph,
                    table[r : 2 * r] * swapped,
                    table[2 * r : 3 * r] * swapped,
                    table[3 * r : 4 * r] * ph,
                ],
                axis=0,
            ).astype(jnp.bfloat16)
            coeffs = got_ref[src, :, b * S : (b + 1) * S]
            rows = lax.dot_general(
                coeffs, weights, (((0,), (0,)), ((), ())), preferred_element_type=jnp.float32
            )
            for c in range(4):
                acc_ref[c, pl.ds(row, S), :] += rows[:, c * 128 : (c + 1) * 128]
        return carry

    lax.fori_loop(0, got_ref.shape[0], per_source, 0)


def grid_kernel(row_ref, got_ref, phase_ref, expand_ref, out_ref, *, chunk, size, per_src):
    out_ref[...] = jnp.zeros_like(out_ref)
    add_blocks(row_ref, got_ref, phase_ref, expand_ref, out_ref, chunk, size, per_src)


def grid_chunk(rows, got, phase, expand, chunk, size, per_src):
    vmem = pl.BlockSpec(memory_space=pltpu.VMEM)
    return pl.pallas_call(
        functools.partial(grid_kernel, chunk=chunk, size=size, per_src=per_src),
        out_shape=jax.ShapeDtypeStruct((4, HALF, 128), jnp.float32),
        in_specs=[pl.BlockSpec(memory_space=pltpu.SMEM), vmem, vmem, vmem],
        out_specs=vmem,
        compiler_params=pltpu.CompilerParams(vmem_limit_bytes=56 * MIB),
        cost_estimate=pl.CostEstimate(
            flops=got.shape[0] * size * 2 * 128 * 256 * 512,
            bytes_accessed=12 * MIB,
            transcendentals=0,
        ),
    )(rows, got, phase, expand)


def dft8(x):
    def add(p, q):
        return (p[0] + q[0], p[1] + q[1])

    def sub(p, q):
        return (p[0] - q[0], p[1] - q[1])

    def turn(p):
        return (-p[1], p[0])

    def dft4(a, b, c, d):
        s, t, v, w = add(a, c), sub(a, c), add(b, d), turn(sub(b, d))
        return add(s, v), add(t, w), sub(s, v), sub(t, w)

    h = math.sqrt(0.5)
    e = dft4(x[0], x[2], x[4], x[6])
    o = list(dft4(x[1], x[3], x[5], x[7]))
    o[1] = ((o[1][0] - o[1][1]) * h, (o[1][0] + o[1][1]) * h)
    o[2] = turn(o[2])
    o[3] = ((-o[3][0] - o[3][1]) * h, (o[3][0] - o[3][1]) * h)
    return [add(e[k], o[k]) for k in range(4)] + [sub(e[k], o[k]) for k in range(4)]


def finish(place_ref, table_ref, mid_ref, screen_ref, full_ref, keep_ref, send_ref, ready):
    def last_step(k, carry):
        ready(k)
        planar = jnp.dot(table_ref[k], mid_ref[k], preferred_element_type=jnp.float32)
        value = planar[:L1] * screen_ref[k, 0] - planar[L1:] * screen_ref[k, 1]
        full_ref[:, k] = value.astype(jnp.bfloat16).reshape(L1 // 16, 16, COLS)
        return carry

    lax.fori_loop(0, L0 // 2, last_step, 0)
    for out_ref, which in ((keep_ref, 0), (send_ref, 1)):
        for i in range(out_ref.shape[0]):
            out_ref[i] = full_ref[place_ref[which, i]]


def even_kernel(
    row_ref, place_ref, got_ref, phase_ref, expand_ref, old_hbm, table_hbm, screen_hbm,
    keep_ref, send_ref, odd_ref, acc_ref, old_ref, table_ref, mid_ref, screen_ref, full_ref, sems,
    *, chunk, size, per_src,
):
    load_old = pltpu.make_async_copy(old_hbm, old_ref, sems.at[0])
    load_table = pltpu.make_async_copy(table_hbm.at[0], table_ref, sems.at[1])
    load_screen = pltpu.make_async_copy(screen_hbm.at[pl.ds(0, L0 // 2)], screen_ref, sems.at[2])
    load_old.start()
    load_table.start()
    load_screen.start()
    acc_ref[...] = jnp.zeros_like(acc_ref)
    add_blocks(row_ref, got_ref, phase_ref, expand_ref, acc_ref, chunk, size, per_src)
    load_old.wait()

    def first_step(i, carry):
        at = pl.multiple_of(i * 16, 16)
        for half in range(2):
            x = [
                tuple(
                    acc_ref[2 * p + half, pl.ds(at + U0 * k, 16), :]
                    + old_ref[2 * p + half, pl.ds(at + U0 * k, 16), :]
                    for p in range(2)
                )
                for k in range(U1)
            ]
            even = dft8(x)
            for k in range(1, U1):
                c, s = math.cos(math.pi * k / U1), math.sin(math.pi * k / U1)
                x[k] = (x[k][0] * c - x[k][1] * s, x[k][0] * s + x[k][1] * c)
            for ref, out in ((mid_ref, even), (odd_ref, dft8(x))):
                for k in range(L0 // 2):
                    for p in range(2):
                        ref[k, pl.ds(U0 * p + at, 16), half * 128 : (half + 1) * 128] = out[k][
                            p
                        ].astype(jnp.bfloat16)
        return carry

    lax.fori_loop(0, U0 // 16, first_step, 0)
    load_table.wait()
    load_screen.wait()
    finish(
        place_ref, table_ref, mid_ref, screen_ref, full_ref, keep_ref, send_ref, lambda k: None
    )


def odd_kernel(
    place_ref, mid_ref, table_hbm, screen_hbm,
    keep_ref, send_ref, table_ref, screen_ref, full_ref, sems,
):
    def loads(k):
        return (
            pltpu.make_async_copy(table_hbm.at[1, k], table_ref.at[k], sems.at[0, k]),
            pltpu.make_async_copy(screen_hbm.at[L0 // 2 + k], screen_ref.at[k], sems.at[1, k]),
        )

    for k in range(L0 // 2):
        for load in loads(k):
            load.start()

    def ready(k):
        for load in loads(k):
            load.wait()

    finish(place_ref, table_ref, mid_ref, screen_ref, full_ref, keep_ref, send_ref, ready)


def make_image(rows, place, got, phase, expand, old, table, screen, chunk, size, per_src):
    vmem = pl.BlockSpec(memory_space=pltpu.VMEM)
    smem = pl.BlockSpec(memory_space=pltpu.SMEM)
    hbm = pl.BlockSpec(memory_space=pl.ANY)
    half = L0 // 2
    piece = jax.ShapeDtypeStruct((place.shape[1], half, 16, COLS), jnp.bfloat16)
    mid = (half, 2 * U0, COLS)
    buffers = [
        pltpu.VMEM(table.shape[1:], jnp.bfloat16),
        pltpu.VMEM((half, *screen.shape[1:]), jnp.float32),
        pltpu.VMEM((16, half, 16, COLS), jnp.bfloat16),
    ]
    keep, send, odd = pl.pallas_call(
        functools.partial(even_kernel, chunk=chunk, size=size, per_src=per_src),
        out_shape=(piece, piece, jax.ShapeDtypeStruct(mid, jnp.bfloat16)),
        in_specs=[smem, smem, vmem, vmem, vmem, hbm, hbm, hbm],
        out_specs=(vmem, vmem, vmem),
        scratch_shapes=[
            pltpu.VMEM(old.shape, jnp.float32),
            pltpu.VMEM(old.shape, jnp.float32),
            buffers[0],
            pltpu.VMEM(mid, jnp.bfloat16),
            *buffers[1:],
            pltpu.SemaphoreType.DMA((3,)),
        ],
        compiler_params=pltpu.CompilerParams(vmem_limit_bytes=50 * MIB),
        cost_estimate=pl.CostEstimate(
            flops=16 * 1024**3, bytes_accessed=24 * MIB, transcendentals=0
        ),
    )(rows, place, got, phase, expand, old, table, screen)
    keep_odd, send_odd = pl.pallas_call(
        odd_kernel,
        out_shape=(piece, piece),
        in_specs=[smem, vmem, hbm, hbm],
        out_specs=(vmem, vmem),
        scratch_shapes=[*buffers, pltpu.SemaphoreType.DMA((2, half))],
        compiler_params=pltpu.CompilerParams(vmem_limit_bytes=60 * MIB),
        cost_estimate=pl.CostEstimate(
            flops=4 * 1024**3, bytes_accessed=12 * MIB, transcendentals=0
        ),
    )(place, odd, table, screen)
    return (keep, send), (keep_odd, send_odd)


def screen_kernel(base_ref, w_ref, out_ref, *, scale):
    k = pl.program_id(0)
    l0 = 2 * lax.rem(k, L0 // 2) + k // (L0 // 2)
    row = l0 + L0 * lax.broadcasted_iota(jnp.int32, (L1, COLS), 0)
    col = base_ref[0] + lax.broadcasted_iota(jnp.int32, (L1, COLS), 1)
    cell = 2.0 * FIELD / N
    dl = row.astype(jnp.float32) * cell
    dm = col.astype(jnp.float32) * cell
    lift = jnp.sqrt(1.0 - dl * dl - dm * dm) - 1.0
    quarters = (4.0 * w_ref[0]) * lift
    whole = jnp.floor(quarters + 0.5)
    f = quarters - whole
    count = whole.astype(jnp.int32) - row - col
    t = f * f
    h = math.pi / 2
    sine, cosine = 0.0, 0.0
    for n in (11, 9, 7, 5, 3, 1):
        sine = sine * t + (-1) ** (n // 2) * h**n / math.factorial(n)
    for n in (12, 10, 8, 6, 4, 2, 0):
        cosine = cosine * t + (-1) ** (n // 2) * h**n / math.factorial(n)
    sine = sine * f
    odd = (count & 1) == 1
    c = jnp.where(odd, sine, cosine)
    s = jnp.where(odd, cosine, sine)
    out_ref[0, 0] = jnp.where(((count + 1) & 2) == 2, -scale, scale) * c
    out_ref[0, 1] = jnp.where((count & 2) == 2, -scale, scale) * s


def make_screen(base, w, scale):
    smem = pl.BlockSpec(memory_space=pltpu.SMEM)
    return pl.pallas_call(
        functools.partial(screen_kernel, scale=scale),
        out_shape=jax.ShapeDtypeStruct((L0, 2, L1, COLS), jnp.float32),
        grid=(L0,),
        in_specs=[smem, smem],
        out_specs=pl.BlockSpec((1, 2, L1, COLS), lambda k: (k, 0, 0, 0)),
        compiler_params=pltpu.CompilerParams(vmem_limit_bytes=60 * MIB),
        cost_estimate=pl.CostEstimate(
            flops=40 * HALF * COLS, bytes_accessed=8 * MIB, transcendentals=HALF * COLS
        ),
    )(base, w)


def sum_planes(keep, send, planes):
    def shifted(values, target):
        pairs = [(i, target(i)) for i in range(planes)]
        return lax.ppermute(values, "wa", pairs).astype(jnp.float32)

    total = keep.astype(jnp.float32) + shifted(send, lambda i: i ^ 1)
    total = total.astype(jnp.bfloat16).reshape(4, 2, L0 // 2, 16, COLS)
    got = [
        shifted(total[step], lambda i, step=step: (i + 4 * step) % planes) for step in (1, 2, 3)
    ]
    total = (total[0].astype(jnp.float32) + got[0] + got[1] + got[2]).astype(jnp.bfloat16)
    return total[0].astype(jnp.float32) + shifted(total[1], lambda i: i ^ 2)


def body(kernel_u, kernel_v, visibilities, vis_count, tile_route, block_offset, plane_w):
    n_tu, n_tv, planes = lax.axis_size("tu"), lax.axis_size("tv"), lax.axis_size("wa")
    owners = n_tu * n_tv
    blocks, slots = kernel_u.shape[0], kernel_u.shape[1]
    size = blocks // CHUNKS
    project, expand = factor_tables(owners)
    table = row_table()

    target = tile_route[:, 0]
    corner = jnp.stack(
        [target // n_tv * TILE + block_offset[:, 0], target % n_tv * TILE + block_offset[:, 1]],
        axis=0,
    )
    halves = jnp.stack([corner // 64, corner % 64], axis=1).reshape(1, 4 * blocks)
    mark = jnp.pad(halves, ((0, 0), (0, S - 4 * blocks))).astype(jnp.float32)
    owner = lax.axis_index(("tu", "tv"))
    col_base = owner * COLS
    scale = 1.0 / math.sqrt(slots * blocks * owners * 16)
    screen = make_screen(col_base.reshape(1), plane_w, scale)
    got = []
    for chunk in range(CHUNKS):
        coeffs = project_chunk(
            vis_count, kernel_u, kernel_v, visibilities, project, mark, owners, chunk, size
        )
        if chunk:
            coeffs, screen = lax.optimization_barrier((coeffs, screen))
        got.append(
            lax.all_to_all(coeffs, ("tu", "tv"), split_axis=0, concat_axis=0, tiled=True)
        )
    marks = got[0][:, MARK, : 4 * blocks].astype(jnp.int32).reshape(owners, 2, 2, blocks)
    corners = marks[:, :, 0] * 64 + marks[:, :, 1]
    rows = corners[:, 0, :].reshape(-1)
    cols = corners[:, 1, :].reshape(-1)

    lane = jnp.arange(COLS, dtype=jnp.int32)
    turns = (cols[:, None] * (col_base + lane)[None, :]) % N
    shift = (S - 1) / 2 * (lane.astype(jnp.float32) - (COLS - 1) / 2)
    angle = (turns.astype(jnp.float32) + shift[None, :]) * (2.0 * math.pi / N)
    phase = jnp.concatenate([jnp.cos(angle), jnp.sin(angle)], axis=1)

    me = lax.axis_index("wa")
    core, z_hi, x = me % 2, me // 2 % 2, me // 4
    step = jnp.arange(8, dtype=jnp.int32)
    pair = ((x + step // 2) % 4) * 4 + (z_hi ^ (step % 2)) * 2
    place = jnp.stack([pair + core, pair + (1 - core)])

    acc = grid_chunk(rows, got[0], phase, expand, 0, size, blocks)
    halves = make_image(
        rows, place, got[1], phase, expand, acc, table, screen, 1, size, blocks
    )
    if planes != 16:
        return halves
    even, odd = (sum_planes(keep, send, planes) for keep, send in halves)
    return jnp.stack([even, odd], axis=1).transpose(2, 0, 1, 3).reshape(L0 * 16, COLS)


def solution(mesh):
    split = ("wa", "tu", "tv")
    placed = (
        P(split, None, None),
        P(split, None, None),
        P(split, None, None),
        P(split),
        P(split, None),
        P(split, None),
        P("wa"),
    )
    return jax.shard_map(
        body, mesh=mesh, in_specs=placed, out_specs=P("wa", ("tu", "tv")), check_vma=False
    )
```

time: 200 us -> 129 us (0.65); the launches traced: 197 us -> 128 us
  blocking collectives: 53.2 us -> 0 us
  other arithmetic: 27.6 us -> 4.92 us
  waiting for transfers between devices: 18.5 us -> 30.3 us
  local copies, waits for them, and re-layouts: 10.2 us -> 2.1 us
  starting transfers between devices: 21.8 us -> 29.7 us
  Pallas kernels: 64.7 us -> 60.3 us
    all_gather x1 -> x0, blocking collectives: 53.2 us -> none  [body(): corners = lax.all_gather(corner, ('tu', 'tv'), axis=0)]
    all_to_all x2, waiting for transfers between devices: 0.01 us -> 23.3 us  [body(): lax.all_to_all(coeffs, ('tu', 'tv'), split_axis=0, concat_axis=0, tiled=T...]
    cos x1 -> x0, other arithmetic: 19 us -> none  [screen_parts(): return jnp.stack([jnp.cos(angle), jnp.sin(angle)]) * scale]
    ppermute x5 -> x10, waiting for transfers between devices: 18.5 us -> 7 us  [shifted(): return lax.ppermute(values, 'wa', pairs).astype(jnp.float32)]
    unnamed x34 -> x10, local copies, waits for them, and re-layouts: 9.08 us -> 0.02 us
    pallas_call x3 -> x5, Pallas kernels: 56.2 us -> 47.7 us  [the longest x1 18.8 us: make_image(): pl.pallas_call(functools.partial(even_kernel, chunk=chunk, size=size, per...]
    ppermute x5 -> x10, starting transfers between devices: 9.54 us -> 17.4 us  [shifted(): return lax.ppermute(values, 'wa', pairs).astype(jnp.float32)]
    mul x2 -> x0, other arithmetic: 4.22 us -> none  [the longest x1 4.21 us: screen_parts(): return jnp.stack([jnp.cos(angle), jnp.sin(angle)]) * scale]
  transfers between devices with their start and end apart: 7 -> 12, of which waited for: 5 -> 4; matrix products, arithmetic and copies ran while one was open for 13% -> 3% of each run, Pallas kernels for 7% -> 29%
where the time goes in v2:
time: 129 us; the launch traced here: 128 us
  Pallas kernels  60.3 us (47%)
  waiting for transfers between devices  30.3 us (23%)
  starting transfers between devices  29.7 us (23%)
  other arithmetic  4.92 us (4%)
  local copies, waits for them, and re-layouts  2.1 us (2%)
    all_to_all x2, waiting for transfers between devices, body(): lax.all_to_all(coeffs, ('tu', 'tv'), split_axis=0, concat_axis=0, tiled=T...  23.3 us
    pallas_call x1, Pallas kernels, make_image(): pl.pallas_call(functools.partial(even_kernel, chunk=chunk, size=size, per...  18.8 us
    ppermute x10, starting transfers between devices, shifted(): return lax.ppermute(values, 'wa', pairs).astype(jnp.float32)  17.4 us
    pallas_call x1, Pallas kernels, grid_chunk(): pl.pallas_call(functools.partial(grid_kernel, chunk=chunk, size=size, per...  12.6 us
    all_to_all x2, starting transfers between devices, body(): lax.all_to_all(coeffs, ('tu', 'tv'), split_axis=0, concat_axis=0, tiled=T...  12.3 us
    pallas_call x1, Pallas kernels, make_screen(): pl.pallas_call(functools.partial(screen_kernel, scale=scale), out_shape=j...  11.4 us
    pallas_call x2, Pallas kernels, project_chunk(): pl.pallas_call(functools.partial(project_kernel, first=chunk * size), out...  9.02 us
    pallas_call x1, Pallas kernels, make_image(): pl.pallas_call(odd_kernel, out_shape=(piece, piece), in_specs=[smem, vmem...  8.47 us
  transfers between devices with their start and end apart: 12, of which 4 were waited for; matrix products, arithmetic and copies ran while one was open for 3% of the time, Pallas kernels for 29%

profile of v2, /device:TPU:2, one launch (start us, length us, event | category | flops | bytes accessed | tf_op | source)
XLA Modules:
  0.0 128.2 jit_solution(694887402566760834)
XLA Ops:
  0.0 0.8 fusion.17
  1.4 4.5 %shard_map.100 = bf16[16,32,1024]{2,1,0:T(8,128)(2,1)} custom-call(s32[16]{0:T(128)} %count_ref.3, bf16[16,256,128]{2,1,0:T(8,128)(2,1)} %ku_ref.3, bf16[16,256,128]{2,1,0:T(8,128)(2,1)} %kv_ref.3, bf16[16,2,256]{2,1,0:T(2,128)(2,1)} %vis_ref.3, bf16[512,256]{1,0:T(8,128)(2,1)} %constant.159.clone.table_ref, f32[1,128]{1,0:T(1,128)} %pad_convert_fusion.mark_ref), custom_call_target="tpu_custom_call" | custom-call | flops 402653184 | bytes 2097152 | tf_op jit(solution)/shard_map/pallas_call | solution.py:104
  5.9 8.6 %all-to-all-start = ((bf16[16,32,1024]{2,1,0:T(8,128)(2,1)}), bf16[16,32,1024]{2,1,0:T(8,128)(2,1)S(1)}, u32[]{:S(2)}, u32[]{:S(2)}) async-start(bf16[16,32,1024]{2,1,0:T(8,128)(2,1)} %shard_map.100), calls=%async_computation | async-start | bytes 2097152 | tf_op jit(solution)/shard_map/all_to_all | solution.py:411
  15.2 11.4 %shard_map.102.screen_hbm = f32[16,2,256,256]{3,2,1,0:T(8,128)} custom-call(s32[1]{0:T(128)} %bitcast.6.base_ref, f32[1]{0:T(128)S(6)} %copy.12.w_ref), custom_call_target="tpu_custom_call" | custom-call | flops 41943040 | bytes 8388608 | tf_op jit(solution)/shard_map/pallas_call | solution.py:357
  26.7 4.5 %shard_map.101 = bf16[16,32,1024]{2,1,0:T(8,128)(2,1)} custom-call(s32[16]{0:T(128)} %count_ref.3, bf16[16,256,128]{2,1,0:T(8,128)(2,1)} %ku_ref.3, bf16[16,256,128]{2,1,0:T(8,128)(2,1)} %kv_ref.3, bf16[16,2,256]{2,1,0:T(2,128)(2,1)} %vis_ref.3, bf16[512,256]{1,0:T(8,128)(2,1)} %constant.159.clone.table_ref, f32[1,128]{1,0:T(1,128)} %pad_convert_fusion.mark_ref), custom_call_target="tpu_custom_call" | custom-call | flops 402653184 | bytes 2097152 | tf_op jit(solution)/shard_map/pallas_call | solution.py:104
  31.2 11.2 %all-to-all-done.got_ref = bf16[16,32,1024]{2,1,0:T(8,128)(2,1)S(1)} async-done(((bf16[16,32,1024]{2,1,0:T(8,128)(2,1)}), bf16[16,32,1024]{2,1,0:T(8,128)(2,1)S(1)}, u32[]{:S(2)}, u32[]{:S(2)}) %all-to-all-start) | async-done | bytes 1048608 | tf_op jit(solution)/shard_map/all_to_all | solution.py:411
  42.4 3.7 %all-to-all-start.1 = ((bf16[16,32,1024]{2,1,0:T(8,128)(2,1)}), bf16[16,32,1024]{2,1,0:T(8,128)(2,1)S(1)}, u32[]{:S(2)}, u32[]{:S(2)}) async-start(bf16[16,32,1024]{2,1,0:T(8,128)(2,1)} %shard_map.101), calls=%async_computation.1 | async-start | bytes 2097152 | tf_op jit(solution)/shard_map/all_to_all | solution.py:411
  47.1 1.1 fusion.7
  48.2 0.9 pad_maximum_fusion.phase_ref
  49.1 12.6 %shard_map.103.old_hbm = f32[4,4096,128]{2,1,0:T(8,128)} custom-call(s32[256]{0:T(256)} %reshape_squeeze.3.row_ref, bf16[16,32,1024]{2,1,0:T(8,128)(2,1)} %copy-done.4, f32[256,512]{1,0:T(8,128)} %pad_maximum_fusion.phase_ref, f32[32,512]{1,0:T(8,128)} %constant.160.clone.expand_ref), custom_call_target="tpu_custom_call" | custom-call | flops 4294967296 | bytes 12582912 | tf_op jit(solution)/shard_map/pallas_call | solution.py:165
  61.7 12.1 %all-to-all-done.1.got_ref = bf16[16,32,1024]{2,1,0:T(8,128)(2,1)S(1)} async-done(((bf16[16,32,1024]{2,1,0:T(8,128)(2,1)}), bf16[16,32,1024]{2,1,0:T(8,128)(2,1)S(1)}, u32[]{:S(2)}, u32[]{:S(2)}) %all-to-all-start.1) | async-done | bytes 1048608 | tf_op jit(solution)/shard_map/all_to_all | solution.py:411
  73.8 18.8 %shard_map.104 = (bf16[8,8,16,256]{3,2,1,0:T(8,128)(2,1)S(1)}, bf16[8,8,16,256]{3,2,1,0:T(8,128)(2,1)S(1)}, bf16[8,1024,256]{2,1,0:T(8,128)(2,1)}) custom-call(s32[256]{0:T(256)S(1)} %copy-done.2, s32[2,8]{1,0:T(2,128)S(1)} %pad_add_fusion.2.place_ref, bf16[16,32,1024]{2,1,0:T(8,128)(2,1)S(1)} %all-to-all-done.1.got_ref, f32[256,512]{1,0:T(8,128)S(1)} %copy-done, ...), custom_call_target="tpu_custom_call" | custom-call | flops 17179869184 | bytes 25165824 | tf_op jit(solution)/shard_map/pallas_call | solution.py:295
  92.7 8.5 %shard_map.105 = (bf16[8,8,16,256]{3,2,1,0:T(8,128)(2,1)}, bf16[8,8,16,256]{3,2,1,0:T(8,128)(2,1)}) custom-call(s32[2,8]{1,0:T(2,128)} %copy-done.1, bf16[8,1024,256]{2,1,0:T(8,128)(2,1)} %get-tuple-element.16.mid_ref, bf16[2,8,512,1024]{3,2,1,0:T(8,128)(2,1)} %constant.161.clone.table_hbm, f32[16,2,256,256]{3,2,1,0:T(8,128)} %shard_map.102.screen_hbm), custom_call_target="tpu_custom_call" | custom-call | flops 4294967296 | bytes 12582912 | tf_op jit(solution)/shard_map/pallas_call | solution.py:313
  101.9 1.6 %collective-permute-start.1 = (bf16[2,8,16,256]{3,2,1,0:T(8,128)(2,1)S(1)}, bf16[2,8,16,256]{3,2,1,0:T(8,128)(2,1)S(1)}, u32[]{:S(2)}, u32[]{:S(2)}) collective-permute-start(bf16[2,8,16,256]{3,2,1,0:T(8,128)(2,1)S(1)} %get-tuple-element.23), channel_id=1, source_target_pairs={{0,64},{16,80},{32,96},{48,112},{64,128},{80,144},{96,160},{112,17... | collective-permute-start | bytes 393224 | tf_op jit(solution)/shard_map/ppermute | solution.py:373
  104.0 2.1 %collective-permute-start.2 = (bf16[2,8,16,256]{3,2,1,0:T(8,128)(2,1)S(1)}, bf16[2,8,16,256]{3,2,1,0:T(8,128)(2,1)S(1)}, u32[]{:S(2)}, u32[]{:S(2)}) collective-permute-start(bf16[2,8,16,256]{3,2,1,0:T(8,128)(2,1)S(1)} %get-tuple-element.25), channel_id=1, source_target_pairs={{0,128},{16,144},{32,160},{48,176},{64,192},{80,208},{96,224},{112... | collective-permute-start | bytes 393224 | tf_op jit(solution)/shard_map/ppermute | solution.py:373
  106.1 1.2 add_convert_fusion
  107.4 1.1 collective-permute-start.6
  108.5 1.0 collective-permute-start.8
  109.5 1.5 %collective-permute-start.7 = (bf16[2,8,16,256]{3,2,1,0:T(8,128)(2,1)S(1)}, bf16[2,8,16,256]{3,2,1,0:T(8,128)(2,1)S(1)}, u32[]{:S(2)}, u32[]{:S(2)}) collective-permute-start(bf16[2,8,16,256]{3,2,1,0:T(8,128)(2,1)S(1)} %get-tuple-element.28), channel_id=1, source_target_pairs={{0,128},{16,144},{32,160},{48,176},{64,192},{80,208},{96,224},{112... | collective-permute-start | bytes 393224 | tf_op jit(solution)/shard_map/ppermute | solution.py:373
  111.0 2.4 %collective-permute-done.2 = bf16[2,8,16,256]{3,2,1,0:T(8,128)(2,1)S(1)} collective-permute-done((bf16[2,8,16,256]{3,2,1,0:T(8,128)(2,1)S(1)}, bf16[2,8,16,256]{3,2,1,0:T(8,128)(2,1)S(1)}, u32[]{:S(2)}, u32[]{:S(2)}) %collective-permute-start.2) | collective-permute-done | bytes 131104 | tf_op jit(solution)/shard_map/ppermute | solution.py:373
  113.4 4.6 %collective-permute-start.4 = (bf16[8,16,256]{2,1,0:T(8,128)(2,1)S(1)}, bf16[8,16,256]{2,1,0:T(8,128)(2,1)S(1)}, u32[]{:S(2)}, u32[]{:S(2)}) collective-permute-start(bf16[8,16,256]{2,1,0:T(8,128)(2,1)S(1)} %slice_bitcast_fusion.2), channel_id=1, source_target_pairs={{0,32},{16,48},{32,0},{48,16},{64,96},{80,112},{96,64},{112,80},{1... | collective-permute-start | bytes 196616 | tf_op jit(solution)/shard_map/ppermute | solution.py:373
  118.2 4.3 %collective-permute-start.9 = (bf16[8,16,256]{2,1,0:T(8,128)(2,1)S(1)}, bf16[8,16,256]{2,1,0:T(8,128)(2,1)S(1)}, u32[]{:S(2)}, u32[]{:S(2)}) collective-permute-start(bf16[8,16,256]{2,1,0:T(8,128)(2,1)S(1)} %slice_bitcast_fusion), channel_id=1, source_target_pairs={{0,32},{16,48},{32,0},{48,16},{64,96},{80,112},{96,64},{112,80},{1... | collective-permute-start | bytes 196616 | tf_op jit(solution)/shard_map/ppermute | solution.py:373
  122.4 4.6 %collective-permute-done.9 = bf16[8,16,256]{2,1,0:T(8,128)(2,1)S(1)} collective-permute-done((bf16[8,16,256]{2,1,0:T(8,128)(2,1)S(1)}, bf16[8,16,256]{2,1,0:T(8,128)(2,1)S(1)}, u32[]{:S(2)}, u32[]{:S(2)}) %collective-permute-start.9) | collective-permute-done | bytes 65568 | tf_op jit(solution)/shard_map/ppermute | solution.py:373
  127.3 0.9 reshape.585
  (47 shorter events, 3.4 us)
Async XLA Ops:
  5.9 36.4 %all-to-all-start = ((bf16[16,32,1024]{2,1,0:T(8,128)(2,1)}), bf16[16,32,1024]{2,1,0:T(8,128)(2,1)S(1)}, u32[]{:S(2)}, u32[]{:S(2)}) async-start(bf16[16,32,1024]{2,1,0:T(8,128)(2,1)} %shard_map.100), calls=%async_computation | async-start | bytes 2097152 | tf_op jit(solution)/shard_map/all_to_all | solution.py:411
  42.4 6.7 %copy-start.4 = (bf16[16,32,1024]{2,1,0:T(8,128)(2,1)}, bf16[16,32,1024]{2,1,0:T(8,128)(2,1)S(1)}, u32[]{:S(2)}) copy-start(bf16[16,32,1024]{2,1,0:T(8,128)(2,1)S(1)} %all-to-all-done.got_ref) | copy-start | bytes 3145732
  42.4 31.4 %all-to-all-start.1 = ((bf16[16,32,1024]{2,1,0:T(8,128)(2,1)}), bf16[16,32,1024]{2,1,0:T(8,128)(2,1)S(1)}, u32[]{:S(2)}, u32[]{:S(2)}) async-start(bf16[16,32,1024]{2,1,0:T(8,128)(2,1)} %shard_map.101), calls=%async_computation.1 | async-start | bytes 2097152 | tf_op jit(solution)/shard_map/all_to_all | solution.py:411
  46.1 27.6 %copy-start.1 = (s32[2,8]{1,0:T(2,128)}, s32[2,8]{1,0:T(2,128)S(1)}, u32[]{:S(2)}) copy-start(s32[2,8]{1,0:T(2,128)S(1)} %pad_add_fusion.2.place_ref) | copy-start | bytes 196
  48.2 25.6 %copy-start.2 = (s32[256]{0:T(256)S(1)}, s32[256]{0:T(256)}, u32[]{:S(2)}) copy-start(s32[256]{0:T(256)} %reshape_squeeze.3.row_ref) | copy-start | bytes 3076
  48.2 25.6 %copy-start.3 = (f32[32,512]{1,0:T(8,128)S(1)}, f32[32,512]{1,0:T(8,128)}, u32[]{:S(2)}) copy-start(f32[32,512]{1,0:T(8,128)} %constant.160.clone.expand_ref) | copy-start | bytes 196612
  49.1 24.7 %copy-start = (f32[256,512]{1,0:T(8,128)S(1)}, f32[256,512]{1,0:T(8,128)}, u32[]{:S(2)}) copy-start(f32[256,512]{1,0:T(8,128)} %pad_maximum_fusion.phase_ref) | copy-start | bytes 1572868
  92.6 9.2 %collective-permute-start = (bf16[8,8,16,256]{3,2,1,0:T(8,128)(2,1)S(1)}, bf16[8,8,16,256]{3,2,1,0:T(8,128)(2,1)S(1)}, u32[]{:S(2)}, u32[]{:S(2)}) collective-permute-start(bf16[8,8,16,256]{3,2,1,0:T(8,128)(2,1)S(1)} %get-tuple-element.15), channel_id=1, source_target_pairs={{0,16},{16,0},{32,48},{48,32},{64,80},{80,64},{96,112},{112,96},{1... | collective-permute-start | bytes 1572872 | tf_op jit(solution)/shard_map/ppermute | solution.py:373
  101.1 5.0 %collective-permute-start.5 = (bf16[8,8,16,256]{3,2,1,0:T(8,128)(2,1)}, bf16[8,8,16,256]{3,2,1,0:T(8,128)(2,1)S(1)}, u32[]{:S(2)}, u32[]{:S(2)}) collective-permute-start(bf16[8,8,16,256]{3,2,1,0:T(8,128)(2,1)} %get-tuple-element.18), channel_id=1, source_target_pairs={{0,16},{16,0},{32,48},{48,32},{64,80},{80,64},{96,112},{112,96},{1... | collective-permute-start | bytes 1572872 | tf_op jit(solution)/shard_map/ppermute | solution.py:373
  101.9 7.6 %collective-permute-start.1 = (bf16[2,8,16,256]{3,2,1,0:T(8,128)(2,1)S(1)}, bf16[2,8,16,256]{3,2,1,0:T(8,128)(2,1)S(1)}, u32[]{:S(2)}, u32[]{:S(2)}) collective-permute-start(bf16[2,8,16,256]{3,2,1,0:T(8,128)(2,1)S(1)} %get-tuple-element.23), channel_id=1, source_target_pairs={{0,64},{16,80},{32,96},{48,112},{64,128},{80,144},{96,160},{112,17... | collective-permute-start | bytes 393224 | tf_op jit(solution)/shard_map/ppermute | solution.py:373
  103.5 7.5 %collective-permute-start.3 = (bf16[2,8,16,256]{3,2,1,0:T(8,128)(2,1)S(1)}, bf16[2,8,16,256]{3,2,1,0:T(8,128)(2,1)S(1)}, u32[]{:S(2)}, u32[]{:S(2)}) collective-permute-start(bf16[2,8,16,256]{3,2,1,0:T(8,128)(2,1)S(1)} %get-tuple-element.24), channel_id=1, source_target_pairs={{0,192},{16,208},{32,224},{48,240},{64,0},{80,16},{96,32},{112,48}... | collective-permute-start | bytes 393224 | tf_op jit(solution)/shard_map/ppermute | solution.py:373
  104.0 9.3 %collective-permute-start.2 = (bf16[2,8,16,256]{3,2,1,0:T(8,128)(2,1)S(1)}, bf16[2,8,16,256]{3,2,1,0:T(8,128)(2,1)S(1)}, u32[]{:S(2)}, u32[]{:S(2)}) collective-permute-start(bf16[2,8,16,256]{3,2,1,0:T(8,128)(2,1)S(1)} %get-tuple-element.25), channel_id=1, source_target_pairs={{0,128},{16,144},{32,160},{48,176},{64,192},{80,208},{96,224},{112... | collective-permute-start | bytes 393224 | tf_op jit(solution)/shard_map/ppermute | solution.py:373
  107.4 10.7 %collective-permute-start.6 = (bf16[2,8,16,256]{3,2,1,0:T(8,128)(2,1)S(1)}, bf16[2,8,16,256]{3,2,1,0:T(8,128)(2,1)S(1)}, u32[]{:S(2)}, u32[]{:S(2)}) collective-permute-start(bf16[2,8,16,256]{3,2,1,0:T(8,128)(2,1)S(1)} %get-tuple-element.26), channel_id=1, source_target_pairs={{0,64},{16,80},{32,96},{48,112},{64,128},{80,144},{96,160},{112,17... | collective-permute-start | bytes 393224 | tf_op jit(solution)/shard_map/ppermute | solution.py:373
  108.5 9.5 %collective-permute-start.8 = (bf16[2,8,16,256]{3,2,1,0:T(8,128)(2,1)S(1)}, bf16[2,8,16,256]{3,2,1,0:T(8,128)(2,1)S(1)}, u32[]{:S(2)}, u32[]{:S(2)}) collective-permute-start(bf16[2,8,16,256]{3,2,1,0:T(8,128)(2,1)S(1)} %get-tuple-element.27), channel_id=1, source_target_pairs={{0,192},{16,208},{32,224},{48,240},{64,0},{80,16},{96,32},{112,48}... | collective-permute-start | bytes 393224 | tf_op jit(solution)/shard_map/ppermute | solution.py:373
  109.5 8.6 %collective-permute-start.7 = (bf16[2,8,16,256]{3,2,1,0:T(8,128)(2,1)S(1)}, bf16[2,8,16,256]{3,2,1,0:T(8,128)(2,1)S(1)}, u32[]{:S(2)}, u32[]{:S(2)}) collective-permute-start(bf16[2,8,16,256]{3,2,1,0:T(8,128)(2,1)S(1)} %get-tuple-element.28), channel_id=1, source_target_pairs={{0,128},{16,144},{32,160},{48,176},{64,192},{80,208},{96,224},{112... | collective-permute-start | bytes 393224 | tf_op jit(solution)/shard_map/ppermute | solution.py:373
  113.4 9.0 %collective-permute-start.4 = (bf16[8,16,256]{2,1,0:T(8,128)(2,1)S(1)}, bf16[8,16,256]{2,1,0:T(8,128)(2,1)S(1)}, u32[]{:S(2)}, u32[]{:S(2)}) collective-permute-start(bf16[8,16,256]{2,1,0:T(8,128)(2,1)S(1)} %slice_bitcast_fusion.2), channel_id=1, source_target_pairs={{0,32},{16,48},{32,0},{48,16},{64,96},{80,112},{96,64},{112,80},{1... | collective-permute-start | bytes 196616 | tf_op jit(solution)/shard_map/ppermute | solution.py:373
  118.2 8.9 %collective-permute-start.9 = (bf16[8,16,256]{2,1,0:T(8,128)(2,1)S(1)}, bf16[8,16,256]{2,1,0:T(8,128)(2,1)S(1)}, u32[]{:S(2)}, u32[]{:S(2)}) collective-permute-start(bf16[8,16,256]{2,1,0:T(8,128)(2,1)S(1)} %slice_bitcast_fusion), channel_id=1, source_target_pairs={{0,32},{16,48},{32,0},{48,16},{64,96},{80,112},{96,64},{112,80},{1... | collective-permute-start | bytes 196616 | tf_op jit(solution)/shard_map/ppermute | solution.py:373

commit v3 on v2

v3 whole, which is shorter than its diff:
```python
import functools
import math

import jax
import jax.numpy as jnp
import ml_dtypes
import numpy as np
from jax import lax
from jax.experimental import pallas as pl
from jax.experimental.pallas import tpu as pltpu
from jax.sharding import PartitionSpec as P

N = 8192
HALF = 4096
S = 128
RANK = 15
STACK = 16
MARK = 15
KEPT = 80
COLS = 256
U0 = 512
U1 = 8
L0 = 16
L1 = 256
TILE = 1024
CHUNKS = 2
FIELD = 0.25
MIB = 1 << 20


def prolate(count, half_band):
    n = np.arange(S)
    diagonal = ((S - 1 - 2 * n) / 2) ** 2 * np.cos(2 * np.pi * half_band)
    beside = n[1:] * (S - n[1:]) / 2
    _, v = np.linalg.eigh(np.diag(diagonal) + np.diag(beside, 1) + np.diag(beside, -1))
    v = v[:, ::-1][:, :count]
    peak = np.argmax(np.abs(v[: S // 2]), axis=0)
    return v * np.sign(v[peak, np.arange(count)])


def factor_tables(owners):
    t = np.arange(S) - (S - 1) / 2
    mu = np.arange(COLS) - (COLS - 1) / 2
    basis = prolate(RANK, COLS / 2 / N)
    spread = basis.T @ np.exp(2j * np.pi * np.outer(t, mu) / N)
    pad = ((0, STACK - RANK), (0, 0))
    basis, spread = np.pad(basis.T, pad), np.pad(spread, pad)
    rows = []
    for j in range(owners):
        centre = COLS * j + (COLS - 1) / 2
        turn = np.exp(2j * np.pi * np.arange(S) * centre / N)
        proj = basis * turn[None, :]
        rows.append(np.concatenate([proj.real, -proj.imag], axis=1))
        rows.append(np.concatenate([proj.imag, proj.real], axis=1))
    project = np.concatenate(rows, axis=0).astype(ml_dtypes.bfloat16)
    sr, si = spread.real, spread.imag
    by_cos = np.block([[sr, si], [-si, sr]]).astype(np.float32)
    by_sin = np.block([[-si, sr], [-sr, -si]]).astype(np.float32)
    return project, np.stack([by_cos, by_sin])


def keep_table(size):
    v = prolate(KEPT, 0.25)
    return np.kron(np.eye(size), v).astype(ml_dtypes.bfloat16)


def row_table():
    u0 = np.arange(U0)[None, None, :]
    l0 = np.arange(L0)[:, None, None]
    l1 = np.arange(L1)[None, :, None]
    a = 2.0 * np.pi * ((u0 * (l0 + L0 * l1 - N // 4)) % N) / N
    c, s = np.cos(a).astype(ml_dtypes.bfloat16), np.sin(a).astype(ml_dtypes.bfloat16)
    table = np.concatenate(
        [np.concatenate([c, -s], axis=2), np.concatenate([s, c], axis=2)], axis=1
    )
    return table[0::2], table[1::2]


def project_kernel(
    count_ref, ku_ref, kv_ref, vis_ref, table_ref, keep_ref, mark_ref, out_ref, *, first
):
    slots = lax.broadcasted_iota(jnp.int32, (2, ku_ref.shape[1]), 1)
    owners, rows, width = out_ref.shape
    turn = lax.broadcasted_iota(jnp.int32, (1, S), 1) & 3
    cosine = jnp.where(turn == 0, 1.0, jnp.where(turn == 2, -1.0, 0.0))
    sine = jnp.where(turn == 1, 1.0, jnp.where(turn == 3, -1.0, 0.0))
    subs = []
    for b in range(ku_ref.shape[0]):
        live = count_ref[first + b]
        vis = jnp.where(slots < live, vis_ref[b].astype(jnp.float32), 0.0)
        kv_t = kv_ref[b].astype(jnp.float32).T
        weighted = jnp.concatenate([kv_t * vis[0:1, :], kv_t * vis[1:2, :]], axis=0)
        sub = jnp.dot(
            weighted.astype(jnp.bfloat16), ku_ref[b], preferred_element_type=jnp.float32
        )
        re, im = sub[:S], sub[S:]
        subs.append(
            jnp.concatenate(
                [re * cosine - im * sine, re * sine + im * cosine], axis=0
            ).astype(jnp.bfloat16)
        )
    table = table_ref[...]
    mark = jnp.concatenate([mark_ref[...], mark_ref[...]], axis=1)
    for lo in range(0, width, 256):
        hi = min(lo + 256, width)
        b0, b1 = lo // KEPT, -(-hi // KEPT)
        kept = jnp.dot(
            jnp.concatenate(subs[b0:b1], axis=1),
            keep_ref[b0 * S : b1 * S, lo:hi],
            preferred_element_type=jnp.float32,
        ).astype(jnp.bfloat16)
        out = jnp.dot(table, kept, preferred_element_type=jnp.float32)
        out = out.reshape(owners, rows, hi - lo)
        line = lax.broadcasted_iota(jnp.int32, (rows, hi - lo), 0)
        out = jnp.where((line == MARK)[None], mark[None, :, : hi - lo], out)
        out_ref[:, :, lo:hi] = out.astype(jnp.bfloat16)


def project_chunk(count, ku, kv, vis, table, keep, mark, owners, chunk, size):
    slots = ku.shape[1]
    return pl.pallas_call(
        functools.partial(project_kernel, first=chunk * size),
        out_shape=jax.ShapeDtypeStruct((owners, 2 * STACK, size * KEPT), jnp.bfloat16),
        grid_spec=pltpu.PrefetchScalarGridSpec(
            num_scalar_prefetch=1,
            grid=(1,),
            in_specs=[
                pl.BlockSpec((size, slots, S), lambda b, _: (chunk, 0, 0)),
                pl.BlockSpec((size, slots, S), lambda b, _: (chunk, 0, 0)),
                pl.BlockSpec((size, 2, slots), lambda b, _: (chunk, 0, 0)),
                pl.BlockSpec(table.shape, lambda b, _: (0, 0)),
                pl.BlockSpec(keep.shape, lambda b, _: (0, 0)),
                pl.BlockSpec(mark.shape, lambda b, _: (0, 0)),
            ],
            out_specs=pl.BlockSpec((owners, 2 * STACK, size * KEPT), lambda b, _: (0, 0, 0)),
        ),
        compiler_params=pltpu.CompilerParams(vmem_limit_bytes=60 * MIB),
        cost_estimate=pl.CostEstimate(
            flops=size * 2 * (256 * 256 * 128 + 512 * 256 * 128),
            bytes_accessed=size * 4 * 65536,
            transcendentals=0,
        ),
    )(count, ku, kv, vis, table, keep, mark)


def add_blocks(
    row_ref, got_ref, phase_ref, expand_ref, back_ref, coeff_ref, acc_ref, chunk, size, per_src
):
    sources, rows, width = got_ref.shape
    for g in range(size // 2):
        lo = 2 * KEPT * g // 128 * 128
        part = jnp.dot(
            got_ref[:, :, lo : lo + 256].reshape(sources * rows, 256),
            back_ref[lo : lo + 256, 256 * g : 256 * (g + 1)],
            preferred_element_type=jnp.float32,
        )
        coeff_ref[:, :, 256 * g : 256 * (g + 1)] = part.astype(jnp.bfloat16).reshape(
            sources, rows, 256
        )
    by_cos, by_sin = expand_ref[0], expand_ref[1]

    def per_source(src, carry):
        for b in range(size):
            g = src * per_src + chunk * size + b
            row = row_ref[g]
            ph = phase_ref[pl.ds(g, 1), :]
            c = jnp.concatenate([ph[:, :COLS], ph[:, :COLS]], axis=1)
            s = jnp.concatenate([ph[:, COLS:], ph[:, COLS:]], axis=1)
            weights = (by_cos * c + by_sin * s).astype(jnp.bfloat16)
            coeffs = coeff_ref[src, :, b * S : (b + 1) * S]
            block = lax.dot_general(
                coeffs, weights, (((0,), (0,)), ((), ())), preferred_element_type=jnp.float32
            )
            for q in range(4):
                acc_ref[q, pl.ds(row, S), :] += block[:, q * 128 : (q + 1) * 128]
        return carry

    lax.fori_loop(0, sources, per_source, 0, unroll=2)


def grid_kernel(
    row_ref, got_ref, phase_ref, expand_ref, back_ref, out_ref, coeff_ref, *, chunk, size, per_src
):
    out_ref[...] = jnp.zeros_like(out_ref)
    add_blocks(
        row_ref, got_ref, phase_ref, expand_ref, back_ref, coeff_ref, out_ref, chunk, size, per_src
    )


def coeff_scratch(got, size):
    return pltpu.VMEM((got.shape[0], got.shape[1], size * S), jnp.bfloat16)


def grid_chunk(rows, got, phase, expand, back, chunk, size, per_src):
    vmem = pl.BlockSpec(memory_space=pltpu.VMEM)
    return pl.pallas_call(
        functools.partial(grid_kernel, chunk=chunk, size=size, per_src=per_src),
        out_shape=jax.ShapeDtypeStruct((4, HALF, 128), jnp.float32),
        in_specs=[pl.BlockSpec(memory_space=pltpu.SMEM), vmem, vmem, vmem, vmem],
        out_specs=vmem,
        scratch_shapes=[coeff_scratch(got, size)],
        compiler_params=pltpu.CompilerParams(vmem_limit_bytes=56 * MIB),
        cost_estimate=pl.CostEstimate(
            flops=got.shape[0] * size * 2 * 128 * 256 * 512,
            bytes_accessed=12 * MIB,
            transcendentals=0,
        ),
    )(rows, got, phase, expand, back)


def dft8(x):
    def add(p, q):
        return (p[0] + q[0], p[1] + q[1])

    def sub(p, q):
        return (p[0] - q[0], p[1] - q[1])

    def turn(p):
        return (-p[1], p[0])

    def dft4(a, b, c, d):
        s, t, v, w = add(a, c), sub(a, c), add(b, d), turn(sub(b, d))
        return add(s, v), add(t, w), sub(s, v), sub(t, w)

    h = math.sqrt(0.5)
    e = dft4(x[0], x[2], x[4], x[6])
    o = list(dft4(x[1], x[3], x[5], x[7]))
    o[1] = ((o[1][0] - o[1][1]) * h, (o[1][0] + o[1][1]) * h)
    o[2] = turn(o[2])
    o[3] = ((-o[3][0] - o[3][1]) * h, (o[3][0] - o[3][1]) * h)
    return [add(e[k], o[k]) for k in range(4)] + [sub(e[k], o[k]) for k in range(4)]


def finish(place_ref, table_ref, mid_ref, screen_ref, full_ref, keep_ref, send_ref):
    def last_step(k, carry):
        planar = jnp.dot(table_ref[k], mid_ref[k], preferred_element_type=jnp.float32)
        value = planar[:L1] * screen_ref[k, 0] - planar[L1:] * screen_ref[k, 1]
        full_ref[:, k] = value.astype(jnp.bfloat16).reshape(L1 // 16, 16, COLS)
        return carry

    lax.fori_loop(0, L0 // 2, last_step, 0, unroll=4)
    for out_ref, which in ((keep_ref, 0), (send_ref, 1)):
        for i in range(out_ref.shape[0]):
            out_ref[i] = full_ref[place_ref[which, i]]


def even_kernel(
    row_ref, place_ref, got_ref, phase_ref, expand_ref, back_ref, old_hbm, table_hbm, screen_hbm,
    keep_ref, send_ref, odd_ref,
    coeff_ref, acc_ref, old_ref, table_ref, mid_ref, screen_ref, full_ref, sems,
    *, chunk, size, per_src,
):
    load_old = pltpu.make_async_copy(old_hbm, old_ref, sems.at[0])
    load_table = pltpu.make_async_copy(table_hbm, table_ref, sems.at[1])
    load_screen = pltpu.make_async_copy(screen_hbm, screen_ref, sems.at[2])
    load_old.start()
    load_table.start()
    load_screen.start()
    acc_ref[...] = jnp.zeros_like(acc_ref)
    add_blocks(
        row_ref, got_ref, phase_ref, expand_ref, back_ref, coeff_ref, acc_ref, chunk, size, per_src
    )
    load_old.wait()

    def first_step(i, carry):
        at = pl.multiple_of(i * 16, 16)
        for half in range(2):
            x = [
                tuple(
                    acc_ref[2 * p + half, pl.ds(at + U0 * k, 16), :]
                    + old_ref[2 * p + half, pl.ds(at + U0 * k, 16), :]
                    for p in range(2)
                )
                for k in range(U1)
            ]
            even = dft8(x)
            for k in range(1, U1):
                c, s = math.cos(math.pi * k / U1), math.sin(math.pi * k / U1)
                x[k] = (x[k][0] * c - x[k][1] * s, x[k][0] * s + x[k][1] * c)
            for ref, out in ((mid_ref, even), (odd_ref, dft8(x))):
                for k in range(L0 // 2):
                    for p in range(2):
                        ref[k, pl.ds(U0 * p + at, 16), half * 128 : (half + 1) * 128] = out[k][
                            p
                        ].astype(jnp.bfloat16)
        return carry

    lax.fori_loop(0, U0 // 16, first_step, 0)
    load_table.wait()
    load_screen.wait()
    finish(place_ref, table_ref, mid_ref, screen_ref, full_ref, keep_ref, send_ref)


def odd_kernel(
    place_ref, mid_ref, table_ref, screen_ref, keep_ref, send_ref, full_ref
):
    finish(place_ref, table_ref, mid_ref, screen_ref, full_ref, keep_ref, send_ref)


def make_image(
    rows, place, got, phase, expand, back, old, tables, screens, chunk, size, per_src
):
    vmem = pl.BlockSpec(memory_space=pltpu.VMEM)
    smem = pl.BlockSpec(memory_space=pltpu.SMEM)
    hbm = pl.BlockSpec(memory_space=pl.ANY)
    half = L0 // 2
    piece = jax.ShapeDtypeStruct((place.shape[1], half, 16, COLS), jnp.bfloat16)
    mid = (half, 2 * U0, COLS)
    buffers = [
        pltpu.VMEM(tables[0].shape, jnp.bfloat16),
        pltpu.VMEM(screens[0].shape, jnp.float32),
        pltpu.VMEM((16, half, 16, COLS), jnp.bfloat16),
    ]
    keep, send, odd = pl.pallas_call(
        functools.partial(even_kernel, chunk=chunk, size=size, per_src=per_src),
        out_shape=(piece, piece, jax.ShapeDtypeStruct(mid, jnp.bfloat16)),
        in_specs=[smem, smem, vmem, vmem, vmem, vmem, hbm, hbm, hbm],
        out_specs=(vmem, vmem, vmem),
        scratch_shapes=[
            coeff_scratch(got, size),
            pltpu.VMEM(old.shape, jnp.float32),
            pltpu.VMEM(old.shape, jnp.float32),
            buffers[0],
            pltpu.VMEM(mid, jnp.bfloat16),
            *buffers[1:],
            pltpu.SemaphoreType.DMA((3,)),
        ],
        compiler_params=pltpu.CompilerParams(vmem_limit_bytes=45 * MIB),
        cost_estimate=pl.CostEstimate(
            flops=16 * 1024**3, bytes_accessed=24 * MIB, transcendentals=0
        ),
    )(rows, place, got, phase, expand, back, old, tables[0], screens[0])
    keep_odd, send_odd = pl.pallas_call(
        odd_kernel,
        out_shape=(piece, piece),
        in_specs=[smem, vmem, vmem, vmem],
        out_specs=(vmem, vmem),
        scratch_shapes=[buffers[2]],
        compiler_params=pltpu.CompilerParams(vmem_limit_bytes=22 * MIB),
        cost_estimate=pl.CostEstimate(
            flops=4 * 1024**3, bytes_accessed=12 * MIB, transcendentals=0
        ),
    )(place, odd, tables[1], screens[1])
    return (keep, send), (keep_odd, send_odd)


def screen_kernel(base_ref, w_ref, even_ref, odd_ref, *, scale):
    cell = 2.0 * FIELD / N
    col = base_ref[0] + lax.broadcasted_iota(jnp.int32, (1, COLS), 1)
    dm = col.astype(jnp.float32) * cell
    h = math.pi / 2
    for half, out_ref in enumerate((even_ref, odd_ref)):
        l0 = 2 * pl.program_id(0) + half
        row = l0 + L0 * lax.broadcasted_iota(jnp.int32, (L1, 1), 0)
        dl = row.astype(jnp.float32) * cell
        lift = jnp.sqrt((1.0 - dl * dl) - dm * dm) - 1.0
        quarters = (4.0 * w_ref[0]) * lift
        whole = jnp.floor(quarters + 0.5)
        f = quarters - whole
        count = whole.astype(jnp.int32) - (row + col)
        t = f * f
        sine, cosine = 0.0, 0.0
        for n in (9, 7, 5, 3, 1):
            sine = sine * t + (-1) ** (n // 2) * h**n / math.factorial(n) * scale
        for n in (10, 8, 6, 4, 2, 0):
            cosine = cosine * t + (-1) ** (n // 2) * h**n / math.factorial(n) * scale
        sine = sine * f
        odd = (count & 1) == 1
        c = jnp.where(odd, sine, cosine)
        s = jnp.where(odd, cosine, sine)
        out_ref[0, 0] = jnp.where(((count + 1) & 2) == 2, -c, c)
        out_ref[0, 1] = jnp.where((count & 2) == 2, -s, s)


def make_screen(base, w, scale):
    smem = pl.BlockSpec(memory_space=pltpu.SMEM)
    half = jax.ShapeDtypeStruct((L0 // 2, 2, L1, COLS), jnp.float32)
    spec = pl.BlockSpec((1, 2, L1, COLS), lambda k: (k, 0, 0, 0))
    return pl.pallas_call(
        functools.partial(screen_kernel, scale=scale),
        out_shape=(half, half),
        grid=(L0 // 2,),
        in_specs=[smem, smem],
        out_specs=(spec, spec),
        compiler_params=pltpu.CompilerParams(vmem_limit_bytes=60 * MIB),
        cost_estimate=pl.CostEstimate(
            flops=40 * HALF * COLS, bytes_accessed=8 * MIB, transcendentals=HALF * COLS
        ),
    )(base, w)


def sum_planes(keep, send, planes):
    def shifted(values, target):
        pairs = [(i, target(i)) for i in range(planes)]
        return lax.ppermute(values, "wa", pairs).astype(jnp.float32)

    total = keep.astype(jnp.float32) + shifted(send, lambda i: i ^ 1)
    total = total.astype(jnp.bfloat16).reshape(4, 2, L0 // 2, 16, COLS)
    got = [
        shifted(total[step], lambda i, step=step: (i + 4 * step) % planes) for step in (1, 2, 3)
    ]
    total = (total[0].astype(jnp.float32) + got[0] + got[1] + got[2]).astype(jnp.bfloat16)
    return total[0].astype(jnp.float32) + shifted(total[1], lambda i: i ^ 2)


def body(kernel_u, kernel_v, visibilities, vis_count, tile_route, block_offset, plane_w):
    n_tu, n_tv, planes = lax.axis_size("tu"), lax.axis_size("tv"), lax.axis_size("wa")
    owners = n_tu * n_tv
    blocks, slots = kernel_u.shape[0], kernel_u.shape[1]
    size = blocks // CHUNKS
    project, expand = factor_tables(owners)
    tables = row_table()
    keep = keep_table(size)
    back = np.ascontiguousarray(keep.T)

    target = tile_route[:, 0]
    corner = jnp.stack(
        [target // n_tv * TILE + block_offset[:, 0], target % n_tv * TILE + block_offset[:, 1]],
        axis=0,
    )
    halves = jnp.stack([corner // 64, corner % 64], axis=1).reshape(1, 4 * blocks)
    mark = jnp.pad(halves, ((0, 0), (0, S - 4 * blocks))).astype(jnp.float32)
    owner = lax.axis_index(("tu", "tv"))
    col_base = owner * COLS
    scale = 1.0 / math.sqrt(slots * blocks * owners * 16)
    screens = make_screen(col_base.reshape(1), plane_w, scale)
    got = []
    for chunk in range(CHUNKS):
        coeffs = project_chunk(
            vis_count, kernel_u, kernel_v, visibilities, project, keep, mark, owners, chunk, size
        )
        if chunk:
            coeffs, screens = lax.optimization_barrier((coeffs, screens))
        got.append(
            lax.all_to_all(coeffs, ("tu", "tv"), split_axis=0, concat_axis=0, tiled=True)
        )
    marks = got[0][:, MARK, : 4 * blocks].astype(jnp.int32).reshape(owners, 2, 2, blocks)
    corners = marks[:, :, 0] * 64 + marks[:, :, 1]
    rows = corners[:, 0, :].reshape(-1)
    cols = corners[:, 1, :].reshape(-1)

    lane = jnp.arange(COLS, dtype=jnp.int32)
    turns = (cols[:, None] * (col_base + lane)[None, :] + N // 4 * rows[:, None]) % N
    shift = (S - 1) / 2 * (lane.astype(jnp.float32) - (COLS - 1) / 2)
    angle = (turns.astype(jnp.float32) + shift[None, :]) * (2.0 * math.pi / N)
    phase = jnp.concatenate([jnp.cos(angle), jnp.sin(angle)], axis=1)

    me = lax.axis_index("wa")
    core, z_hi, x = me % 2, me // 2 % 2, me // 4
    step = jnp.arange(8, dtype=jnp.int32)
    pair = ((x + step // 2) % 4) * 4 + (z_hi ^ (step % 2)) * 2
    place = jnp.stack([pair + core, pair + (1 - core)])

    acc = grid_chunk(rows, got[0], phase, expand, back, 0, size, blocks)
    halves = make_image(
        rows, place, got[1], phase, expand, back, acc, tables, screens, 1, size, blocks
    )
    if planes != 16:
        return halves
    even, odd = (sum_planes(keep, send, planes) for keep, send in halves)
    return jnp.stack([even, odd], axis=1).transpose(2, 0, 1, 3).reshape(L0 * 16, COLS)


def solution(mesh):
    split = ("wa", "tu", "tv")
    placed = (
        P(split, None, None),
        P(split, None, None),
        P(split, None, None),
        P(split),
        P(split, None),
        P(split, None),
        P("wa"),
    )
    return jax.shard_map(
        body, mesh=mesh, in_specs=placed, out_specs=P("wa", ("tu", "tv")), check_vma=False
    )
```

time: 129 us -> 106 us (0.82)
  waiting for transfers between devices: 30.3 us -> 16.6 us
  Pallas kernels: 60.3 us -> 48 us
  local copies, waits for them, and re-layouts: 2.1 us -> 5.61 us
    all_to_all x2, waiting for transfers between devices: 23.3 us -> 9.6 us  [body(): lax.all_to_all(coeffs, ('tu', 'tv'), split_axis=0, concat_axis=0, tiled=T...]
    pallas_call x1, Pallas kernels: 8.47 us -> 3.14 us  [make_image(): pl.pallas_call(odd_kernel, out_shape=(piece, piece), in_specs=[smem, vmem...]
    unnamed x10 -> x16, local copies, waits for them, and re-layouts: 0.02 us -> 4.08 us
    pallas_call x1, Pallas kernels: 18.8 us -> 14.8 us  [make_image(): pl.pallas_call(functools.partial(even_kernel, chunk=chunk, size=size, per...]
    pallas_call x1, Pallas kernels: 11.4 us -> 9.02 us  [make_screen(): pl.pallas_call(functools.partial(screen_kernel, scale=scale), out_shape=(...]
  transfers between devices with their start and end apart: 12 -> 12, of which waited for: 4 -> 4; matrix products, arithmetic and copies ran while one was open for 3% -> 3% of each run, Pallas kernels for 29% -> 27%
where the time goes in v3:
time: 106 us; the launch traced here: 105 us
  Pallas kernels  48 us (45%)
  starting transfers between devices  30.2 us (28%)
  waiting for transfers between devices  16.6 us (16%)
  local copies, waits for them, and re-layouts  5.61 us (5%)
  other arithmetic  3.89 us (4%)
    ppermute x10, starting transfers between devices, shifted(): return lax.ppermute(values, 'wa', pairs).astype(jnp.float32)  18 us
    pallas_call x1, Pallas kernels, make_image(): pl.pallas_call(functools.partial(even_kernel, chunk=chunk, size=size, per...  14.8 us
    all_to_all x2, starting transfers between devices, body(): lax.all_to_all(coeffs, ('tu', 'tv'), split_axis=0, concat_axis=0, tiled=T...  12.2 us
    pallas_call x1, Pallas kernels, grid_chunk(): pl.pallas_call(functools.partial(grid_kernel, chunk=chunk, size=size, per...  12.1 us
    all_to_all x2, waiting for transfers between devices, body(): lax.all_to_all(coeffs, ('tu', 'tv'), split_axis=0, concat_axis=0, tiled=T...  9.6 us
    pallas_call x1, Pallas kernels, make_screen(): pl.pallas_call(functools.partial(screen_kernel, scale=scale), out_shape=(...  9.02 us
    pallas_call x2, Pallas kernels, project_chunk(): pl.pallas_call(functools.partial(project_kernel, first=chunk * size), out...  8.92 us
    ppermute x10, waiting for transfers between devices, shifted(): return lax.ppermute(values, 'wa', pairs).astype(jnp.float32)  6.97 us
  transfers between devices with their start and end apart: 12, of which 4 were waited for; matrix products, arithmetic and copies ran while one was open for 3% of the time, Pallas kernels for 27%

profile of v3, /device:TPU:2, one launch (start us, length us, event | category | flops | bytes accessed | tf_op | source)
XLA Modules:
  0.0 105.2 jit_solution(9115474243023555060)
XLA Ops:
  0.0 0.8 fusion.17
  1.4 4.5 %shard_map.127 = bf16[16,32,640]{2,1,0:T(8,128)(2,1)} custom-call(s32[16]{0:T(128)} %count_ref.3, bf16[16,256,128]{2,1,0:T(8,128)(2,1)} %ku_ref.3, bf16[16,256,128]{2,1,0:T(8,128)(2,1)} %kv_ref.3, bf16[16,2,256]{2,1,0:T(2,128)(2,1)} %vis_ref.3, bf16[512,256]{1,0:T(8,128)(2,1)} %constant.167.clone.table_ref, bf16[1024,640]{1,0:T(8,128)(2,1)} %constant.168.clone.keep_ref, ...), custom_call_target="tpu_custom_call" | custom-call | flops 402653184 | bytes 2097152 | tf_op jit(solution)/shard_map/pallas_call | solution.py:121
  5.9 8.6 %all-to-all-start = ((bf16[16,32,640]{2,1,0:T(8,128)(2,1)}), bf16[16,32,640]{2,1,0:T(8,128)(2,1)S(1)}, u32[]{:S(2)}, u32[]{:S(2)}) async-start(bf16[16,32,640]{2,1,0:T(8,128)(2,1)} %shard_map.127), calls=%async_computation | async-start | bytes 1310720 | tf_op jit(solution)/shard_map/all_to_all | solution.py:435
  15.2 9.0 %shard_map.129 = (f32[8,2,256,256]{3,2,1,0:T(8,128)}, f32[8,2,256,256]{3,2,1,0:T(8,128)}) custom-call(s32[1]{0:T(128)} %bitcast.6.base_ref, f32[1]{0:T(128)S(6)} %copy.15.w_ref), custom_call_target="tpu_custom_call" | custom-call | flops 41943040 | bytes 8388608 | tf_op jit(solution)/shard_map/pallas_call | solution.py:379
  24.2 4.5 %shard_map.128 = bf16[16,32,640]{2,1,0:T(8,128)(2,1)} custom-call(s32[16]{0:T(128)} %count_ref.3, bf16[16,256,128]{2,1,0:T(8,128)(2,1)} %ku_ref.3, bf16[16,256,128]{2,1,0:T(8,128)(2,1)} %kv_ref.3, bf16[16,2,256]{2,1,0:T(2,128)(2,1)} %vis_ref.3, bf16[512,256]{1,0:T(8,128)(2,1)} %constant.167.clone.table_ref, bf16[1024,640]{1,0:T(8,128)(2,1)} %constant.168.clone.keep_ref, ...), custom_call_target="tpu_custom_call" | custom-call | flops 402653184 | bytes 2097152 | tf_op jit(solution)/shard_map/pallas_call | solution.py:121
  28.7 5.1 %all-to-all-done.got_ref = bf16[16,32,640]{2,1,0:T(8,128)(2,1)S(1)} async-done(((bf16[16,32,640]{2,1,0:T(8,128)(2,1)}), bf16[16,32,640]{2,1,0:T(8,128)(2,1)S(1)}, u32[]{:S(2)}, u32[]{:S(2)}) %all-to-all-start) | async-done | bytes 655392 | tf_op jit(solution)/shard_map/all_to_all | solution.py:435
  33.8 3.6 %all-to-all-start.1 = ((bf16[16,32,640]{2,1,0:T(8,128)(2,1)}), bf16[16,32,640]{2,1,0:T(8,128)(2,1)S(1)}, u32[]{:S(2)}, u32[]{:S(2)}) async-start(bf16[16,32,640]{2,1,0:T(8,128)(2,1)} %shard_map.128), calls=%async_computation.1 | async-start | bytes 1310720 | tf_op jit(solution)/shard_map/all_to_all | solution.py:435
  37.8 1.1 %fusion.5 = (f32[256,256]{1,0:T(8,128)S(1)}, f32[256,256]{1,0:T(8,128)S(1)}) fusion(f32[256]{0:T(256)S(1)} %add_multiply_fusion, s32[256]{0:T(256)S(1)} %get-tuple-element.42, s32[256]{0:T(256)S(1)} %get-tuple-element.41, s32[256]{0:T(256)S(1)} %mul.147), kind=kLoop, calls=%fused_computation.14 | loop fusion | flops 1048576 | bytes 528384 | tf_op jit(solution)/shard_map/cos | solution.py:446
  39.0 0.9 pad_maximum_fusion.phase_ref
  39.9 12.1 %shard_map.130.old_hbm = f32[4,4096,128]{2,1,0:T(8,128)} custom-call(s32[256]{0:T(256)} %copy-done.3, bf16[16,32,640]{2,1,0:T(8,128)(2,1)} %copy-done.7, f32[256,512]{1,0:T(8,128)} %pad_maximum_fusion.phase_ref, f32[2,32,512]{2,1,0:T(8,128)} %constant.169.clone.expand_ref, bf16[640,1024]{1,0:T(8,128)(2,1)} %constant.170.clone.back_ref), custom_call_target="tpu_custom_call" | custom-call | flops 4294967296 | bytes 12582912 | tf_op jit(solution)/shard_map/pallas_call | solution.py:196
  52.0 4.5 %all-to-all-done.1.got_ref = bf16[16,32,640]{2,1,0:T(8,128)(2,1)S(1)} async-done(((bf16[16,32,640]{2,1,0:T(8,128)(2,1)}), bf16[16,32,640]{2,1,0:T(8,128)(2,1)S(1)}, u32[]{:S(2)}, u32[]{:S(2)}) %all-to-all-start.1) | async-done | bytes 655392 | tf_op jit(solution)/shard_map/all_to_all | solution.py:435
  57.2 14.8 %shard_map.131 = (bf16[8,8,16,256]{3,2,1,0:T(8,128)(2,1)S(1)}, bf16[8,8,16,256]{3,2,1,0:T(8,128)(2,1)S(1)}, bf16[8,1024,256]{2,1,0:T(8,128)(2,1)S(1)}) custom-call(s32[256]{0:T(256)S(1)} %copy-done.4, s32[2,8]{1,0:T(2,128)S(1)} %pad_add_fusion.2.place_ref, bf16[16,32,640]{2,1,0:T(8,128)(2,1)S(1)} %all-to-all-done.1.got_ref, f32[256,512]{1,0:T(8,128)S(1)} %copy-done.2, ...), custom_call_target="tpu_custom_call" | custom-call | flops 17179869184 | bytes 25165824 | tf_op jit(solution)/shard_map/pallas_call | solution.py:314
  72.1 3.4 %copy-done = bf16[8,512,1024]{2,1,0:T(8,128)(2,1)S(1)} copy-done((bf16[8,512,1024]{2,1,0:T(8,128)(2,1)S(1)}, bf16[8,512,1024]{2,1,0:T(8,128)(2,1)}, u32[]{:S(2)}) %copy-start) | copy-done | bytes 8388632
  75.5 3.1 %shard_map.132 = (bf16[8,8,16,256]{3,2,1,0:T(8,128)(2,1)S(1)}, bf16[8,8,16,256]{3,2,1,0:T(8,128)(2,1)S(1)}) custom-call(s32[2,8]{1,0:T(2,128)S(1)} %pad_add_fusion.2.place_ref, bf16[8,1024,256]{2,1,0:T(8,128)(2,1)S(1)} %get-tuple-element.21.mid_ref, bf16[8,512,1024]{2,1,0:T(8,128)(2,1)S(1)} %copy-done, f32[8,2,256,256]{3,2,1,0:T(8,128)S(1)} %copy-done.1), custom_call_target="tpu_custom_call" | custom-call | flops 4294967296 | bytes 12582912 | tf_op jit(solution)/shard_map/pallas_call | solution.py:333
  79.6 1.6 %collective-permute-start.1 = (bf16[2,8,16,256]{3,2,1,0:T(8,128)(2,1)S(1)}, bf16[2,8,16,256]{3,2,1,0:T(8,128)(2,1)S(1)}, u32[]{:S(2)}, u32[]{:S(2)}) collective-permute-start(bf16[2,8,16,256]{3,2,1,0:T(8,128)(2,1)S(1)} %get-tuple-element.29), channel_id=1, source_target_pairs={{0,64},{16,80},{32,96},{48,112},{64,128},{80,144},{96,160},{112,17... | collective-permute-start | bytes 393224 | tf_op jit(solution)/shard_map/ppermute | solution.py:395
  81.7 2.2 %collective-permute-start.2 = (bf16[2,8,16,256]{3,2,1,0:T(8,128)(2,1)S(1)}, bf16[2,8,16,256]{3,2,1,0:T(8,128)(2,1)S(1)}, u32[]{:S(2)}, u32[]{:S(2)}) collective-permute-start(bf16[2,8,16,256]{3,2,1,0:T(8,128)(2,1)S(1)} %get-tuple-element.31), channel_id=1, source_target_pairs={{0,128},{16,144},{32,160},{48,176},{64,192},{80,208},{96,224},{112... | collective-permute-start | bytes 393224 | tf_op jit(solution)/shard_map/ppermute | solution.py:395
  84.0 1.2 %collective-permute-start.6 = (bf16[2,8,16,256]{3,2,1,0:T(8,128)(2,1)S(1)}, bf16[2,8,16,256]{3,2,1,0:T(8,128)(2,1)S(1)}, u32[]{:S(2)}, u32[]{:S(2)}) collective-permute-start(bf16[2,8,16,256]{3,2,1,0:T(8,128)(2,1)S(1)} %get-tuple-element.32), channel_id=1, source_target_pairs={{0,64},{16,80},{32,96},{48,112},{64,128},{80,144},{96,160},{112,17... | collective-permute-start | bytes 393224 | tf_op jit(solution)/shard_map/ppermute | solution.py:395
  85.2 0.9 collective-permute-start.8
  86.1 1.9 %collective-permute-start.7 = (bf16[2,8,16,256]{3,2,1,0:T(8,128)(2,1)S(1)}, bf16[2,8,16,256]{3,2,1,0:T(8,128)(2,1)S(1)}, u32[]{:S(2)}, u32[]{:S(2)}) collective-permute-start(bf16[2,8,16,256]{3,2,1,0:T(8,128)(2,1)S(1)} %get-tuple-element.34), channel_id=1, source_target_pairs={{0,128},{16,144},{32,160},{48,176},{64,192},{80,208},{96,224},{112... | collective-permute-start | bytes 393224 | tf_op jit(solution)/shard_map/ppermute | solution.py:395
  88.1 3.0 %collective-permute-done.2 = bf16[2,8,16,256]{3,2,1,0:T(8,128)(2,1)S(1)} collective-permute-done((bf16[2,8,16,256]{3,2,1,0:T(8,128)(2,1)S(1)}, bf16[2,8,16,256]{3,2,1,0:T(8,128)(2,1)S(1)}, u32[]{:S(2)}, u32[]{:S(2)}) %collective-permute-start.2) | collective-permute-done | bytes 131104 | tf_op jit(solution)/shard_map/ppermute | solution.py:395
  91.1 4.6 %collective-permute-start.4 = (bf16[8,16,256]{2,1,0:T(8,128)(2,1)S(1)}, bf16[8,16,256]{2,1,0:T(8,128)(2,1)S(1)}, u32[]{:S(2)}, u32[]{:S(2)}) collective-permute-start(bf16[8,16,256]{2,1,0:T(8,128)(2,1)S(1)} %slice_bitcast_fusion.2), channel_id=1, source_target_pairs={{0,32},{16,48},{32,0},{48,16},{64,96},{80,112},{96,64},{112,80},{1... | collective-permute-start | bytes 196616 | tf_op jit(solution)/shard_map/ppermute | solution.py:395
  95.8 4.3 %collective-permute-start.9 = (bf16[8,16,256]{2,1,0:T(8,128)(2,1)S(1)}, bf16[8,16,256]{2,1,0:T(8,128)(2,1)S(1)}, u32[]{:S(2)}, u32[]{:S(2)}) collective-permute-start(bf16[8,16,256]{2,1,0:T(8,128)(2,1)S(1)} %slice_bitcast_fusion), channel_id=1, source_target_pairs={{0,32},{16,48},{32,0},{48,16},{64,96},{80,112},{96,64},{112,80},{1... | collective-permute-start | bytes 196616 | tf_op jit(solution)/shard_map/ppermute | solution.py:395
  100.1 4.0 %collective-permute-done.9 = bf16[8,16,256]{2,1,0:T(8,128)(2,1)S(1)} collective-permute-done((bf16[8,16,256]{2,1,0:T(8,128)(2,1)S(1)}, bf16[8,16,256]{2,1,0:T(8,128)(2,1)S(1)}, u32[]{:S(2)}, u32[]{:S(2)}) %collective-permute-start.9) | collective-permute-done | bytes 65568 | tf_op jit(solution)/shard_map/ppermute | solution.py:395
  104.3 0.9 reshape.592
  (53 shorter events, 3.9 us)
Async XLA Ops:
  5.9 28.0 %all-to-all-start = ((bf16[16,32,640]{2,1,0:T(8,128)(2,1)}), bf16[16,32,640]{2,1,0:T(8,128)(2,1)S(1)}, u32[]{:S(2)}, u32[]{:S(2)}) async-start(bf16[16,32,640]{2,1,0:T(8,128)(2,1)} %shard_map.127), calls=%async_computation | async-start | bytes 1310720 | tf_op jit(solution)/shard_map/all_to_all | solution.py:435
  33.8 6.0 %copy-start.7 = (bf16[16,32,640]{2,1,0:T(8,128)(2,1)}, bf16[16,32,640]{2,1,0:T(8,128)(2,1)S(1)}, u32[]{:S(2)}) copy-start(bf16[16,32,640]{2,1,0:T(8,128)(2,1)S(1)} %all-to-all-done.got_ref) | copy-start | bytes 1966084
  33.8 22.6 %all-to-all-start.1 = ((bf16[16,32,640]{2,1,0:T(8,128)(2,1)}), bf16[16,32,640]{2,1,0:T(8,128)(2,1)S(1)}, u32[]{:S(2)}, u32[]{:S(2)}) async-start(bf16[16,32,640]{2,1,0:T(8,128)(2,1)} %shard_map.128), calls=%async_computation.1 | async-start | bytes 1310720 | tf_op jit(solution)/shard_map/all_to_all | solution.py:435
  37.8 2.0 %copy-start.3 = (s32[256]{0:T(256)}, s32[256]{0:T(256)S(1)}, u32[]{:S(2)}) copy-start(s32[256]{0:T(256)S(1)} %reshape_squeeze.3.row_ref) | copy-start | bytes 3076
  39.8 16.6 %copy-start.2 = (f32[256,512]{1,0:T(8,128)S(1)}, f32[256,512]{1,0:T(8,128)}, u32[]{:S(2)}) copy-start(f32[256,512]{1,0:T(8,128)} %pad_maximum_fusion.phase_ref) | copy-start | bytes 1572868
  39.8 16.6 %copy-start.5 = (bf16[640,1024]{1,0:T(8,128)(2,1)S(1)}, bf16[640,1024]{1,0:T(8,128)(2,1)}, u32[]{:S(2)}) copy-start(bf16[640,1024]{1,0:T(8,128)(2,1)} %constant.170.clone.back_ref) | copy-start | bytes 3932164
  39.8 16.6 %copy-start.6 = (f32[2,32,512]{2,1,0:T(8,128)S(1)}, f32[2,32,512]{2,1,0:T(8,128)}, u32[]{:S(2)}) copy-start(f32[2,32,512]{2,1,0:T(8,128)} %constant.169.clone.expand_ref) | copy-start | bytes 393220
  56.5 0.7 copy-start.4
  57.1 14.9 %copy-start.1 = (f32[8,2,256,256]{3,2,1,0:T(8,128)S(1)}, f32[8,2,256,256]{3,2,1,0:T(8,128)}, u32[]{:S(2)}) copy-start(f32[8,2,256,256]{3,2,1,0:T(8,128)} %get-tuple-element.22.screen_ref) | copy-start | bytes 12582916
  72.0 7.4 %collective-permute-start = (bf16[8,8,16,256]{3,2,1,0:T(8,128)(2,1)S(1)}, bf16[8,8,16,256]{3,2,1,0:T(8,128)(2,1)S(1)}, u32[]{:S(2)}, u32[]{:S(2)}) collective-permute-start(bf16[8,8,16,256]{3,2,1,0:T(8,128)(2,1)S(1)} %get-tuple-element.20), channel_id=1, source_target_pairs={{0,16},{16,0},{32,48},{48,32},{64,80},{80,64},{96,112},{112,96},{1... | collective-permute-start | bytes 1572872 | tf_op jit(solution)/shard_map/ppermute | solution.py:395
  72.1 3.4 %copy-start = (bf16[8,512,1024]{2,1,0:T(8,128)(2,1)S(1)}, bf16[8,512,1024]{2,1,0:T(8,128)(2,1)}, u32[]{:S(2)}) copy-start(bf16[8,512,1024]{2,1,0:T(8,128)(2,1)} %constant.172.clone.table_ref) | copy-start | bytes 25165828
  78.6 5.2 %collective-permute-start.5 = (bf16[8,8,16,256]{3,2,1,0:T(8,128)(2,1)S(1)}, bf16[8,8,16,256]{3,2,1,0:T(8,128)(2,1)S(1)}, u32[]{:S(2)}, u32[]{:S(2)}) collective-permute-start(bf16[8,8,16,256]{3,2,1,0:T(8,128)(2,1)S(1)} %get-tuple-element.24), channel_id=1, source_target_pairs={{0,16},{16,0},{32,48},{48,32},{64,80},{80,64},{96,112},{112,96},{1... | collective-permute-start | bytes 1572872 | tf_op jit(solution)/shard_map/ppermute | solution.py:395
  79.6 6.6 %collective-permute-start.1 = (bf16[2,8,16,256]{3,2,1,0:T(8,128)(2,1)S(1)}, bf16[2,8,16,256]{3,2,1,0:T(8,128)(2,1)S(1)}, u32[]{:S(2)}, u32[]{:S(2)}) collective-permute-start(bf16[2,8,16,256]{3,2,1,0:T(8,128)(2,1)S(1)} %get-tuple-element.29), channel_id=1, source_target_pairs={{0,64},{16,80},{32,96},{48,112},{64,128},{80,144},{96,160},{112,17... | collective-permute-start | bytes 393224 | tf_op jit(solution)/shard_map/ppermute | solution.py:395
  81.2 6.9 %collective-permute-start.3 = (bf16[2,8,16,256]{3,2,1,0:T(8,128)(2,1)S(1)}, bf16[2,8,16,256]{3,2,1,0:T(8,128)(2,1)S(1)}, u32[]{:S(2)}, u32[]{:S(2)}) collective-permute-start(bf16[2,8,16,256]{3,2,1,0:T(8,128)(2,1)S(1)} %get-tuple-element.30), channel_id=1, source_target_pairs={{0,192},{16,208},{32,224},{48,240},{64,0},{80,16},{96,32},{112,48}... | collective-permute-start | bytes 393224 | tf_op jit(solution)/shard_map/ppermute | solution.py:395
  81.7 9.3 %collective-permute-start.2 = (bf16[2,8,16,256]{3,2,1,0:T(8,128)(2,1)S(1)}, bf16[2,8,16,256]{3,2,1,0:T(8,128)(2,1)S(1)}, u32[]{:S(2)}, u32[]{:S(2)}) collective-permute-start(bf16[2,8,16,256]{3,2,1,0:T(8,128)(2,1)S(1)} %get-tuple-element.31), channel_id=1, source_target_pairs={{0,128},{16,144},{32,160},{48,176},{64,192},{80,208},{96,224},{112... | collective-permute-start | bytes 393224 | tf_op jit(solution)/shard_map/ppermute | solution.py:395
  84.0 11.7 %collective-permute-start.6 = (bf16[2,8,16,256]{3,2,1,0:T(8,128)(2,1)S(1)}, bf16[2,8,16,256]{3,2,1,0:T(8,128)(2,1)S(1)}, u32[]{:S(2)}, u32[]{:S(2)}) collective-permute-start(bf16[2,8,16,256]{3,2,1,0:T(8,128)(2,1)S(1)} %get-tuple-element.32), channel_id=1, source_target_pairs={{0,64},{16,80},{32,96},{48,112},{64,128},{80,144},{96,160},{112,17... | collective-permute-start | bytes 393224 | tf_op jit(solution)/shard_map/ppermute | solution.py:395
  85.2 10.5 %collective-permute-start.8 = (bf16[2,8,16,256]{3,2,1,0:T(8,128)(2,1)S(1)}, bf16[2,8,16,256]{3,2,1,0:T(8,128)(2,1)S(1)}, u32[]{:S(2)}, u32[]{:S(2)}) collective-permute-start(bf16[2,8,16,256]{3,2,1,0:T(8,128)(2,1)S(1)} %get-tuple-element.33), channel_id=1, source_target_pairs={{0,192},{16,208},{32,224},{48,240},{64,0},{80,16},{96,32},{112,48}... | collective-permute-start | bytes 393224 | tf_op jit(solution)/shard_map/ppermute | solution.py:395
  86.1 9.6 %collective-permute-start.7 = (bf16[2,8,16,256]{3,2,1,0:T(8,128)(2,1)S(1)}, bf16[2,8,16,256]{3,2,1,0:T(8,128)(2,1)S(1)}, u32[]{:S(2)}, u32[]{:S(2)}) collective-permute-start(bf16[2,8,16,256]{3,2,1,0:T(8,128)(2,1)S(1)} %get-tuple-element.34), channel_id=1, source_target_pairs={{0,128},{16,144},{32,160},{48,176},{64,192},{80,208},{96,224},{112... | collective-permute-start | bytes 393224 | tf_op jit(solution)/shard_map/ppermute | solution.py:395
  91.1 8.9 %collective-permute-start.4 = (bf16[8,16,256]{2,1,0:T(8,128)(2,1)S(1)}, bf16[8,16,256]{2,1,0:T(8,128)(2,1)S(1)}, u32[]{:S(2)}, u32[]{:S(2)}) collective-permute-start(bf16[8,16,256]{2,1,0:T(8,128)(2,1)S(1)} %slice_bitcast_fusion.2), channel_id=1, source_target_pairs={{0,32},{16,48},{32,0},{48,16},{64,96},{80,112},{96,64},{112,80},{1... | collective-permute-start | bytes 196616 | tf_op jit(solution)/shard_map/ppermute | solution.py:395
  95.8 8.3 %collective-permute-start.9 = (bf16[8,16,256]{2,1,0:T(8,128)(2,1)S(1)}, bf16[8,16,256]{2,1,0:T(8,128)(2,1)S(1)}, u32[]{:S(2)}, u32[]{:S(2)}) collective-permute-start(bf16[8,16,256]{2,1,0:T(8,128)(2,1)S(1)} %slice_bitcast_fusion), channel_id=1, source_target_pairs={{0,32},{16,48},{32,0},{48,16},{64,96},{80,112},{96,64},{112,80},{1... | collective-permute-start | bytes 196616 | tf_op jit(solution)/shard_map/ppermute | solution.py:395

commit v4 on v3

--- a/solution.py
+++ b/solution.py
@@ -13,9 +13,11 @@
 N = 8192
 HALF = 4096
 S = 128
-RANK = 15
-STACK = 16
-MARK = 15
+RANK = 14
+ROWS = 2 * RANK
+STACK = 32
+PACKED = 144
+MARK = 140
 KEPT = 80
 COLS = 256
 U0 = 512
@@ -26,6 +28,8 @@
 CHUNKS = 2
 FIELD = 0.25
 MIB = 1 << 20
+EVEN_MIB = 45
+ODD_MIB = 22
 
 
 def prolate(count, half_band):
@@ -43,28 +47,42 @@
     mu = np.arange(COLS) - (COLS - 1) / 2
     basis = prolate(RANK, COLS / 2 / N)
     spread = basis.T @ np.exp(2j * np.pi * np.outer(t, mu) / N)
-    pad = ((0, STACK - RANK), (0, 0))
-    basis, spread = np.pad(basis.T, pad), np.pad(spread, pad)
-    rows = []
-    for j in range(owners):
-        centre = COLS * j + (COLS - 1) / 2
-        turn = np.exp(2j * np.pi * np.arange(S) * centre / N)
-        proj = basis * turn[None, :]
-        rows.append(np.concatenate([proj.real, -proj.imag], axis=1))
-        rows.append(np.concatenate([proj.imag, proj.real], axis=1))
-    project = np.concatenate(rows, axis=0).astype(ml_dtypes.bfloat16)
+    project = []
+    for pad in ((0, STACK - ROWS), (STACK - ROWS, 0)):
+        rows = []
+        for j in range(owners):
+            centre = COLS * j + (COLS - 1) / 2
+            turn = np.exp(2j * np.pi * np.arange(S) * centre / N)
+            proj = basis.T * turn[None, :]
+            rows.append(np.pad(np.block([[proj.real, -proj.imag], [proj.imag, proj.real]]), (pad, (0, 0))))
+        project.append(np.concatenate(rows, axis=0))
     sr, si = spread.real, spread.imag
-    by_cos = np.block([[sr, si], [-si, sr]]).astype(np.float32)
-    by_sin = np.block([[-si, sr], [-sr, -si]]).astype(np.float32)
-    return project, np.stack([by_cos, by_sin])
-
-
-def keep_table(size):
-    v = prolate(KEPT, 0.25)
-    return np.kron(np.eye(size), v).astype(ml_dtypes.bfloat16)
-
-
-def row_table():
+    pad = ((0, STACK - ROWS), (0, 0))
+    by_cos = np.pad(np.block([[sr, si], [-si, sr]]), pad).astype(np.float32)
+    by_sin = np.pad(np.block([[-si, sr], [-sr, -si]]), pad).astype(np.float32)
+    return np.stack(project).astype(ml_dtypes.bfloat16), np.stack([by_cos, by_sin])
+
+
+def keep_spans(size):
+    width = size * KEPT
+    runs = [(lo, min(lo + 256, width)) for lo in range(0, width, 256)]
+    return [(lo, hi, lo // KEPT, -(-hi // KEPT)) for lo, hi in runs]
+
+
+def keep_tables(size):
+    whole = np.kron(np.eye(size), prolate(KEPT, 0.25)).astype(ml_dtypes.bfloat16)
+    to = [
+        np.pad(whole[b0 * S : b1 * S, lo:hi], ((0, 0), (0, 256 - (hi - lo))))
+        for lo, hi, b0, b1 in keep_spans(size)
+    ]
+    back = []
+    for g in range(size // 2):
+        lo = 2 * KEPT * g // 128 * 128
+        back.append(whole[2 * S * g : 2 * S * (g + 1), lo : lo + 256].T)
+    return np.concatenate(to, axis=0), np.stack(back)
+
+
+def row_tables():
     u0 = np.arange(U0)[None, None, :]
     l0 = np.arange(L0)[:, None, None]
     l1 = np.arange(L1)[None, :, None]
@@ -76,11 +94,27 @@
     return table[0::2], table[1::2]
 
 
+def corner_marks(route_ref, offset_ref, n_tv):
+    lane = lax.broadcasted_iota(jnp.int32, (1, S), 1)
+    marks = jnp.zeros((1, S), jnp.int32)
+    blocks = route_ref.shape[1]
+    for b in range(blocks):
+        tile = route_ref[0, b]
+        place = (tile // n_tv, tile % n_tv)
+        for axis in range(2):
+            corner = place[axis] * TILE + offset_ref[axis, b]
+            at = 2 * blocks * axis + b
+            marks = jnp.where(lane == at, corner // 64, marks)
+            marks = jnp.where(lane == at + blocks, corner % 64, marks)
+    return marks.astype(jnp.float32)
+
+
 def project_kernel(
-    count_ref, ku_ref, kv_ref, vis_ref, table_ref, keep_ref, mark_ref, out_ref, *, first
+    count_ref, route_ref, offset_ref, ku_ref, kv_ref, vis_ref, table_ref, keep_ref, out_ref,
+    *, first, n_tv,
 ):
     slots = lax.broadcasted_iota(jnp.int32, (2, ku_ref.shape[1]), 1)
-    owners, rows, width = out_ref.shape
+    owners, rows, _ = out_ref.shape
     turn = lax.broadcasted_iota(jnp.int32, (1, S), 1) & 3
     cosine = jnp.where(turn == 0, 1.0, jnp.where(turn == 2, -1.0, 0.0))
     sine = jnp.where(turn == 1, 1.0, jnp.where(turn == 3, -1.0, 0.0))
@@ -99,40 +133,60 @@
                 [re * cosine - im * sine, re * sine + im * cosine], axis=0
             ).astype(jnp.bfloat16)
         )
-    table = table_ref[...]
-    mark = jnp.concatenate([mark_ref[...], mark_ref[...]], axis=1)
-    for lo in range(0, width, 256):
-        hi = min(lo + 256, width)
-        b0, b1 = lo // KEPT, -(-hi // KEPT)
+    start, runs = 0, []
+    for lo, hi, b0, b1 in keep_spans(ku_ref.shape[0]):
+        depth = (b1 - b0) * S
         kept = jnp.dot(
             jnp.concatenate(subs[b0:b1], axis=1),
-            keep_ref[b0 * S : b1 * S, lo:hi],
+            keep_ref[start : start + depth, : hi - lo],
             preferred_element_type=jnp.float32,
         ).astype(jnp.bfloat16)
-        out = jnp.dot(table, kept, preferred_element_type=jnp.float32)
-        out = out.reshape(owners, rows, hi - lo)
-        line = lax.broadcasted_iota(jnp.int32, (rows, hi - lo), 0)
-        out = jnp.where((line == MARK)[None], mark[None, :, : hi - lo], out)
-        out_ref[:, :, lo:hi] = out.astype(jnp.bfloat16)
-
-
-def project_chunk(count, ku, kv, vis, table, keep, mark, owners, chunk, size):
+        start += depth
+        runs += [kept[:, i : i + 128] for i in range(0, hi - lo, 128)]
+
+    tiles = [None] * len(runs)
+    for which in range(2):
+        mine = list(range(which, len(runs), 2))
+        for i in range(0, len(mine), 2):
+            pair = mine[i : i + 2]
+            out = jnp.dot(
+                table_ref[which],
+                jnp.concatenate([runs[t] for t in pair], axis=1),
+                preferred_element_type=jnp.float32,
+            ).reshape(owners, STACK, 128 * len(pair))
+            for n, t in enumerate(pair):
+                tiles[t] = out[:, :, 128 * n : 128 * (n + 1)]
+    whole, part = ROWS // 8 * 8, STACK - ROWS
+    pieces = []
+    for t in range(0, len(tiles), 2):
+        pieces.append(tiles[t][:, :whole])
+        if t + 1 < len(tiles):
+            pieces += [tiles[t][:, whole:] + tiles[t + 1][:, :8], tiles[t + 1][:, 8:]]
+        else:
+            line = lax.broadcasted_iota(jnp.int32, (8, S), 0)
+            marks = corner_marks(route_ref, offset_ref, n_tv) if first == 0 else 0.0
+            last = jnp.where((line == MARK % 8)[None], marks, tiles[t][:, whole:])
+            pieces += [last, jnp.zeros((owners, rows - MARK // 8 * 8 - 8, S), jnp.float32)]
+    pieces = [p for p in pieces if p.shape[1]]
+    out_ref[...] = jnp.concatenate(pieces, axis=1).astype(jnp.bfloat16)
+
+
+def project_chunk(count, route, offset, ku, kv, vis, table, keep, owners, n_tv, chunk, size):
     slots = ku.shape[1]
     return pl.pallas_call(
-        functools.partial(project_kernel, first=chunk * size),
-        out_shape=jax.ShapeDtypeStruct((owners, 2 * STACK, size * KEPT), jnp.bfloat16),
+        functools.partial(project_kernel, first=chunk * size, n_tv=n_tv),
+        out_shape=jax.ShapeDtypeStruct((owners, PACKED, S), jnp.bfloat16),
         grid_spec=pltpu.PrefetchScalarGridSpec(
-            num_scalar_prefetch=1,
+            num_scalar_prefetch=3,
             grid=(1,),
             in_specs=[
-                pl.BlockSpec((size, slots, S), lambda b, _: (chunk, 0, 0)),
-                pl.BlockSpec((size, slots, S), lambda b, _: (chunk, 0, 0)),
-                pl.BlockSpec((size, 2, slots), lambda b, _: (chunk, 0, 0)),
-                pl.BlockSpec(table.shape, lambda b, _: (0, 0)),
-                pl.BlockSpec(keep.shape, lambda b, _: (0, 0)),
-                pl.BlockSpec(mark.shape, lambda b, _: (0, 0)),
+                pl.BlockSpec((size, slots, S), lambda b, *_: (chunk, 0, 0)),
+                pl.BlockSpec((size, slots, S), lambda b, *_: (chunk, 0, 0)),
+                pl.BlockSpec((size, 2, slots), lambda b, *_: (chunk, 0, 0)),
+                pl.BlockSpec(table.shape, lambda b, *_: (0, 0, 0)),
+                pl.BlockSpec(keep.shape, lambda b, *_: (0, 0)),
             ],
-            out_specs=pl.BlockSpec((owners, 2 * STACK, size * KEPT), lambda b, _: (0, 0, 0)),
+            out_specs=pl.BlockSpec((owners, PACKED, S), lambda b, *_: (0, 0, 0)),
         ),
         compiler_params=pltpu.CompilerParams(vmem_limit_bytes=60 * MIB),
         cost_estimate=pl.CostEstimate(
@@ -140,22 +194,28 @@
             bytes_accessed=size * 4 * 65536,
             transcendentals=0,
         ),
-    )(count, ku, kv, vis, table, keep, mark)
+    )(count, route, offset, ku, kv, vis, table, keep)
 
 
 def add_blocks(
     row_ref, got_ref, phase_ref, expand_ref, back_ref, coeff_ref, acc_ref, chunk, size, per_src
 ):
-    sources, rows, width = got_ref.shape
+    sources = got_ref.shape[0]
+    packed = got_ref[...].astype(jnp.float32)
+    blank = jnp.zeros((sources, STACK - ROWS, S), jnp.float32)
+    tiles = [
+        jnp.concatenate([packed[:, ROWS * t : ROWS * (t + 1)], blank], axis=1)
+        .astype(jnp.bfloat16)
+        .reshape(sources * STACK, S)
+        for t in range(size * KEPT // S)
+    ]
     for g in range(size // 2):
-        lo = 2 * KEPT * g // 128 * 128
+        t = 2 * KEPT * g // S
         part = jnp.dot(
-            got_ref[:, :, lo : lo + 256].reshape(sources * rows, 256),
-            back_ref[lo : lo + 256, 256 * g : 256 * (g + 1)],
-            preferred_element_type=jnp.float32,
+            jnp.concatenate(tiles[t : t + 2], axis=1), back_ref[g], preferred_element_type=jnp.float32
         )
         coeff_ref[:, :, 256 * g : 256 * (g + 1)] = part.astype(jnp.bfloat16).reshape(
-            sources, rows, 256
+            sources, STACK, 256
         )
     by_cos, by_sin = expand_ref[0], expand_ref[1]
 
@@ -188,7 +248,7 @@
 
 
 def coeff_scratch(got, size):
-    return pltpu.VMEM((got.shape[0], got.shape[1], size * S), jnp.bfloat16)
+    return pltpu.VMEM((got.shape[0], STACK, size * S), jnp.bfloat16)
 
 
 def grid_chunk(rows, got, phase, expand, back, chunk, size, per_src):
@@ -325,7 +385,7 @@
             *buffers[1:],
             pltpu.SemaphoreType.DMA((3,)),
         ],
-        compiler_params=pltpu.CompilerParams(vmem_limit_bytes=45 * MIB),
+        compiler_params=pltpu.CompilerParams(vmem_limit_bytes=EVEN_MIB * MIB),
         cost_estimate=pl.CostEstimate(
             flops=16 * 1024**3, bytes_accessed=24 * MIB, transcendentals=0
         ),
@@ -336,7 +396,7 @@
         in_specs=[smem, vmem, vmem, vmem],
         out_specs=(vmem, vmem),
         scratch_shapes=[buffers[2]],
-        compiler_params=pltpu.CompilerParams(vmem_limit_bytes=22 * MIB),
+        compiler_params=pltpu.CompilerParams(vmem_limit_bytes=ODD_MIB * MIB),
         cost_estimate=pl.CostEstimate(
             flops=4 * 1024**3, bytes_accessed=12 * MIB, transcendentals=0
         ),
@@ -409,17 +469,9 @@
     blocks, slots = kernel_u.shape[0], kernel_u.shape[1]
     size = blocks // CHUNKS
     project, expand = factor_tables(owners)
-    tables = row_table()
-    keep = keep_table(size)
-    back = np.ascontiguousarray(keep.T)
-
-    target = tile_route[:, 0]
-    corner = jnp.stack(
-        [target // n_tv * TILE + block_offset[:, 0], target % n_tv * TILE + block_offset[:, 1]],
-        axis=0,
-    )
-    halves = jnp.stack([corner // 64, corner % 64], axis=1).reshape(1, 4 * blocks)
-    mark = jnp.pad(halves, ((0, 0), (0, S - 4 * blocks))).astype(jnp.float32)
+    tables = row_tables()
+    keep, back = keep_tables(size)
+
     owner = lax.axis_index(("tu", "tv"))
     col_base = owner * COLS
     scale = 1.0 / math.sqrt(slots * blocks * owners * 16)
@@ -427,7 +479,8 @@
     got = []
     for chunk in range(CHUNKS):
         coeffs = project_chunk(
-            vis_count, kernel_u, kernel_v, visibilities, project, keep, mark, owners, chunk, size
+            vis_count, tile_route.T, block_offset.T, kernel_u, kernel_v, visibilities, project, keep,
+            owners, n_tv, chunk, size,
         )
         if chunk:
             coeffs, screens = lax.optimization_barrier((coeffs, screens))

time: 106 us -> 101 us (0.953)
  waiting for transfers between devices: 16.6 us -> 14.4 us
  other arithmetic: 3.89 us -> 2.61 us
    all_to_all x2, waiting for transfers between devices: 9.6 us -> 7.25 us  [body(): lax.all_to_all(coeffs, ('tu', 'tv'), split_axis=0, concat_axis=0, tiled=T...]
  transfers between devices with their start and end apart: 12 -> 12, of which waited for: 4 -> 4; matrix products, arithmetic and copies ran while one was open for 3% -> 3% of each run, Pallas kernels for 27% -> 28%
where the time goes in v4:
time: 101 us
  Pallas kernels  47.1 us (47%)
  starting transfers between devices  30.1 us (30%)
  waiting for transfers between devices  14.4 us (14%)
  local copies, waits for them, and re-layouts  5.53 us (5%)
  other arithmetic  2.61 us (3%)
    ppermute x10, starting transfers between devices, shifted(): return lax.ppermute(values, 'wa', pairs).astype(jnp.float32)  17.9 us
    pallas_call x1, Pallas kernels, make_image(): pl.pallas_call(functools.partial(even_kernel, chunk=chunk, size=size, per...  14.8 us
    all_to_all x2, starting transfers between devices, body(): lax.all_to_all(coeffs, ('tu', 'tv'), split_axis=0, concat_axis=0, tiled=T...  12.2 us
    pallas_call x1, Pallas kernels, grid_chunk(): pl.pallas_call(functools.partial(grid_kernel, chunk=chunk, size=size, per...  11.7 us
    pallas_call x1, Pallas kernels, make_screen(): pl.pallas_call(functools.partial(screen_kernel, scale=scale), out_shape=(...  9.03 us
    pallas_call x2, Pallas kernels, project_chunk(): pl.pallas_call(functools.partial(project_kernel, first=chunk * size, n_tv...  8.41 us
    all_to_all x2, waiting for transfers between devices, body(): lax.all_to_all(coeffs, ('tu', 'tv'), split_axis=0, concat_axis=0, tiled=T...  7.25 us
    ppermute x10, waiting for transfers between devices, shifted(): return lax.ppermute(values, 'wa', pairs).astype(jnp.float32)  7.14 us
  transfers between devices with their start and end apart: 12, of which 4 were waited for; matrix products, arithmetic and copies ran while one was open for 3% of the time, Pallas kernels for 28%

profile of v4, /device:TPU:2, one launch (start us, length us, event | category | flops | bytes accessed | tf_op | source)
XLA Modules:
  0.0 100.7 jit_solution(14279814059343807144)
XLA Ops:
  0.0 4.2 %shard_map.127 = bf16[16,144,128]{2,1,0:T(8,128)(2,1)} custom-call(s32[16]{0:T(128)} %count_ref.3, s32[1,16]{1,0:T(1,128)} %bitcast.27, s32[2,16]{1,0:T(2,128)} %bitcast.25, bf16[16,256,128]{2,1,0:T(8,128)(2,1)} %ku_ref.3, bf16[16,256,128]{2,1,0:T(8,128)(2,1)} %kv_ref.3, bf16[16,2,256]{2,1,0:T(2,128)(2,1)} %vis_ref.3, ...), custom_call_target="tpu_custom_call" | custom-call | flops 402653184 | bytes 2097152 | tf_op jit(solution)/shard_map/pallas_call | solution.py:176
  4.2 8.6 %all-to-all-start = ((bf16[16,144,128]{2,1,0:T(8,128)(2,1)}), bf16[16,144,128]{2,1,0:T(8,128)(2,1)S(1)}, u32[]{:S(2)}, u32[]{:S(2)}) async-start(bf16[16,144,128]{2,1,0:T(8,128)(2,1)} %shard_map.127), calls=%async_computation | async-start | bytes 1179648 | tf_op jit(solution)/shard_map/all_to_all | solution.py:488
  13.6 9.0 %shard_map.129 = (f32[8,2,256,256]{3,2,1,0:T(8,128)}, f32[8,2,256,256]{3,2,1,0:T(8,128)}) custom-call(s32[1]{0:T(128)} %bitcast.3.base_ref, f32[1]{0:T(128)S(6)} %copy.15.w_ref), custom_call_target="tpu_custom_call" | custom-call | flops 41943040 | bytes 8388608 | tf_op jit(solution)/shard_map/pallas_call | solution.py:439
  22.6 4.2 %shard_map.128 = bf16[16,144,128]{2,1,0:T(8,128)(2,1)} custom-call(s32[16]{0:T(128)} %count_ref.3, s32[1,16]{1,0:T(1,128)} %bitcast.28, s32[2,16]{1,0:T(2,128)} %bitcast.26, bf16[16,256,128]{2,1,0:T(8,128)(2,1)} %ku_ref.3, bf16[16,256,128]{2,1,0:T(8,128)(2,1)} %kv_ref.3, bf16[16,2,256]{2,1,0:T(2,128)(2,1)} %vis_ref.3, ...), custom_call_target="tpu_custom_call" | custom-call | flops 402653184 | bytes 2097152 | tf_op jit(solution)/shard_map/pallas_call | solution.py:176
  26.8 3.9 %all-to-all-done.got_ref = bf16[16,144,128]{2,1,0:T(8,128)(2,1)S(1)} async-done(((bf16[16,144,128]{2,1,0:T(8,128)(2,1)}), bf16[16,144,128]{2,1,0:T(8,128)(2,1)S(1)}, u32[]{:S(2)}, u32[]{:S(2)}) %all-to-all-start) | async-done | bytes 589856 | tf_op jit(solution)/shard_map/all_to_all | solution.py:488
  30.8 3.6 %all-to-all-start.1 = ((bf16[16,144,128]{2,1,0:T(8,128)(2,1)}), bf16[16,144,128]{2,1,0:T(8,128)(2,1)S(1)}, u32[]{:S(2)}, u32[]{:S(2)}) async-start(bf16[16,144,128]{2,1,0:T(8,128)(2,1)} %shard_map.128), calls=%async_computation.1 | async-start | bytes 1179648 | tf_op jit(solution)/shard_map/all_to_all | solution.py:488
  34.8 1.1 %fusion.5 = (f32[256,256]{1,0:T(8,128)S(1)}, f32[256,256]{1,0:T(8,128)S(1)}) fusion(f32[256]{0:T(256)S(1)} %add_multiply_fusion, s32[256]{0:T(256)S(1)} %get-tuple-element.38, s32[256]{0:T(256)S(1)} %get-tuple-element.37, s32[256]{0:T(256)S(1)} %mul.89), kind=kLoop, calls=%fused_computation.14 | loop fusion | flops 1048576 | bytes 528384 | tf_op jit(solution)/shard_map/cos | solution.py:499
  35.9 0.9 pad_maximum_fusion.phase_ref
  36.8 11.7 %shard_map.130.old_hbm = f32[4,4096,128]{2,1,0:T(8,128)} custom-call(s32[256]{0:T(256)} %copy-done.3, bf16[16,144,128]{2,1,0:T(8,128)(2,1)} %copy-done.7, f32[256,512]{1,0:T(8,128)} %pad_maximum_fusion.phase_ref, f32[2,32,512]{2,1,0:T(8,128)} %constant.125.clone.expand_ref, bf16[4,256,256]{2,1,0:T(8,128)(2,1)} %constant.126.clone.back_ref), custom_call_target="tpu_custom_call" | custom-call | flops 4294967296 | bytes 12582912 | tf_op jit(solution)/shard_map/pallas_call | solution.py:256
  48.6 3.3 %all-to-all-done.1.got_ref = bf16[16,144,128]{2,1,0:T(8,128)(2,1)S(1)} async-done(((bf16[16,144,128]{2,1,0:T(8,128)(2,1)}), bf16[16,144,128]{2,1,0:T(8,128)(2,1)S(1)}, u32[]{:S(2)}, u32[]{:S(2)}) %all-to-all-start.1) | async-done | bytes 589856 | tf_op jit(solution)/shard_map/all_to_all | solution.py:488
  52.6 14.8 %shard_map.131 = (bf16[8,8,16,256]{3,2,1,0:T(8,128)(2,1)S(1)}, bf16[8,8,16,256]{3,2,1,0:T(8,128)(2,1)S(1)}, bf16[8,1024,256]{2,1,0:T(8,128)(2,1)S(1)}) custom-call(s32[256]{0:T(256)S(1)} %copy-done.4, s32[2,8]{1,0:T(2,128)S(1)} %pad_add_fusion.place_ref, bf16[16,144,128]{2,1,0:T(8,128)(2,1)S(1)} %all-to-all-done.1.got_ref, f32[256,512]{1,0:T(8,128)S(1)} %copy-done.2, ...), custom_call_target="tpu_custom_call" | custom-call | flops 17179869184 | bytes 25165824 | tf_op jit(solution)/shard_map/pallas_call | solution.py:374
  67.5 3.4 %copy-done = bf16[8,512,1024]{2,1,0:T(8,128)(2,1)S(1)} copy-done((bf16[8,512,1024]{2,1,0:T(8,128)(2,1)S(1)}, bf16[8,512,1024]{2,1,0:T(8,128)(2,1)}, u32[]{:S(2)}) %copy-start) | copy-done | bytes 8388632
  70.9 3.1 %shard_map.132 = (bf16[8,8,16,256]{3,2,1,0:T(8,128)(2,1)S(1)}, bf16[8,8,16,256]{3,2,1,0:T(8,128)(2,1)S(1)}) custom-call(s32[2,8]{1,0:T(2,128)S(1)} %pad_add_fusion.place_ref, bf16[8,1024,256]{2,1,0:T(8,128)(2,1)S(1)} %get-tuple-element.21.mid_ref, bf16[8,512,1024]{2,1,0:T(8,128)(2,1)S(1)} %copy-done, f32[8,2,256,256]{3,2,1,0:T(8,128)S(1)} %copy-done.1), custom_call_target="tpu_custom_call" | custom-call | flops 4294967296 | bytes 12582912 | tf_op jit(solution)/shard_map/pallas_call | solution.py:393
  74.0 0.8 collective-permute-start.5
  75.0 1.6 %collective-permute-start.1 = (bf16[2,8,16,256]{3,2,1,0:T(8,128)(2,1)S(1)}, bf16[2,8,16,256]{3,2,1,0:T(8,128)(2,1)S(1)}, u32[]{:S(2)}, u32[]{:S(2)}) collective-permute-start(bf16[2,8,16,256]{3,2,1,0:T(8,128)(2,1)S(1)} %get-tuple-element.27), channel_id=1, source_target_pairs={{0,64},{16,80},{32,96},{48,112},{64,128},{80,144},{96,160},{112,17... | collective-permute-start | bytes 393224 | tf_op jit(solution)/shard_map/ppermute | solution.py:455
  77.1 2.1 %collective-permute-start.2 = (bf16[2,8,16,256]{3,2,1,0:T(8,128)(2,1)S(1)}, bf16[2,8,16,256]{3,2,1,0:T(8,128)(2,1)S(1)}, u32[]{:S(2)}, u32[]{:S(2)}) collective-permute-start(bf16[2,8,16,256]{3,2,1,0:T(8,128)(2,1)S(1)} %get-tuple-element.29), channel_id=1, source_target_pairs={{0,128},{16,144},{32,160},{48,176},{64,192},{80,208},{96,224},{112... | collective-permute-start | bytes 393224 | tf_op jit(solution)/shard_map/ppermute | solution.py:455
  79.4 1.2 %collective-permute-start.6 = (bf16[2,8,16,256]{3,2,1,0:T(8,128)(2,1)S(1)}, bf16[2,8,16,256]{3,2,1,0:T(8,128)(2,1)S(1)}, u32[]{:S(2)}, u32[]{:S(2)}) collective-permute-start(bf16[2,8,16,256]{3,2,1,0:T(8,128)(2,1)S(1)} %get-tuple-element.30), channel_id=1, source_target_pairs={{0,64},{16,80},{32,96},{48,112},{64,128},{80,144},{96,160},{112,17... | collective-permute-start | bytes 393224 | tf_op jit(solution)/shard_map/ppermute | solution.py:455
  80.6 0.9 collective-permute-start.8
  81.5 1.9 %collective-permute-start.7 = (bf16[2,8,16,256]{3,2,1,0:T(8,128)(2,1)S(1)}, bf16[2,8,16,256]{3,2,1,0:T(8,128)(2,1)S(1)}, u32[]{:S(2)}, u32[]{:S(2)}) collective-permute-start(bf16[2,8,16,256]{3,2,1,0:T(8,128)(2,1)S(1)} %get-tuple-element.32), channel_id=1, source_target_pairs={{0,128},{16,144},{32,160},{48,176},{64,192},{80,208},{96,224},{112... | collective-permute-start | bytes 393224 | tf_op jit(solution)/shard_map/ppermute | solution.py:455
  83.4 3.0 %collective-permute-done.2 = bf16[2,8,16,256]{3,2,1,0:T(8,128)(2,1)S(1)} collective-permute-done((bf16[2,8,16,256]{3,2,1,0:T(8,128)(2,1)S(1)}, bf16[2,8,16,256]{3,2,1,0:T(8,128)(2,1)S(1)}, u32[]{:S(2)}, u32[]{:S(2)}) %collective-permute-start.2) | collective-permute-done | bytes 131104 | tf_op jit(solution)/shard_map/ppermute | solution.py:455
  86.5 4.6 %collective-permute-start.4 = (bf16[8,16,256]{2,1,0:T(8,128)(2,1)S(1)}, bf16[8,16,256]{2,1,0:T(8,128)(2,1)S(1)}, u32[]{:S(2)}, u32[]{:S(2)}) collective-permute-start(bf16[8,16,256]{2,1,0:T(8,128)(2,1)S(1)} %slice_bitcast_fusion.2), channel_id=1, source_target_pairs={{0,32},{16,48},{32,0},{48,16},{64,96},{80,112},{96,64},{112,80},{1... | collective-permute-start | bytes 196616 | tf_op jit(solution)/shard_map/ppermute | solution.py:455
  91.2 4.3 %collective-permute-start.9 = (bf16[8,16,256]{2,1,0:T(8,128)(2,1)S(1)}, bf16[8,16,256]{2,1,0:T(8,128)(2,1)S(1)}, u32[]{:S(2)}, u32[]{:S(2)}) collective-permute-start(bf16[8,16,256]{2,1,0:T(8,128)(2,1)S(1)} %slice_bitcast_fusion), channel_id=1, source_target_pairs={{0,32},{16,48},{32,0},{48,16},{64,96},{80,112},{96,64},{112,80},{1... | collective-permute-start | bytes 196616 | tf_op jit(solution)/shard_map/ppermute | solution.py:455
  95.5 4.1 %collective-permute-done.9 = bf16[8,16,256]{2,1,0:T(8,128)(2,1)S(1)} collective-permute-done((bf16[8,16,256]{2,1,0:T(8,128)(2,1)S(1)}, bf16[8,16,256]{2,1,0:T(8,128)(2,1)S(1)}, u32[]{:S(2)}, u32[]{:S(2)}) %collective-permute-start.9) | collective-permute-done | bytes 65568 | tf_op jit(solution)/shard_map/ppermute | solution.py:455
  99.8 0.9 reshape.158
  (47 shorter events, 2.5 us)
Async XLA Ops:
  4.2 26.6 %all-to-all-start = ((bf16[16,144,128]{2,1,0:T(8,128)(2,1)}), bf16[16,144,128]{2,1,0:T(8,128)(2,1)S(1)}, u32[]{:S(2)}, u32[]{:S(2)}) async-start(bf16[16,144,128]{2,1,0:T(8,128)(2,1)} %shard_map.127), calls=%async_computation | async-start | bytes 1179648 | tf_op jit(solution)/shard_map/all_to_all | solution.py:488
  30.8 6.1 %copy-start.7 = (bf16[16,144,128]{2,1,0:T(8,128)(2,1)}, bf16[16,144,128]{2,1,0:T(8,128)(2,1)S(1)}, u32[]{:S(2)}) copy-start(bf16[16,144,128]{2,1,0:T(8,128)(2,1)S(1)} %all-to-all-done.got_ref) | copy-start | bytes 1769476
  30.8 21.1 %all-to-all-start.1 = ((bf16[16,144,128]{2,1,0:T(8,128)(2,1)}), bf16[16,144,128]{2,1,0:T(8,128)(2,1)S(1)}, u32[]{:S(2)}, u32[]{:S(2)}) async-start(bf16[16,144,128]{2,1,0:T(8,128)(2,1)} %shard_map.128), calls=%async_computation.1 | async-start | bytes 1179648 | tf_op jit(solution)/shard_map/all_to_all | solution.py:488
  34.7 2.1 %copy-start.3 = (s32[256]{0:T(256)}, s32[256]{0:T(256)S(1)}, u32[]{:S(2)}) copy-start(s32[256]{0:T(256)S(1)} %reshape_squeeze.3.row_ref) | copy-start | bytes 3076
  35.9 16.0 %copy-start.5 = (bf16[4,256,256]{2,1,0:T(8,128)(2,1)S(1)}, bf16[4,256,256]{2,1,0:T(8,128)(2,1)}, u32[]{:S(2)}) copy-start(bf16[4,256,256]{2,1,0:T(8,128)(2,1)} %constant.126.clone.back_ref) | copy-start | bytes 1572868
  35.9 16.0 %copy-start.6 = (f32[2,32,512]{2,1,0:T(8,128)S(1)}, f32[2,32,512]{2,1,0:T(8,128)}, u32[]{:S(2)}) copy-start(f32[2,32,512]{2,1,0:T(8,128)} %constant.125.clone.expand_ref) | copy-start | bytes 393220
  36.8 15.0 %copy-start.2 = (f32[256,512]{1,0:T(8,128)S(1)}, f32[256,512]{1,0:T(8,128)}, u32[]{:S(2)}) copy-start(f32[256,512]{1,0:T(8,128)} %pad_maximum_fusion.phase_ref) | copy-start | bytes 1572868
  51.9 0.7 copy-start.4
  52.6 14.9 %copy-start.1 = (f32[8,2,256,256]{3,2,1,0:T(8,128)S(1)}, f32[8,2,256,256]{3,2,1,0:T(8,128)}, u32[]{:S(2)}) copy-start(f32[8,2,256,256]{3,2,1,0:T(8,128)} %get-tuple-element.22.screen_ref) | copy-start | bytes 12582916
  67.4 7.4 %collective-permute-start = (bf16[8,8,16,256]{3,2,1,0:T(8,128)(2,1)S(1)}, bf16[8,8,16,256]{3,2,1,0:T(8,128)(2,1)S(1)}, u32[]{:S(2)}, u32[]{:S(2)}) collective-permute-start(bf16[8,8,16,256]{3,2,1,0:T(8,128)(2,1)S(1)} %get-tuple-element.20), channel_id=1, source_target_pairs={{0,16},{16,0},{32,48},{48,32},{64,80},{80,64},{96,112},{112,96},{1... | collective-permute-start | bytes 1572872 | tf_op jit(solution)/shard_map/ppermute | solution.py:455
  67.5 3.4 %copy-start = (bf16[8,512,1024]{2,1,0:T(8,128)(2,1)S(1)}, bf16[8,512,1024]{2,1,0:T(8,128)(2,1)}, u32[]{:S(2)}) copy-start(bf16[8,512,1024]{2,1,0:T(8,128)(2,1)} %constant.128.clone.table_ref) | copy-start | bytes 25165828
  74.0 5.2 %collective-permute-start.5 = (bf16[8,8,16,256]{3,2,1,0:T(8,128)(2,1)S(1)}, bf16[8,8,16,256]{3,2,1,0:T(8,128)(2,1)S(1)}, u32[]{:S(2)}, u32[]{:S(2)}) collective-permute-start(bf16[8,8,16,256]{3,2,1,0:T(8,128)(2,1)S(1)} %get-tuple-element.24), channel_id=1, source_target_pairs={{0,16},{16,0},{32,48},{48,32},{64,80},{80,64},{96,112},{112,96},{1... | collective-permute-start | bytes 1572872 | tf_op jit(solution)/shard_map/ppermute | solution.py:455
  75.0 6.5 %collective-permute-start.1 = (bf16[2,8,16,256]{3,2,1,0:T(8,128)(2,1)S(1)}, bf16[2,8,16,256]{3,2,1,0:T(8,128)(2,1)S(1)}, u32[]{:S(2)}, u32[]{:S(2)}) collective-permute-start(bf16[2,8,16,256]{3,2,1,0:T(8,128)(2,1)S(1)} %get-tuple-element.27), channel_id=1, source_target_pairs={{0,64},{16,80},{32,96},{48,112},{64,128},{80,144},{96,160},{112,17... | collective-permute-start | bytes 393224 | tf_op jit(solution)/shard_map/ppermute | solution.py:455
  76.6 6.8 %collective-permute-start.3 = (bf16[2,8,16,256]{3,2,1,0:T(8,128)(2,1)S(1)}, bf16[2,8,16,256]{3,2,1,0:T(8,128)(2,1)S(1)}, u32[]{:S(2)}, u32[]{:S(2)}) collective-permute-start(bf16[2,8,16,256]{3,2,1,0:T(8,128)(2,1)S(1)} %get-tuple-element.28), channel_id=1, source_target_pairs={{0,192},{16,208},{32,224},{48,240},{64,0},{80,16},{96,32},{112,48}... | collective-permute-start | bytes 393224 | tf_op jit(solution)/shard_map/ppermute | solution.py:455
  77.1 9.3 %collective-permute-start.2 = (bf16[2,8,16,256]{3,2,1,0:T(8,128)(2,1)S(1)}, bf16[2,8,16,256]{3,2,1,0:T(8,128)(2,1)S(1)}, u32[]{:S(2)}, u32[]{:S(2)}) collective-permute-start(bf16[2,8,16,256]{3,2,1,0:T(8,128)(2,1)S(1)} %get-tuple-element.29), channel_id=1, source_target_pairs={{0,128},{16,144},{32,160},{48,176},{64,192},{80,208},{96,224},{112... | collective-permute-start | bytes 393224 | tf_op jit(solution)/shard_map/ppermute | solution.py:455
  79.4 11.7 %collective-permute-start.6 = (bf16[2,8,16,256]{3,2,1,0:T(8,128)(2,1)S(1)}, bf16[2,8,16,256]{3,2,1,0:T(8,128)(2,1)S(1)}, u32[]{:S(2)}, u32[]{:S(2)}) collective-permute-start(bf16[2,8,16,256]{3,2,1,0:T(8,128)(2,1)S(1)} %get-tuple-element.30), channel_id=1, source_target_pairs={{0,64},{16,80},{32,96},{48,112},{64,128},{80,144},{96,160},{112,17... | collective-permute-start | bytes 393224 | tf_op jit(solution)/shard_map/ppermute | solution.py:455
  80.6 10.5 %collective-permute-start.8 = (bf16[2,8,16,256]{3,2,1,0:T(8,128)(2,1)S(1)}, bf16[2,8,16,256]{3,2,1,0:T(8,128)(2,1)S(1)}, u32[]{:S(2)}, u32[]{:S(2)}) collective-permute-start(bf16[2,8,16,256]{3,2,1,0:T(8,128)(2,1)S(1)} %get-tuple-element.31), channel_id=1, source_target_pairs={{0,192},{16,208},{32,224},{48,240},{64,0},{80,16},{96,32},{112,48}... | collective-permute-start | bytes 393224 | tf_op jit(solution)/shard_map/ppermute | solution.py:455
  81.5 9.6 %collective-permute-start.7 = (bf16[2,8,16,256]{3,2,1,0:T(8,128)(2,1)S(1)}, bf16[2,8,16,256]{3,2,1,0:T(8,128)(2,1)S(1)}, u32[]{:S(2)}, u32[]{:S(2)}) collective-permute-start(bf16[2,8,16,256]{3,2,1,0:T(8,128)(2,1)S(1)} %get-tuple-element.32), channel_id=1, source_target_pairs={{0,128},{16,144},{32,160},{48,176},{64,192},{80,208},{96,224},{112... | collective-permute-start | bytes 393224 | tf_op jit(solution)/shard_map/ppermute | solution.py:455
  86.5 9.0 %collective-permute-start.4 = (bf16[8,16,256]{2,1,0:T(8,128)(2,1)S(1)}, bf16[8,16,256]{2,1,0:T(8,128)(2,1)S(1)}, u32[]{:S(2)}, u32[]{:S(2)}) collective-permute-start(bf16[8,16,256]{2,1,0:T(8,128)(2,1)S(1)} %slice_bitcast_fusion.2), channel_id=1, source_target_pairs={{0,32},{16,48},{32,0},{48,16},{64,96},{80,112},{96,64},{112,80},{1... | collective-permute-start | bytes 196616 | tf_op jit(solution)/shard_map/ppermute | solution.py:455
  91.2 8.4 %collective-permute-start.9 = (bf16[8,16,256]{2,1,0:T(8,128)(2,1)S(1)}, bf16[8,16,256]{2,1,0:T(8,128)(2,1)S(1)}, u32[]{:S(2)}, u32[]{:S(2)}) collective-permute-start(bf16[8,16,256]{2,1,0:T(8,128)(2,1)S(1)} %slice_bitcast_fusion), channel_id=1, source_target_pairs={{0,32},{16,48},{32,0},{48,16},{64,96},{80,112},{96,64},{112,80},{1... | collective-permute-start | bytes 196616 | tf_op jit(solution)/shard_map/ppermute | solution.py:455

commit v5 on v4

--- a/solution.py
+++ b/solution.py
@@ -19,6 +19,7 @@
 PACKED = 144
 MARK = 140
 KEPT = 80
+PIECE = 2
 COLS = 256
 U0 = 512
 U1 = 8
@@ -42,7 +43,7 @@
     return v * np.sign(v[peak, np.arange(count)])
 
 
-def factor_tables(owners):
+def factor_tables(n_tu, n_tv):
     t = np.arange(S) - (S - 1) / 2
     mu = np.arange(COLS) - (COLS - 1) / 2
     basis = prolate(RANK, COLS / 2 / N)
@@ -50,7 +51,7 @@
     project = []
     for pad in ((0, STACK - ROWS), (STACK - ROWS, 0)):
         rows = []
-        for j in range(owners):
+        for j in [tu * n_tv + tv for tv in range(n_tv) for tu in range(n_tu)]:
             centre = COLS * j + (COLS - 1) / 2
             turn = np.exp(2j * np.pi * np.arange(S) * centre / N)
             proj = basis.T * turn[None, :]
@@ -91,7 +92,7 @@
     table = np.concatenate(
         [np.concatenate([c, -s], axis=2), np.concatenate([s, c], axis=2)], axis=1
     )
-    return table[0::2], table[1::2]
+    return table[0::2], [table[k : 2 * PIECE + k : 2] for k in range(1, L0, 2 * PIECE)]
 
 
 def corner_marks(route_ref, offset_ref, n_tv):
@@ -291,14 +292,14 @@
     return [add(e[k], o[k]) for k in range(4)] + [sub(e[k], o[k]) for k in range(4)]
 
 
-def finish(place_ref, table_ref, mid_ref, screen_ref, full_ref, keep_ref, send_ref):
-    def last_step(k, carry):
-        planar = jnp.dot(table_ref[k], mid_ref[k], preferred_element_type=jnp.float32)
+def finish(place_ref, table_refs, mid_ref, screen_ref, full_ref, keep_ref, send_ref):
+    for k in range(L0 // 2):
+        ref = table_refs[k // table_refs[0].shape[0]]
+        planar = jnp.dot(
+            ref[k % ref.shape[0]], mid_ref[k], preferred_element_type=jnp.float32
+        )
         value = planar[:L1] * screen_ref[k, 0] - planar[L1:] * screen_ref[k, 1]
         full_ref[:, k] = value.astype(jnp.bfloat16).reshape(L1 // 16, 16, COLS)
-        return carry
-
-    lax.fori_loop(0, L0 // 2, last_step, 0, unroll=4)
     for out_ref, which in ((keep_ref, 0), (send_ref, 1)):
         for i in range(out_ref.shape[0]):
             out_ref[i] = full_ref[place_ref[which, i]]
@@ -348,13 +349,12 @@
     lax.fori_loop(0, U0 // 16, first_step, 0)
     load_table.wait()
     load_screen.wait()
-    finish(place_ref, table_ref, mid_ref, screen_ref, full_ref, keep_ref, send_ref)
-
-
-def odd_kernel(
-    place_ref, mid_ref, table_ref, screen_ref, keep_ref, send_ref, full_ref
-):
-    finish(place_ref, table_ref, mid_ref, screen_ref, full_ref, keep_ref, send_ref)
+    finish(place_ref, [table_ref], mid_ref, screen_ref, full_ref, keep_ref, send_ref)
+
+
+def odd_kernel(place_ref, mid_ref, screen_ref, *refs):
+    *table_refs, keep_ref, send_ref, full_ref = refs
+    finish(place_ref, table_refs, mid_ref, screen_ref, full_ref, keep_ref, send_ref)
 
 
 def make_image(
@@ -393,14 +393,14 @@
     keep_odd, send_odd = pl.pallas_call(
         odd_kernel,
         out_shape=(piece, piece),
-        in_specs=[smem, vmem, vmem, vmem],
+        in_specs=[smem, *[vmem] * (2 + len(tables[1]))],
         out_specs=(vmem, vmem),
         scratch_shapes=[buffers[2]],
         compiler_params=pltpu.CompilerParams(vmem_limit_bytes=ODD_MIB * MIB),
         cost_estimate=pl.CostEstimate(
             flops=4 * 1024**3, bytes_accessed=12 * MIB, transcendentals=0
         ),
-    )(place, odd, tables[1], screens[1])
+    )(place, odd, screens[1], *tables[1])
     return (keep, send), (keep_odd, send_odd)
 
 
@@ -468,7 +468,7 @@
     owners = n_tu * n_tv
     blocks, slots = kernel_u.shape[0], kernel_u.shape[1]
     size = blocks // CHUNKS
-    project, expand = factor_tables(owners)
+    project, expand = factor_tables(n_tu, n_tv)
     tables = row_tables()
     keep, back = keep_tables(size)
 
@@ -485,7 +485,7 @@
         if chunk:
             coeffs, screens = lax.optimization_barrier((coeffs, screens))
         got.append(
-            lax.all_to_all(coeffs, ("tu", "tv"), split_axis=0, concat_axis=0, tiled=True)
+            lax.all_to_all(coeffs, ("tv", "tu"), split_axis=0, concat_axis=0, tiled=True)
         )
     marks = got[0][:, MARK, : 4 * blocks].astype(jnp.int32).reshape(owners, 2, 2, blocks)
     corners = marks[:, :, 0] * 64 + marks[:, :, 1]

time: 101 us -> 99.1 us (0.981)
  waiting for transfers between devices: 14.4 us -> 11.8 us
  starting transfers between devices: 30.1 us -> 31.5 us
    all_to_all x2, waiting for transfers between devices: 7.25 us -> 4.52 us  [body(): lax.all_to_all(coeffs, ('tv', 'tu'), split_axis=0, concat_axis=0, tiled=T...]
    all_to_all x2, starting transfers between devices: 12.2 us -> 13.5 us  [body(): lax.all_to_all(coeffs, ('tv', 'tu'), split_axis=0, concat_axis=0, tiled=T...]
    unnamed x16 -> x22, local copies, waits for them, and re-layouts: 4.08 us -> 3.34 us
where the time goes in v5:
time: 99.1 us; the launch traced here: 98.5 us
  Pallas kernels  46.8 us (47%)
  starting transfers between devices  31.5 us (32%)
  waiting for transfers between devices  11.8 us (12%)
  local copies, waits for them, and re-layouts  4.79 us (5%)
  other arithmetic  2.6 us (3%)
    ppermute x10, starting transfers between devices, shifted(): return lax.ppermute(values, 'wa', pairs).astype(jnp.float32)  18 us
    pallas_call x1, Pallas kernels, make_image(): pl.pallas_call(functools.partial(even_kernel, chunk=chunk, size=size, per...  14.7 us
    all_to_all x2, starting transfers between devices, body(): lax.all_to_all(coeffs, ('tv', 'tu'), split_axis=0, concat_axis=0, tiled=T...  13.5 us
    pallas_call x1, Pallas kernels, grid_chunk(): pl.pallas_call(functools.partial(grid_kernel, chunk=chunk, size=size, per...  11.7 us
    pallas_call x1, Pallas kernels, make_screen(): pl.pallas_call(functools.partial(screen_kernel, scale=scale), out_shape=(...  9.02 us
    pallas_call x2, Pallas kernels, project_chunk(): pl.pallas_call(functools.partial(project_kernel, first=chunk * size, n_tv...  8.43 us
    ppermute x10, waiting for transfers between devices, shifted(): return lax.ppermute(values, 'wa', pairs).astype(jnp.float32)  7.32 us
    all_to_all x2, waiting for transfers between devices, body(): lax.all_to_all(coeffs, ('tv', 'tu'), split_axis=0, concat_axis=0, tiled=T...  4.52 us
  transfers between devices with their start and end apart: 12, of which 4 were waited for; matrix products, arithmetic and copies ran while one was open for 3% of the time, Pallas kernels for 28%

profile of v5, /device:TPU:2, one launch (start us, length us, event | category | flops | bytes accessed | tf_op | source)
XLA Modules:
  0.0 98.5 jit_solution(10472037577012755377)
XLA Ops:
  0.0 4.2 %shard_map.154 = bf16[16,144,128]{2,1,0:T(8,128)(2,1)} custom-call(s32[16]{0:T(128)} %count_ref.3, s32[1,16]{1,0:T(1,128)} %bitcast.27, s32[2,16]{1,0:T(2,128)} %bitcast.25, bf16[16,256,128]{2,1,0:T(8,128)(2,1)} %ku_ref.3, bf16[16,256,128]{2,1,0:T(8,128)(2,1)} %kv_ref.3, bf16[16,2,256]{2,1,0:T(2,128)(2,1)} %vis_ref.3, ...), custom_call_target="tpu_custom_call" | custom-call | flops 402653184 | bytes 2097152 | tf_op jit(solution)/shard_map/pallas_call | solution.py:177
  4.2 8.6 %all-to-all-start = ((bf16[16,144,128]{2,1,0:T(8,128)(2,1)}), bf16[16,144,128]{2,1,0:T(8,128)(2,1)S(1)}, u32[]{:S(2)}, u32[]{:S(2)}) async-start(bf16[16,144,128]{2,1,0:T(8,128)(2,1)} %shard_map.154), calls=%async_computation | async-start | bytes 1179648 | tf_op jit(solution)/shard_map/all_to_all | solution.py:488
  13.6 9.0 %shard_map.156 = (f32[8,2,256,256]{3,2,1,0:T(8,128)}, f32[8,2,256,256]{3,2,1,0:T(8,128)}) custom-call(s32[1]{0:T(128)} %bitcast.3.base_ref, f32[1]{0:T(128)S(6)} %copy.18.w_ref), custom_call_target="tpu_custom_call" | custom-call | flops 41943040 | bytes 8388608 | tf_op jit(solution)/shard_map/pallas_call | solution.py:439
  22.6 4.2 %shard_map.155 = bf16[16,144,128]{2,1,0:T(8,128)(2,1)} custom-call(s32[16]{0:T(128)} %count_ref.3, s32[1,16]{1,0:T(1,128)} %bitcast.28, s32[2,16]{1,0:T(2,128)} %bitcast.26, bf16[16,256,128]{2,1,0:T(8,128)(2,1)} %ku_ref.3, bf16[16,256,128]{2,1,0:T(8,128)(2,1)} %kv_ref.3, bf16[16,2,256]{2,1,0:T(2,128)(2,1)} %vis_ref.3, ...), custom_call_target="tpu_custom_call" | custom-call | flops 402653184 | bytes 2097152 | tf_op jit(solution)/shard_map/pallas_call | solution.py:177
  26.8 2.6 %all-to-all-done.got_ref = bf16[16,144,128]{2,1,0:T(8,128)(2,1)S(1)} async-done(((bf16[16,144,128]{2,1,0:T(8,128)(2,1)}), bf16[16,144,128]{2,1,0:T(8,128)(2,1)S(1)}, u32[]{:S(2)}, u32[]{:S(2)}) %all-to-all-start) | async-done | bytes 589856 | tf_op jit(solution)/shard_map/all_to_all | solution.py:488
  29.5 4.9 %all-to-all-start.1 = ((bf16[16,144,128]{2,1,0:T(8,128)(2,1)}), bf16[16,144,128]{2,1,0:T(8,128)(2,1)S(1)}, u32[]{:S(2)}, u32[]{:S(2)}) async-start(bf16[16,144,128]{2,1,0:T(8,128)(2,1)} %shard_map.155), calls=%async_computation.1 | async-start | bytes 1179648 | tf_op jit(solution)/shard_map/all_to_all | solution.py:488
  34.7 1.1 %fusion.5 = (f32[256,256]{1,0:T(8,128)S(1)}, f32[256,256]{1,0:T(8,128)S(1)}) fusion(f32[256]{0:T(256)S(1)} %add_multiply_fusion, s32[256]{0:T(256)S(1)} %get-tuple-element.38, s32[256]{0:T(256)S(1)} %get-tuple-element.37, s32[256]{0:T(256)S(1)} %mul.89), kind=kLoop, calls=%fused_computation.14 | loop fusion | flops 1048576 | bytes 528384 | tf_op jit(solution)/shard_map/cos | solution.py:499
  35.9 0.9 pad_maximum_fusion.phase_ref
  36.8 11.7 %shard_map.157.old_hbm = f32[4,4096,128]{2,1,0:T(8,128)} custom-call(s32[256]{0:T(256)} %copy-done.6, bf16[16,144,128]{2,1,0:T(8,128)(2,1)} %copy-done.10, f32[256,512]{1,0:T(8,128)} %pad_maximum_fusion.phase_ref, f32[2,32,512]{2,1,0:T(8,128)} %constant.131.clone.expand_ref, bf16[4,256,256]{2,1,0:T(8,128)(2,1)} %constant.132.clone.back_ref), custom_call_target="tpu_custom_call" | custom-call | flops 4294967296 | bytes 12582912 | tf_op jit(solution)/shard_map/pallas_call | solution.py:257
  48.5 1.9 %all-to-all-done.1.got_ref = bf16[16,144,128]{2,1,0:T(8,128)(2,1)S(1)} async-done(((bf16[16,144,128]{2,1,0:T(8,128)(2,1)}), bf16[16,144,128]{2,1,0:T(8,128)(2,1)S(1)}, u32[]{:S(2)}, u32[]{:S(2)}) %all-to-all-start.1) | async-done | bytes 589856 | tf_op jit(solution)/shard_map/all_to_all | solution.py:488
  51.1 1.0 %copy-done.8 = bf16[4,256,256]{2,1,0:T(8,128)(2,1)S(1)} copy-done((bf16[4,256,256]{2,1,0:T(8,128)(2,1)S(1)}, bf16[4,256,256]{2,1,0:T(8,128)(2,1)}, u32[]{:S(2)}) %copy-start.8) | copy-done | bytes 524312
  52.1 14.7 %shard_map.158 = (bf16[8,8,16,256]{3,2,1,0:T(8,128)(2,1)S(1)}, bf16[8,8,16,256]{3,2,1,0:T(8,128)(2,1)S(1)}, bf16[8,1024,256]{2,1,0:T(8,128)(2,1)S(1)}) custom-call(s32[256]{0:T(256)S(1)} %copy-done.7, s32[2,8]{1,0:T(2,128)S(1)} %pad_add_fusion.place_ref, bf16[16,144,128]{2,1,0:T(8,128)(2,1)S(1)} %all-to-all-done.1.got_ref, f32[256,512]{1,0:T(8,128)S(1)} %copy-done.5, ...), custom_call_target="tpu_custom_call" | custom-call | flops 17179869184 | bytes 25165824 | tf_op jit(solution)/shard_map/pallas_call | solution.py:374
  67.1 1.6 %copy-done.4 = bf16[2,512,1024]{2,1,0:T(8,128)(2,1)S(1)} copy-done((bf16[2,512,1024]{2,1,0:T(8,128)(2,1)S(1)}, bf16[2,512,1024]{2,1,0:T(8,128)(2,1)}, u32[]{:S(2)}) %copy-start.4) | copy-done | bytes 2097176
  68.7 3.0 %shard_map.159 = (bf16[8,8,16,256]{3,2,1,0:T(8,128)(2,1)S(1)}, bf16[8,8,16,256]{3,2,1,0:T(8,128)(2,1)S(1)}) custom-call(s32[2,8]{1,0:T(2,128)S(1)} %pad_add_fusion.place_ref, bf16[8,1024,256]{2,1,0:T(8,128)(2,1)S(1)} %get-tuple-element.21.mid_ref, f32[8,2,256,256]{3,2,1,0:T(8,128)S(1)} %copy-done, bf16[2,512,1024]{2,1,0:T(8,128)(2,1)S(1)} %copy-done.4, ...), custom_call_target="tpu_custom_call" | custom-call | flops 4294967296 | bytes 12582912 | tf_op jit(solution)/shard_map/pallas_call | solution.py:393
  72.5 1.6 %collective-permute-start.1 = (bf16[2,8,16,256]{3,2,1,0:T(8,128)(2,1)S(1)}, bf16[2,8,16,256]{3,2,1,0:T(8,128)(2,1)S(1)}, u32[]{:S(2)}, u32[]{:S(2)}) collective-permute-start(bf16[2,8,16,256]{3,2,1,0:T(8,128)(2,1)S(1)} %get-tuple-element.27), channel_id=1, source_target_pairs={{0,64},{16,80},{32,96},{48,112},{64,128},{80,144},{96,160},{112,17... | collective-permute-start | bytes 393224 | tf_op jit(solution)/shard_map/ppermute | solution.py:455
  74.6 2.1 %collective-permute-start.2 = (bf16[2,8,16,256]{3,2,1,0:T(8,128)(2,1)S(1)}, bf16[2,8,16,256]{3,2,1,0:T(8,128)(2,1)S(1)}, u32[]{:S(2)}, u32[]{:S(2)}) collective-permute-start(bf16[2,8,16,256]{3,2,1,0:T(8,128)(2,1)S(1)} %get-tuple-element.29), channel_id=1, source_target_pairs={{0,128},{16,144},{32,160},{48,176},{64,192},{80,208},{96,224},{112... | collective-permute-start | bytes 393224 | tf_op jit(solution)/shard_map/ppermute | solution.py:455
  76.9 1.2 %collective-permute-start.6 = (bf16[2,8,16,256]{3,2,1,0:T(8,128)(2,1)S(1)}, bf16[2,8,16,256]{3,2,1,0:T(8,128)(2,1)S(1)}, u32[]{:S(2)}, u32[]{:S(2)}) collective-permute-start(bf16[2,8,16,256]{3,2,1,0:T(8,128)(2,1)S(1)} %get-tuple-element.30), channel_id=1, source_target_pairs={{0,64},{16,80},{32,96},{48,112},{64,128},{80,144},{96,160},{112,17... | collective-permute-start | bytes 393224 | tf_op jit(solution)/shard_map/ppermute | solution.py:455
  78.1 0.9 collective-permute-start.8
  79.0 1.9 %collective-permute-start.7 = (bf16[2,8,16,256]{3,2,1,0:T(8,128)(2,1)S(1)}, bf16[2,8,16,256]{3,2,1,0:T(8,128)(2,1)S(1)}, u32[]{:S(2)}, u32[]{:S(2)}) collective-permute-start(bf16[2,8,16,256]{3,2,1,0:T(8,128)(2,1)S(1)} %get-tuple-element.32), channel_id=1, source_target_pairs={{0,128},{16,144},{32,160},{48,176},{64,192},{80,208},{96,224},{112... | collective-permute-start | bytes 393224 | tf_op jit(solution)/shard_map/ppermute | solution.py:455
  81.0 2.9 %collective-permute-done.2 = bf16[2,8,16,256]{3,2,1,0:T(8,128)(2,1)S(1)} collective-permute-done((bf16[2,8,16,256]{3,2,1,0:T(8,128)(2,1)S(1)}, bf16[2,8,16,256]{3,2,1,0:T(8,128)(2,1)S(1)}, u32[]{:S(2)}, u32[]{:S(2)}) %collective-permute-start.2) | collective-permute-done | bytes 131104 | tf_op jit(solution)/shard_map/ppermute | solution.py:455
  84.0 4.6 %collective-permute-start.4 = (bf16[8,16,256]{2,1,0:T(8,128)(2,1)S(1)}, bf16[8,16,256]{2,1,0:T(8,128)(2,1)S(1)}, u32[]{:S(2)}, u32[]{:S(2)}) collective-permute-start(bf16[8,16,256]{2,1,0:T(8,128)(2,1)S(1)} %slice_bitcast_fusion.2), channel_id=1, source_target_pairs={{0,32},{16,48},{32,0},{48,16},{64,96},{80,112},{96,64},{112,80},{1... | collective-permute-start | bytes 196616 | tf_op jit(solution)/shard_map/ppermute | solution.py:455
  88.7 4.3 %collective-permute-start.9 = (bf16[8,16,256]{2,1,0:T(8,128)(2,1)S(1)}, bf16[8,16,256]{2,1,0:T(8,128)(2,1)S(1)}, u32[]{:S(2)}, u32[]{:S(2)}) collective-permute-start(bf16[8,16,256]{2,1,0:T(8,128)(2,1)S(1)} %slice_bitcast_fusion), channel_id=1, source_target_pairs={{0,32},{16,48},{32,0},{48,16},{64,96},{80,112},{96,64},{112,80},{1... | collective-permute-start | bytes 196616 | tf_op jit(solution)/shard_map/ppermute | solution.py:455
  93.0 4.4 %collective-permute-done.9 = bf16[8,16,256]{2,1,0:T(8,128)(2,1)S(1)} collective-permute-done((bf16[8,16,256]{2,1,0:T(8,128)(2,1)S(1)}, bf16[8,16,256]{2,1,0:T(8,128)(2,1)S(1)}, u32[]{:S(2)}, u32[]{:S(2)}) %collective-permute-start.9) | collective-permute-done | bytes 65568 | tf_op jit(solution)/shard_map/ppermute | solution.py:455
  97.6 0.9 reshape.158
  (53 shorter events, 3.2 us)
Async XLA Ops:
  4.2 25.2 %all-to-all-start = ((bf16[16,144,128]{2,1,0:T(8,128)(2,1)}), bf16[16,144,128]{2,1,0:T(8,128)(2,1)S(1)}, u32[]{:S(2)}, u32[]{:S(2)}) async-start(bf16[16,144,128]{2,1,0:T(8,128)(2,1)} %shard_map.154), calls=%async_computation | async-start | bytes 1179648 | tf_op jit(solution)/shard_map/all_to_all | solution.py:488
  29.5 7.3 %copy-start.10 = (bf16[16,144,128]{2,1,0:T(8,128)(2,1)}, bf16[16,144,128]{2,1,0:T(8,128)(2,1)S(1)}, u32[]{:S(2)}) copy-start(bf16[16,144,128]{2,1,0:T(8,128)(2,1)S(1)} %all-to-all-done.got_ref) | copy-start | bytes 1769476
  29.5 20.9 %all-to-all-start.1 = ((bf16[16,144,128]{2,1,0:T(8,128)(2,1)}), bf16[16,144,128]{2,1,0:T(8,128)(2,1)S(1)}, u32[]{:S(2)}, u32[]{:S(2)}) async-start(bf16[16,144,128]{2,1,0:T(8,128)(2,1)} %shard_map.155), calls=%async_computation.1 | async-start | bytes 1179648 | tf_op jit(solution)/shard_map/all_to_all | solution.py:488
  34.7 2.0 %copy-start.6 = (s32[256]{0:T(256)}, s32[256]{0:T(256)S(1)}, u32[]{:S(2)}) copy-start(s32[256]{0:T(256)S(1)} %reshape_squeeze.3.row_ref) | copy-start | bytes 3076
  36.8 13.6 %copy-start.5 = (f32[256,512]{1,0:T(8,128)S(1)}, f32[256,512]{1,0:T(8,128)}, u32[]{:S(2)}) copy-start(f32[256,512]{1,0:T(8,128)} %pad_maximum_fusion.phase_ref) | copy-start | bytes 1572868
  36.8 13.6 %copy-start.9 = (f32[2,32,512]{2,1,0:T(8,128)S(1)}, f32[2,32,512]{2,1,0:T(8,128)}, u32[]{:S(2)}) copy-start(f32[2,32,512]{2,1,0:T(8,128)} %constant.131.clone.expand_ref) | copy-start | bytes 393220
  48.5 18.6 %copy-start.1 = (bf16[2,512,1024]{2,1,0:T(8,128)(2,1)S(1)}, bf16[2,512,1024]{2,1,0:T(8,128)(2,1)}, u32[]{:S(2)}) copy-start(bf16[2,512,1024]{2,1,0:T(8,128)(2,1)} %constant.137.clone.refs_3_) | copy-start | bytes 6291460
  50.4 0.7 copy-start.7
  51.1 1.0 %copy-start.8 = (bf16[4,256,256]{2,1,0:T(8,128)(2,1)S(1)}, bf16[4,256,256]{2,1,0:T(8,128)(2,1)}, u32[]{:S(2)}) copy-start(bf16[4,256,256]{2,1,0:T(8,128)(2,1)} %constant.132.clone.back_ref) | copy-start | bytes 1572868
  52.1 15.0 %copy-start = (f32[8,2,256,256]{3,2,1,0:T(8,128)S(1)}, f32[8,2,256,256]{3,2,1,0:T(8,128)}, u32[]{:S(2)}) copy-start(f32[8,2,256,256]{3,2,1,0:T(8,128)} %get-tuple-element.22.screen_ref) | copy-start | bytes 12582916
  52.1 15.0 %copy-start.2 = (bf16[2,512,1024]{2,1,0:T(8,128)(2,1)S(1)}, bf16[2,512,1024]{2,1,0:T(8,128)(2,1)}, u32[]{:S(2)}) copy-start(bf16[2,512,1024]{2,1,0:T(8,128)(2,1)} %constant.136.clone.refs_2_) | copy-start | bytes 6291460
  52.1 15.0 %copy-start.3 = (bf16[2,512,1024]{2,1,0:T(8,128)(2,1)S(1)}, bf16[2,512,1024]{2,1,0:T(8,128)(2,1)}, u32[]{:S(2)}) copy-start(bf16[2,512,1024]{2,1,0:T(8,128)(2,1)} %constant.135.clone.refs_1_) | copy-start | bytes 6291460
  66.8 5.5 %collective-permute-start = (bf16[8,8,16,256]{3,2,1,0:T(8,128)(2,1)S(1)}, bf16[8,8,16,256]{3,2,1,0:T(8,128)(2,1)S(1)}, u32[]{:S(2)}, u32[]{:S(2)}) collective-permute-start(bf16[8,8,16,256]{3,2,1,0:T(8,128)(2,1)S(1)} %get-tuple-element.20), channel_id=1, source_target_pairs={{0,16},{16,0},{32,48},{48,32},{64,80},{80,64},{96,112},{112,96},{1... | collective-permute-start | bytes 1572872 | tf_op jit(solution)/shard_map/ppermute | solution.py:455
  67.1 1.6 %copy-start.4 = (bf16[2,512,1024]{2,1,0:T(8,128)(2,1)S(1)}, bf16[2,512,1024]{2,1,0:T(8,128)(2,1)}, u32[]{:S(2)}) copy-start(bf16[2,512,1024]{2,1,0:T(8,128)(2,1)} %constant.134.clone.refs_0_) | copy-start | bytes 6291460
  71.7 5.0 %collective-permute-start.5 = (bf16[8,8,16,256]{3,2,1,0:T(8,128)(2,1)S(1)}, bf16[8,8,16,256]{3,2,1,0:T(8,128)(2,1)S(1)}, u32[]{:S(2)}, u32[]{:S(2)}) collective-permute-start(bf16[8,8,16,256]{3,2,1,0:T(8,128)(2,1)S(1)} %get-tuple-element.24), channel_id=1, source_target_pairs={{0,16},{16,0},{32,48},{48,32},{64,80},{80,64},{96,112},{112,96},{1... | collective-permute-start | bytes 1572872 | tf_op jit(solution)/shard_map/ppermute | solution.py:455
  72.5 6.5 %collective-permute-start.1 = (bf16[2,8,16,256]{3,2,1,0:T(8,128)(2,1)S(1)}, bf16[2,8,16,256]{3,2,1,0:T(8,128)(2,1)S(1)}, u32[]{:S(2)}, u32[]{:S(2)}) collective-permute-start(bf16[2,8,16,256]{3,2,1,0:T(8,128)(2,1)S(1)} %get-tuple-element.27), channel_id=1, source_target_pairs={{0,64},{16,80},{32,96},{48,112},{64,128},{80,144},{96,160},{112,17... | collective-permute-start | bytes 393224 | tf_op jit(solution)/shard_map/ppermute | solution.py:455
  74.1 6.9 %collective-permute-start.3 = (bf16[2,8,16,256]{3,2,1,0:T(8,128)(2,1)S(1)}, bf16[2,8,16,256]{3,2,1,0:T(8,128)(2,1)S(1)}, u32[]{:S(2)}, u32[]{:S(2)}) collective-permute-start(bf16[2,8,16,256]{3,2,1,0:T(8,128)(2,1)S(1)} %get-tuple-element.28), channel_id=1, source_target_pairs={{0,192},{16,208},{32,224},{48,240},{64,0},{80,16},{96,32},{112,48}... | collective-permute-start | bytes 393224 | tf_op jit(solution)/shard_map/ppermute | solution.py:455
  74.6 9.3 %collective-permute-start.2 = (bf16[2,8,16,256]{3,2,1,0:T(8,128)(2,1)S(1)}, bf16[2,8,16,256]{3,2,1,0:T(8,128)(2,1)S(1)}, u32[]{:S(2)}, u32[]{:S(2)}) collective-permute-start(bf16[2,8,16,256]{3,2,1,0:T(8,128)(2,1)S(1)} %get-tuple-element.29), channel_id=1, source_target_pairs={{0,128},{16,144},{32,160},{48,176},{64,192},{80,208},{96,224},{112... | collective-permute-start | bytes 393224 | tf_op jit(solution)/shard_map/ppermute | solution.py:455
  76.9 11.7 %collective-permute-start.6 = (bf16[2,8,16,256]{3,2,1,0:T(8,128)(2,1)S(1)}, bf16[2,8,16,256]{3,2,1,0:T(8,128)(2,1)S(1)}, u32[]{:S(2)}, u32[]{:S(2)}) collective-permute-start(bf16[2,8,16,256]{3,2,1,0:T(8,128)(2,1)S(1)} %get-tuple-element.30), channel_id=1, source_target_pairs={{0,64},{16,80},{32,96},{48,112},{64,128},{80,144},{96,160},{112,17... | collective-permute-start | bytes 393224 | tf_op jit(solution)/shard_map/ppermute | solution.py:455
  78.1 10.5 %collective-permute-start.8 = (bf16[2,8,16,256]{3,2,1,0:T(8,128)(2,1)S(1)}, bf16[2,8,16,256]{3,2,1,0:T(8,128)(2,1)S(1)}, u32[]{:S(2)}, u32[]{:S(2)}) collective-permute-start(bf16[2,8,16,256]{3,2,1,0:T(8,128)(2,1)S(1)} %get-tuple-element.31), channel_id=1, source_target_pairs={{0,192},{16,208},{32,224},{48,240},{64,0},{80,16},{96,32},{112,48}... | collective-permute-start | bytes 393224 | tf_op jit(solution)/shard_map/ppermute | solution.py:455
  79.0 9.6 %collective-permute-start.7 = (bf16[2,8,16,256]{3,2,1,0:T(8,128)(2,1)S(1)}, bf16[2,8,16,256]{3,2,1,0:T(8,128)(2,1)S(1)}, u32[]{:S(2)}, u32[]{:S(2)}) collective-permute-start(bf16[2,8,16,256]{3,2,1,0:T(8,128)(2,1)S(1)} %get-tuple-element.32), channel_id=1, source_target_pairs={{0,128},{16,144},{32,160},{48,176},{64,192},{80,208},{96,224},{112... | collective-permute-start | bytes 393224 | tf_op jit(solution)/shard_map/ppermute | solution.py:455
  84.0 9.0 %collective-permute-start.4 = (bf16[8,16,256]{2,1,0:T(8,128)(2,1)S(1)}, bf16[8,16,256]{2,1,0:T(8,128)(2,1)S(1)}, u32[]{:S(2)}, u32[]{:S(2)}) collective-permute-start(bf16[8,16,256]{2,1,0:T(8,128)(2,1)S(1)} %slice_bitcast_fusion.2), channel_id=1, source_target_pairs={{0,32},{16,48},{32,0},{48,16},{64,96},{80,112},{96,64},{112,80},{1... | collective-permute-start | bytes 196616 | tf_op jit(solution)/shard_map/ppermute | solution.py:455
  88.7 8.7 %collective-permute-start.9 = (bf16[8,16,256]{2,1,0:T(8,128)(2,1)S(1)}, bf16[8,16,256]{2,1,0:T(8,128)(2,1)S(1)}, u32[]{:S(2)}, u32[]{:S(2)}) collective-permute-start(bf16[8,16,256]{2,1,0:T(8,128)(2,1)S(1)} %slice_bitcast_fusion), channel_id=1, source_target_pairs={{0,32},{16,48},{32,0},{48,16},{64,96},{80,112},{96,64},{112,80},{1... | collective-permute-start | bytes 196616 | tf_op jit(solution)/shard_map/ppermute | solution.py:455

commit v6 on v5

--- a/solution.py
+++ b/solution.py
@@ -19,7 +19,7 @@
 PACKED = 144
 MARK = 140
 KEPT = 80
-PIECE = 2
+PIECE = 1
 COLS = 256
 U0 = 512
 U1 = 8
@@ -80,7 +80,7 @@
     for g in range(size // 2):
         lo = 2 * KEPT * g // 128 * 128
         back.append(whole[2 * S * g : 2 * S * (g + 1), lo : lo + 256].T)
-    return np.concatenate(to, axis=0), np.stack(back)
+    return np.concatenate(to, axis=0), np.concatenate(back, axis=1)
 
 
 def row_tables():
@@ -93,6 +93,27 @@
         [np.concatenate([c, -s], axis=2), np.concatenate([s, c], axis=2)], axis=1
     )
     return table[0::2], [table[k : 2 * PIECE + k : 2] for k in range(1, L0, 2 * PIECE)]
+
+
+def turned(quarters, back, scale):
+    h = math.pi / 2
+    whole = jnp.floor(quarters + 0.5)
+    f = quarters - whole
+    count = whole.astype(jnp.int32) - back
+    t = f * f
+    sine, cosine = 0.0, 0.0
+    for n in (9, 7, 5, 3, 1):
+        sine = sine * t + (-1) ** (n // 2) * h**n / math.factorial(n) * scale
+    for n in (10, 8, 6, 4, 2, 0):
+        cosine = cosine * t + (-1) ** (n // 2) * h**n / math.factorial(n) * scale
+    sine = sine * f
+    odd = (count & 1) == 1
+    c = jnp.where(odd, sine, cosine)
+    s = jnp.where(odd, cosine, sine)
+    return (
+        jnp.where(((count + 1) & 2) == 2, -c, c),
+        jnp.where((count & 2) == 2, -s, s),
+    )
 
 
 def corner_marks(route_ref, offset_ref, n_tv):
@@ -199,7 +220,7 @@
 
 
 def add_blocks(
-    row_ref, got_ref, phase_ref, expand_ref, back_ref, coeff_ref, acc_ref, chunk, size, per_src
+    row_ref, got_ref, phase_ref, expand_ref, back_ref, coeff_ref, acc_ref, size
 ):
     sources = got_ref.shape[0]
     packed = got_ref[...].astype(jnp.float32)
@@ -213,18 +234,27 @@
     for g in range(size // 2):
         t = 2 * KEPT * g // S
         part = jnp.dot(
-            jnp.concatenate(tiles[t : t + 2], axis=1), back_ref[g], preferred_element_type=jnp.float32
+            jnp.concatenate(tiles[t : t + 2], axis=1),
+            back_ref[:, 256 * g : 256 * (g + 1)],
+            preferred_element_type=jnp.float32,
         )
         coeff_ref[:, :, 256 * g : 256 * (g + 1)] = part.astype(jnp.bfloat16).reshape(
             sources, STACK, 256
         )
     by_cos, by_sin = expand_ref[0], expand_ref[1]
 
+    lane = lax.broadcasted_iota(jnp.int32, (1, COLS), 1)
+    centre = (S - 1) / 2 * (lane.astype(jnp.float32) - (COLS - 1) / 2)
+
     def per_source(src, carry):
+        base = phase_ref[pl.ds(pl.multiple_of(src * size, size), size), :]
+        turns = (base[:, 0:1] * lane + base[:, 1:2]) & (N - 1)
+        phases = jnp.concatenate(
+            turned((turns.astype(jnp.float32) + centre) * (4.0 / N), 0, 1.0), axis=1
+        )
         for b in range(size):
-            g = src * per_src + chunk * size + b
-            row = row_ref[g]
-            ph = phase_ref[pl.ds(g, 1), :]
+            row = row_ref[src * size + b]
+            ph = phases[b : b + 1]
             c = jnp.concatenate([ph[:, :COLS], ph[:, :COLS]], axis=1)
             s = jnp.concatenate([ph[:, COLS:], ph[:, COLS:]], axis=1)
             weights = (by_cos * c + by_sin * s).astype(jnp.bfloat16)
@@ -236,15 +266,15 @@
                 acc_ref[q, pl.ds(row, S), :] += block[:, q * 128 : (q + 1) * 128]
         return carry
 
-    lax.fori_loop(0, sources, per_source, 0, unroll=2)
+    lax.fori_loop(0, sources, per_source, 0, unroll=4)
 
 
 def grid_kernel(
-    row_ref, got_ref, phase_ref, expand_ref, back_ref, out_ref, coeff_ref, *, chunk, size, per_src
+    row_ref, got_ref, phase_ref, expand_ref, back_ref, out_ref, coeff_ref, *, size
 ):
     out_ref[...] = jnp.zeros_like(out_ref)
     add_blocks(
-        row_ref, got_ref, phase_ref, expand_ref, back_ref, coeff_ref, out_ref, chunk, size, per_src
+        row_ref, got_ref, phase_ref, expand_ref, back_ref, coeff_ref, out_ref, size
     )
 
 
@@ -252,10 +282,10 @@
     return pltpu.VMEM((got.shape[0], STACK, size * S), jnp.bfloat16)
 
 
-def grid_chunk(rows, got, phase, expand, back, chunk, size, per_src):
+def grid_chunk(rows, got, phase, expand, back, size):
     vmem = pl.BlockSpec(memory_space=pltpu.VMEM)
     return pl.pallas_call(
-        functools.partial(grid_kernel, chunk=chunk, size=size, per_src=per_src),
+        functools.partial(grid_kernel, size=size),
         out_shape=jax.ShapeDtypeStruct((4, HALF, 128), jnp.float32),
         in_specs=[pl.BlockSpec(memory_space=pltpu.SMEM), vmem, vmem, vmem, vmem],
         out_specs=vmem,
@@ -298,7 +328,8 @@
         planar = jnp.dot(
             ref[k % ref.shape[0]], mid_ref[k], preferred_element_type=jnp.float32
         )
-        value = planar[:L1] * screen_ref[k, 0] - planar[L1:] * screen_ref[k, 1]
+        c, s = (screen_ref[k, p].astype(jnp.float32) for p in range(2))
+        value = planar[:L1] * c - planar[L1:] * s
         full_ref[:, k] = value.astype(jnp.bfloat16).reshape(L1 // 16, 16, COLS)
     for out_ref, which in ((keep_ref, 0), (send_ref, 1)):
         for i in range(out_ref.shape[0]):
@@ -306,20 +337,28 @@
 
 
 def even_kernel(
-    row_ref, place_ref, got_ref, phase_ref, expand_ref, back_ref, old_hbm, table_hbm, screen_hbm,
+    row_ref, place_ref, got_ref, phase_ref, expand_ref, old_hbm, table_hbm, screen_hbm,
     keep_ref, send_ref, odd_ref,
-    coeff_ref, acc_ref, old_ref, table_ref, mid_ref, screen_ref, full_ref, sems,
-    *, chunk, size, per_src,
+    back_ref, coeff_ref, acc_ref, old_ref, table_ref, mid_ref, screen_ref, full_ref, sems,
+    *, size,
 ):
     load_old = pltpu.make_async_copy(old_hbm, old_ref, sems.at[0])
-    load_table = pltpu.make_async_copy(table_hbm, table_ref, sems.at[1])
-    load_screen = pltpu.make_async_copy(screen_hbm, screen_ref, sems.at[2])
+    half = L0 // 2
+    load_back = pltpu.make_async_copy(
+        table_hbm.at[half, pl.ds(0, back_ref.shape[0])], back_ref, sems.at[3]
+    )
+    load_back.start()
+    load_table = pltpu.make_async_copy(table_hbm.at[pl.ds(0, half)], table_ref, sems.at[1])
+    load_screen = pltpu.make_async_copy(
+        screen_hbm.at[pl.ds(0, half)], screen_ref, sems.at[2]
+    )
     load_old.start()
     load_table.start()
     load_screen.start()
     acc_ref[...] = jnp.zeros_like(acc_ref)
+    load_back.wait()
     add_blocks(
-        row_ref, got_ref, phase_ref, expand_ref, back_ref, coeff_ref, acc_ref, chunk, size, per_src
+        row_ref, got_ref, phase_ref, expand_ref, back_ref, coeff_ref, acc_ref, size
     )
     load_old.wait()
 
@@ -346,7 +385,7 @@
                         ].astype(jnp.bfloat16)
         return carry
 
-    lax.fori_loop(0, U0 // 16, first_step, 0)
+    lax.fori_loop(0, U0 // 16, first_step, 0, unroll=2)
     load_table.wait()
     load_screen.wait()
     finish(place_ref, [table_ref], mid_ref, screen_ref, full_ref, keep_ref, send_ref)
@@ -358,7 +397,7 @@
 
 
 def make_image(
-    rows, place, got, phase, expand, back, old, tables, screens, chunk, size, per_src
+    rows, place, got, phase, expand, back_shape, old, tables, screens, size
 ):
     vmem = pl.BlockSpec(memory_space=pltpu.VMEM)
     smem = pl.BlockSpec(memory_space=pltpu.SMEM)
@@ -367,29 +406,30 @@
     piece = jax.ShapeDtypeStruct((place.shape[1], half, 16, COLS), jnp.bfloat16)
     mid = (half, 2 * U0, COLS)
     buffers = [
-        pltpu.VMEM(tables[0].shape, jnp.bfloat16),
-        pltpu.VMEM(screens[0].shape, jnp.float32),
+        pltpu.VMEM((half, *tables[0].shape[1:]), jnp.bfloat16),
+        pltpu.VMEM(screens[1].shape, jnp.bfloat16),
         pltpu.VMEM((16, half, 16, COLS), jnp.bfloat16),
     ]
     keep, send, odd = pl.pallas_call(
-        functools.partial(even_kernel, chunk=chunk, size=size, per_src=per_src),
+        functools.partial(even_kernel, size=size),
         out_shape=(piece, piece, jax.ShapeDtypeStruct(mid, jnp.bfloat16)),
-        in_specs=[smem, smem, vmem, vmem, vmem, vmem, hbm, hbm, hbm],
+        in_specs=[smem, smem, vmem, vmem, vmem, hbm, hbm, hbm],
         out_specs=(vmem, vmem, vmem),
         scratch_shapes=[
+            pltpu.VMEM(back_shape, jnp.bfloat16),
             coeff_scratch(got, size),
             pltpu.VMEM(old.shape, jnp.float32),
             pltpu.VMEM(old.shape, jnp.float32),
             buffers[0],
             pltpu.VMEM(mid, jnp.bfloat16),
             *buffers[1:],
-            pltpu.SemaphoreType.DMA((3,)),
+            pltpu.SemaphoreType.DMA((4,)),
         ],
         compiler_params=pltpu.CompilerParams(vmem_limit_bytes=EVEN_MIB * MIB),
         cost_estimate=pl.CostEstimate(
             flops=16 * 1024**3, bytes_accessed=24 * MIB, transcendentals=0
         ),
-    )(rows, place, got, phase, expand, back, old, tables[0], screens[0])
+    )(rows, place, got, phase, expand, old, tables[0], screens[0])
     keep_odd, send_odd = pl.pallas_call(
         odd_kernel,
         out_shape=(piece, piece),
@@ -408,37 +448,25 @@
     cell = 2.0 * FIELD / N
     col = base_ref[0] + lax.broadcasted_iota(jnp.int32, (1, COLS), 1)
     dm = col.astype(jnp.float32) * cell
-    h = math.pi / 2
     for half, out_ref in enumerate((even_ref, odd_ref)):
         l0 = 2 * pl.program_id(0) + half
         row = l0 + L0 * lax.broadcasted_iota(jnp.int32, (L1, 1), 0)
         dl = row.astype(jnp.float32) * cell
         lift = jnp.sqrt((1.0 - dl * dl) - dm * dm) - 1.0
         quarters = (4.0 * w_ref[0]) * lift
-        whole = jnp.floor(quarters + 0.5)
-        f = quarters - whole
-        count = whole.astype(jnp.int32) - (row + col)
-        t = f * f
-        sine, cosine = 0.0, 0.0
-        for n in (9, 7, 5, 3, 1):
-            sine = sine * t + (-1) ** (n // 2) * h**n / math.factorial(n) * scale
-        for n in (10, 8, 6, 4, 2, 0):
-            cosine = cosine * t + (-1) ** (n // 2) * h**n / math.factorial(n) * scale
-        sine = sine * f
-        odd = (count & 1) == 1
-        c = jnp.where(odd, sine, cosine)
-        s = jnp.where(odd, cosine, sine)
-        out_ref[0, 0] = jnp.where(((count + 1) & 2) == 2, -c, c)
-        out_ref[0, 1] = jnp.where((count & 2) == 2, -s, s)
+        c, s = turned(quarters, row + col, scale)
+        out_ref[0, 0] = c.astype(out_ref.dtype)
+        out_ref[0, 1] = s.astype(out_ref.dtype)
 
 
 def make_screen(base, w, scale):
     smem = pl.BlockSpec(memory_space=pltpu.SMEM)
-    half = jax.ShapeDtypeStruct((L0 // 2, 2, L1, COLS), jnp.float32)
+    half = jax.ShapeDtypeStruct((L0 // 2, 2, L1, COLS), jnp.bfloat16)
+    wide = jax.ShapeDtypeStruct((2 * L0, 2, L1, COLS), jnp.bfloat16)
     spec = pl.BlockSpec((1, 2, L1, COLS), lambda k: (k, 0, 0, 0))
     return pl.pallas_call(
         functools.partial(screen_kernel, scale=scale),
-        out_shape=(half, half),
+        out_shape=(wide, half),
         grid=(L0 // 2,),
         in_specs=[smem, smem],
         out_specs=(spec, spec),
@@ -471,6 +499,9 @@
     project, expand = factor_tables(n_tu, n_tv)
     tables = row_tables()
     keep, back = keep_tables(size)
+    slab = np.zeros((1, *tables[0].shape[1:]), tables[0].dtype)
+    slab[0, : back.shape[0], : back.shape[1]] = back
+    tables = (np.concatenate([tables[0], slab]), tables[1])
 
     owner = lax.axis_index(("tu", "tv"))
     col_base = owner * COLS
@@ -489,14 +520,12 @@
         )
     marks = got[0][:, MARK, : 4 * blocks].astype(jnp.int32).reshape(owners, 2, 2, blocks)
     corners = marks[:, :, 0] * 64 + marks[:, :, 1]
-    rows = corners[:, 0, :].reshape(-1)
-    cols = corners[:, 1, :].reshape(-1)
-
-    lane = jnp.arange(COLS, dtype=jnp.int32)
-    turns = (cols[:, None] * (col_base + lane)[None, :] + N // 4 * rows[:, None]) % N
-    shift = (S - 1) / 2 * (lane.astype(jnp.float32) - (COLS - 1) / 2)
-    angle = (turns.astype(jnp.float32) + shift[None, :]) * (2.0 * math.pi / N)
-    phase = jnp.concatenate([jnp.cos(angle), jnp.sin(angle)], axis=1)
+    first = (corners[:, 1] * col_base + N // 4 * corners[:, 0]) % N
+    rows, phase = [], []
+    for chunk in range(CHUNKS):
+        mine = slice(chunk * size, (chunk + 1) * size)
+        rows.append(corners[:, 0, mine].reshape(-1))
+        phase.append(jnp.stack([corners[:, 1, mine], first[:, mine]], axis=2).reshape(-1, 2))
 
     me = lax.axis_index("wa")
     core, z_hi, x = me % 2, me // 2 % 2, me // 4
@@ -504,9 +533,9 @@
     pair = ((x + step // 2) % 4) * 4 + (z_hi ^ (step % 2)) * 2
     place = jnp.stack([pair + core, pair + (1 - core)])
 
-    acc = grid_chunk(rows, got[0], phase, expand, back, 0, size, blocks)
+    acc = grid_chunk(rows[0], got[0], phase[0], expand, back, size)
     halves = make_image(
-        rows, place, got[1], phase, expand, back, acc, tables, screens, 1, size, blocks
+        rows[1], place, got[1], phase[1], expand, back.shape, acc, tables, screens, size
     )
     if planes != 16:
         return halves

time: 99.1 us -> 96.6 us (0.975)
  other arithmetic: 2.6 us -> 0.59 us
  local copies, waits for them, and re-layouts: 4.79 us -> 3.38 us
    unnamed x22, local copies, waits for them, and re-layouts: 3.34 us -> 0.05 us
    another operation x1 -> x8, local copies, waits for them, and re-layouts: 0.08 us -> 1.91 us  [the longest x6 1.2 us: body(): jnp.stack([corners[:, 1, mine], first[:, mine]], axis=2).reshape(-1, 2)]
    cos x1 -> x0, other arithmetic: 1.14 us -> none  [body(): phase = jnp.concatenate([jnp.cos(angle), jnp.sin(angle)], axis=1)]
  transfers between devices with their start and end apart: 12 -> 12, of which waited for: 4 -> 4; matrix products, arithmetic and copies ran while one was open for 3% -> 3% of each run, Pallas kernels for 28% -> 29%
where the time goes in v6:
time: 96.6 us; the launch traced here: 96.2 us
  Pallas kernels  47.5 us (49%)
  starting transfers between devices  31.5 us (33%)
  waiting for transfers between devices  12.2 us (13%)
  local copies, waits for them, and re-layouts  3.38 us (3%)
  between operations  1.01 us (1%)
    ppermute x10, starting transfers between devices, shifted(): return lax.ppermute(values, 'wa', pairs).astype(jnp.float32)  17.9 us
    pallas_call x1, Pallas kernels, make_image(): pl.pallas_call(functools.partial(even_kernel, size=size), out_shape=(piec...  15.3 us
    all_to_all x2, starting transfers between devices, body(): lax.all_to_all(coeffs, ('tv', 'tu'), split_axis=0, concat_axis=0, tiled=T...  13.6 us
    pallas_call x1, Pallas kernels, grid_chunk(): pl.pallas_call(functools.partial(grid_kernel, size=size), out_shape=jax.S...  11.5 us
    pallas_call x1, Pallas kernels, make_screen(): pl.pallas_call(functools.partial(screen_kernel, scale=scale), out_shape=(...  9.06 us
    pallas_call x2, Pallas kernels, project_chunk(): pl.pallas_call(functools.partial(project_kernel, first=chunk * size, n_tv...  8.49 us
    ppermute x10, waiting for transfers between devices, shifted(): return lax.ppermute(values, 'wa', pairs).astype(jnp.float32)  7.39 us
    all_to_all x2, waiting for transfers between devices, body(): lax.all_to_all(coeffs, ('tv', 'tu'), split_axis=0, concat_axis=0, tiled=T...  4.84 us
  transfers between devices with their start and end apart: 12, of which 4 were waited for; matrix products, arithmetic and copies ran while one was open for 3% of the time, Pallas kernels for 29%

profile of v6, /device:TPU:2, one launch (start us, length us, event | category | flops | bytes accessed | tf_op | source)
XLA Modules:
  0.0 96.2 jit_solution(6352940411895038099)
XLA Ops:
  0.0 4.3 %shard_map.190 = bf16[16,144,128]{2,1,0:T(8,128)(2,1)} custom-call(s32[16]{0:T(128)} %count_ref.3, s32[1,16]{1,0:T(1,128)} %bitcast.41, s32[2,16]{1,0:T(2,128)} %bitcast.39, bf16[16,256,128]{2,1,0:T(8,128)(2,1)} %ku_ref.3, bf16[16,256,128]{2,1,0:T(8,128)(2,1)} %kv_ref.3, bf16[16,2,256]{2,1,0:T(2,128)(2,1)} %vis_ref.3, ...), custom_call_target="tpu_custom_call" | custom-call | flops 402653184 | bytes 2097152 | tf_op jit(solution)/shard_map/pallas_call | solution.py:198
  4.3 8.6 %all-to-all-start = ((bf16[16,144,128]{2,1,0:T(8,128)(2,1)}), bf16[16,144,128]{2,1,0:T(8,128)(2,1)S(1)}, u32[]{:S(2)}, u32[]{:S(2)}) async-start(bf16[16,144,128]{2,1,0:T(8,128)(2,1)} %shard_map.190), calls=%async_computation | async-start | bytes 1179648 | tf_op jit(solution)/shard_map/all_to_all | solution.py:519
  13.6 9.1 %shard_map.192 = (bf16[32,2,256,256]{3,2,1,0:T(8,128)(2,1)}, bf16[8,2,256,256]{3,2,1,0:T(8,128)(2,1)}) custom-call(s32[1]{0:T(128)} %bitcast.3.base_ref, f32[1]{0:T(128)S(6)} %copy.47.w_ref), custom_call_target="tpu_custom_call" | custom-call | flops 41943040 | bytes 8388608 | tf_op jit(solution)/shard_map/pallas_call | solution.py:467
  22.7 4.2 %shard_map.191 = bf16[16,144,128]{2,1,0:T(8,128)(2,1)} custom-call(s32[16]{0:T(128)} %count_ref.3, s32[1,16]{1,0:T(1,128)} %bitcast.42, s32[2,16]{1,0:T(2,128)} %bitcast.40, bf16[16,256,128]{2,1,0:T(8,128)(2,1)} %ku_ref.3, bf16[16,256,128]{2,1,0:T(8,128)(2,1)} %kv_ref.3, bf16[16,2,256]{2,1,0:T(2,128)(2,1)} %vis_ref.3, ...), custom_call_target="tpu_custom_call" | custom-call | flops 402653184 | bytes 2097152 | tf_op jit(solution)/shard_map/pallas_call | solution.py:198
  26.9 2.6 %all-to-all-done.got_ref = bf16[16,144,128]{2,1,0:T(8,128)(2,1)S(1)} async-done(((bf16[16,144,128]{2,1,0:T(8,128)(2,1)}), bf16[16,144,128]{2,1,0:T(8,128)(2,1)S(1)}, u32[]{:S(2)}, u32[]{:S(2)}) %all-to-all-start) | async-done | bytes 589856 | tf_op jit(solution)/shard_map/all_to_all | solution.py:519
  29.5 4.9 %all-to-all-start.1 = ((bf16[16,144,128]{2,1,0:T(8,128)(2,1)}), bf16[16,144,128]{2,1,0:T(8,128)(2,1)S(1)}, u32[]{:S(2)}, u32[]{:S(2)}) async-start(bf16[16,144,128]{2,1,0:T(8,128)(2,1)} %shard_map.191), calls=%async_computation.1 | async-start | bytes 1179648 | tf_op jit(solution)/shard_map/all_to_all | solution.py:519
  35.1 0.6 reshape_squeeze.7.row_ref
  36.0 0.7 copy.36.phase_ref
  36.8 11.5 %shard_map.193.old_hbm = f32[4,4096,128]{2,1,0:T(8,128)} custom-call(s32[128]{0:T(128)} %reshape_squeeze.7.row_ref, bf16[16,144,128]{2,1,0:T(8,128)(2,1)} %copy-done.10, s32[128,2]{1,0:T(8,128)} %copy.36.phase_ref, f32[2,32,512]{2,1,0:T(8,128)} %constant.132.clone.expand_ref, bf16[256,1024]{1,0:T(8,128)(2,1)} %constant.133.clone.back_ref), custom_call_target="tpu_custom_call" | custom-call | flops 4294967296 | bytes 12582912 | tf_op jit(solution)/shard_map/pallas_call | solution.py:287
  48.2 2.2 %all-to-all-done.1.got_ref = bf16[16,144,128]{2,1,0:T(8,128)(2,1)S(1)} async-done(((bf16[16,144,128]{2,1,0:T(8,128)(2,1)}), bf16[16,144,128]{2,1,0:T(8,128)(2,1)S(1)}, u32[]{:S(2)}, u32[]{:S(2)}) %all-to-all-start.1) | async-done | bytes 589856 | tf_op jit(solution)/shard_map/all_to_all | solution.py:519
  50.5 15.3 %shard_map.194 = (bf16[8,8,16,256]{3,2,1,0:T(8,128)(2,1)S(1)}, bf16[8,8,16,256]{3,2,1,0:T(8,128)(2,1)S(1)}, bf16[8,1024,256]{2,1,0:T(8,128)(2,1)S(1)}) custom-call(s32[128]{0:T(128)S(1)} %reshape_squeeze.6.row_ref, s32[2,8]{1,0:T(2,128)S(1)} %pad_add_fusion.place_ref, bf16[16,144,128]{2,1,0:T(8,128)(2,1)S(1)} %all-to-all-done.1.got_ref, ...), custom_call_target="tpu_custom_call" | custom-call | flops 17179869184 | bytes 25165824 | tf_op jit(solution)/shard_map/pallas_call | solution.py:413
  66.3 3.2 %shard_map.195 = (bf16[8,8,16,256]{3,2,1,0:T(8,128)(2,1)S(1)}, bf16[8,8,16,256]{3,2,1,0:T(8,128)(2,1)S(1)}) custom-call(s32[2,8]{1,0:T(2,128)S(1)} %pad_add_fusion.place_ref, bf16[8,1024,256]{2,1,0:T(8,128)(2,1)S(1)} %get-tuple-element.21.mid_ref, bf16[8,2,256,256]{3,2,1,0:T(8,128)(2,1)S(1)} %copy-done.9, bf16[1,512,1024]{2,1,0:T(8,128)(2,1)S(1)} %copy-done.7, ...), custom_call_target="tpu_custom_call" | custom-call | flops 4294967296 | bytes 12582912 | tf_op jit(solution)/shard_map/pallas_call | solution.py:433
  69.4 0.6 collective-permute-start.5
  70.2 1.6 %collective-permute-start.1 = (bf16[2,8,16,256]{3,2,1,0:T(8,128)(2,1)S(1)}, bf16[2,8,16,256]{3,2,1,0:T(8,128)(2,1)S(1)}, u32[]{:S(2)}, u32[]{:S(2)}) collective-permute-start(bf16[2,8,16,256]{3,2,1,0:T(8,128)(2,1)S(1)} %get-tuple-element.25), channel_id=1, source_target_pairs={{0,64},{16,80},{32,96},{48,112},{64,128},{80,144},{96,160},{112,17... | collective-permute-start | bytes 393224 | tf_op jit(solution)/shard_map/ppermute | solution.py:483
  71.8 0.5 collective-permute-start.3
  72.3 2.1 %collective-permute-start.2 = (bf16[2,8,16,256]{3,2,1,0:T(8,128)(2,1)S(1)}, bf16[2,8,16,256]{3,2,1,0:T(8,128)(2,1)S(1)}, u32[]{:S(2)}, u32[]{:S(2)}) collective-permute-start(bf16[2,8,16,256]{3,2,1,0:T(8,128)(2,1)S(1)} %get-tuple-element.27), channel_id=1, source_target_pairs={{0,128},{16,144},{32,160},{48,176},{64,192},{80,208},{96,224},{112... | collective-permute-start | bytes 393224 | tf_op jit(solution)/shard_map/ppermute | solution.py:483
  74.6 1.2 %collective-permute-start.6 = (bf16[2,8,16,256]{3,2,1,0:T(8,128)(2,1)S(1)}, bf16[2,8,16,256]{3,2,1,0:T(8,128)(2,1)S(1)}, u32[]{:S(2)}, u32[]{:S(2)}) collective-permute-start(bf16[2,8,16,256]{3,2,1,0:T(8,128)(2,1)S(1)} %get-tuple-element.28), channel_id=1, source_target_pairs={{0,64},{16,80},{32,96},{48,112},{64,128},{80,144},{96,160},{112,17... | collective-permute-start | bytes 393224 | tf_op jit(solution)/shard_map/ppermute | solution.py:483
  75.8 0.9 collective-permute-start.8
  76.7 1.9 %collective-permute-start.7 = (bf16[2,8,16,256]{3,2,1,0:T(8,128)(2,1)S(1)}, bf16[2,8,16,256]{3,2,1,0:T(8,128)(2,1)S(1)}, u32[]{:S(2)}, u32[]{:S(2)}) collective-permute-start(bf16[2,8,16,256]{3,2,1,0:T(8,128)(2,1)S(1)} %get-tuple-element.30), channel_id=1, source_target_pairs={{0,128},{16,144},{32,160},{48,176},{64,192},{80,208},{96,224},{112... | collective-permute-start | bytes 393224 | tf_op jit(solution)/shard_map/ppermute | solution.py:483
  78.6 3.0 %collective-permute-done.2 = bf16[2,8,16,256]{3,2,1,0:T(8,128)(2,1)S(1)} collective-permute-done((bf16[2,8,16,256]{3,2,1,0:T(8,128)(2,1)S(1)}, bf16[2,8,16,256]{3,2,1,0:T(8,128)(2,1)S(1)}, u32[]{:S(2)}, u32[]{:S(2)}) %collective-permute-start.2) | collective-permute-done | bytes 131104 | tf_op jit(solution)/shard_map/ppermute | solution.py:483
  81.7 4.6 %collective-permute-start.4 = (bf16[8,16,256]{2,1,0:T(8,128)(2,1)S(1)}, bf16[8,16,256]{2,1,0:T(8,128)(2,1)S(1)}, u32[]{:S(2)}, u32[]{:S(2)}) collective-permute-start(bf16[8,16,256]{2,1,0:T(8,128)(2,1)S(1)} %slice_bitcast_fusion.2), channel_id=1, source_target_pairs={{0,32},{16,48},{32,0},{48,16},{64,96},{80,112},{96,64},{112,80},{1... | collective-permute-start | bytes 196616 | tf_op jit(solution)/shard_map/ppermute | solution.py:483
  86.4 4.3 %collective-permute-start.9 = (bf16[8,16,256]{2,1,0:T(8,128)(2,1)S(1)}, bf16[8,16,256]{2,1,0:T(8,128)(2,1)S(1)}, u32[]{:S(2)}, u32[]{:S(2)}) collective-permute-start(bf16[8,16,256]{2,1,0:T(8,128)(2,1)S(1)} %slice_bitcast_fusion), channel_id=1, source_target_pairs={{0,32},{16,48},{32,0},{48,16},{64,96},{80,112},{96,64},{112,80},{1... | collective-permute-start | bytes 196616 | tf_op jit(solution)/shard_map/ppermute | solution.py:483
  90.7 4.4 %collective-permute-done.9 = bf16[8,16,256]{2,1,0:T(8,128)(2,1)S(1)} collective-permute-done((bf16[8,16,256]{2,1,0:T(8,128)(2,1)S(1)}, bf16[8,16,256]{2,1,0:T(8,128)(2,1)S(1)}, u32[]{:S(2)}, u32[]{:S(2)}) %collective-permute-start.9) | collective-permute-done | bytes 65568 | tf_op jit(solution)/shard_map/ppermute | solution.py:483
  95.3 0.9 reshape.155
  (60 shorter events, 2.0 us)
Async XLA Ops:
  4.3 25.2 %all-to-all-start = ((bf16[16,144,128]{2,1,0:T(8,128)(2,1)}), bf16[16,144,128]{2,1,0:T(8,128)(2,1)S(1)}, u32[]{:S(2)}, u32[]{:S(2)}) async-start(bf16[16,144,128]{2,1,0:T(8,128)(2,1)} %shard_map.190), calls=%async_computation | async-start | bytes 1179648 | tf_op jit(solution)/shard_map/all_to_all | solution.py:519
  29.5 7.2 %copy-start.10 = (bf16[16,144,128]{2,1,0:T(8,128)(2,1)}, bf16[16,144,128]{2,1,0:T(8,128)(2,1)S(1)}, u32[]{:S(2)}) copy-start(bf16[16,144,128]{2,1,0:T(8,128)(2,1)S(1)} %all-to-all-done.got_ref) | copy-start | bytes 1769476
  29.5 21.0 %all-to-all-start.1 = ((bf16[16,144,128]{2,1,0:T(8,128)(2,1)}), bf16[16,144,128]{2,1,0:T(8,128)(2,1)S(1)}, u32[]{:S(2)}, u32[]{:S(2)}) async-start(bf16[16,144,128]{2,1,0:T(8,128)(2,1)} %shard_map.191), calls=%async_computation.1 | async-start | bytes 1179648 | tf_op jit(solution)/shard_map/all_to_all | solution.py:519
  34.4 16.0 %copy-start.8 = (f32[2,32,512]{2,1,0:T(8,128)S(1)}, f32[2,32,512]{2,1,0:T(8,128)}, u32[]{:S(2)}) copy-start(f32[2,32,512]{2,1,0:T(8,128)} %constant.132.clone.expand_ref) | copy-start | bytes 393220
  48.2 17.9 %copy-start = (bf16[1,512,1024]{2,1,0:T(8,128)(2,1)S(1)}, bf16[1,512,1024]{2,1,0:T(8,128)(2,1)}, u32[]{:S(2)}) copy-start(bf16[1,512,1024]{2,1,0:T(8,128)(2,1)} %constant.142.clone.refs_7_) | copy-start | bytes 3145732
  48.2 17.9 %copy-start.1 = (bf16[1,512,1024]{2,1,0:T(8,128)(2,1)S(1)}, bf16[1,512,1024]{2,1,0:T(8,128)(2,1)}, u32[]{:S(2)}) copy-start(bf16[1,512,1024]{2,1,0:T(8,128)(2,1)} %constant.141.clone.refs_6_) | copy-start | bytes 3145732
  50.5 15.7 %copy-start.2 = (bf16[1,512,1024]{2,1,0:T(8,128)(2,1)S(1)}, bf16[1,512,1024]{2,1,0:T(8,128)(2,1)}, u32[]{:S(2)}) copy-start(bf16[1,512,1024]{2,1,0:T(8,128)(2,1)} %constant.140.clone.refs_5_) | copy-start | bytes 3145732
  50.5 15.7 %copy-start.3 = (bf16[1,512,1024]{2,1,0:T(8,128)(2,1)S(1)}, bf16[1,512,1024]{2,1,0:T(8,128)(2,1)}, u32[]{:S(2)}) copy-start(bf16[1,512,1024]{2,1,0:T(8,128)(2,1)} %constant.139.clone.refs_4_) | copy-start | bytes 3145732
  50.5 15.7 %copy-start.4 = (bf16[1,512,1024]{2,1,0:T(8,128)(2,1)S(1)}, bf16[1,512,1024]{2,1,0:T(8,128)(2,1)}, u32[]{:S(2)}) copy-start(bf16[1,512,1024]{2,1,0:T(8,128)(2,1)} %constant.138.clone.refs_3_) | copy-start | bytes 3145732
  50.5 15.7 %copy-start.5 = (bf16[1,512,1024]{2,1,0:T(8,128)(2,1)S(1)}, bf16[1,512,1024]{2,1,0:T(8,128)(2,1)}, u32[]{:S(2)}) copy-start(bf16[1,512,1024]{2,1,0:T(8,128)(2,1)} %constant.137.clone.refs_2_) | copy-start | bytes 3145732
  50.5 15.7 %copy-start.6 = (bf16[1,512,1024]{2,1,0:T(8,128)(2,1)S(1)}, bf16[1,512,1024]{2,1,0:T(8,128)(2,1)}, u32[]{:S(2)}) copy-start(bf16[1,512,1024]{2,1,0:T(8,128)(2,1)} %constant.136.clone.refs_1_) | copy-start | bytes 3145732
  50.5 15.7 %copy-start.7 = (bf16[1,512,1024]{2,1,0:T(8,128)(2,1)S(1)}, bf16[1,512,1024]{2,1,0:T(8,128)(2,1)}, u32[]{:S(2)}) copy-start(bf16[1,512,1024]{2,1,0:T(8,128)(2,1)} %constant.135.clone.refs_0_) | copy-start | bytes 3145732
  50.5 15.7 %copy-start.9 = (bf16[8,2,256,256]{3,2,1,0:T(8,128)(2,1)S(1)}, bf16[8,2,256,256]{3,2,1,0:T(8,128)(2,1)}, u32[]{:S(2)}) copy-start(bf16[8,2,256,256]{3,2,1,0:T(8,128)(2,1)} %get-tuple-element.22.screen_ref) | copy-start | bytes 6291460
  65.9 4.1 %collective-permute-start = (bf16[8,8,16,256]{3,2,1,0:T(8,128)(2,1)S(1)}, bf16[8,8,16,256]{3,2,1,0:T(8,128)(2,1)S(1)}, u32[]{:S(2)}, u32[]{:S(2)}) collective-permute-start(bf16[8,8,16,256]{3,2,1,0:T(8,128)(2,1)S(1)} %get-tuple-element.20), channel_id=1, source_target_pairs={{0,16},{16,0},{32,48},{48,32},{64,80},{80,64},{96,112},{112,96},{1... | collective-permute-start | bytes 1572872 | tf_op jit(solution)/shard_map/ppermute | solution.py:483
  69.4 5.0 %collective-permute-start.5 = (bf16[8,8,16,256]{3,2,1,0:T(8,128)(2,1)S(1)}, bf16[8,8,16,256]{3,2,1,0:T(8,128)(2,1)S(1)}, u32[]{:S(2)}, u32[]{:S(2)}) collective-permute-start(bf16[8,8,16,256]{3,2,1,0:T(8,128)(2,1)S(1)} %get-tuple-element.24), channel_id=1, source_target_pairs={{0,16},{16,0},{32,48},{48,32},{64,80},{80,64},{96,112},{112,96},{1... | collective-permute-start | bytes 1572872 | tf_op jit(solution)/shard_map/ppermute | solution.py:483
  70.2 6.5 %collective-permute-start.1 = (bf16[2,8,16,256]{3,2,1,0:T(8,128)(2,1)S(1)}, bf16[2,8,16,256]{3,2,1,0:T(8,128)(2,1)S(1)}, u32[]{:S(2)}, u32[]{:S(2)}) collective-permute-start(bf16[2,8,16,256]{3,2,1,0:T(8,128)(2,1)S(1)} %get-tuple-element.25), channel_id=1, source_target_pairs={{0,64},{16,80},{32,96},{48,112},{64,128},{80,144},{96,160},{112,17... | collective-permute-start | bytes 393224 | tf_op jit(solution)/shard_map/ppermute | solution.py:483
  71.8 6.8 %collective-permute-start.3 = (bf16[2,8,16,256]{3,2,1,0:T(8,128)(2,1)S(1)}, bf16[2,8,16,256]{3,2,1,0:T(8,128)(2,1)S(1)}, u32[]{:S(2)}, u32[]{:S(2)}) collective-permute-start(bf16[2,8,16,256]{3,2,1,0:T(8,128)(2,1)S(1)} %get-tuple-element.26), channel_id=1, source_target_pairs={{0,192},{16,208},{32,224},{48,240},{64,0},{80,16},{96,32},{112,48}... | collective-permute-start | bytes 393224 | tf_op jit(solution)/shard_map/ppermute | solution.py:483
  72.3 9.3 %collective-permute-start.2 = (bf16[2,8,16,256]{3,2,1,0:T(8,128)(2,1)S(1)}, bf16[2,8,16,256]{3,2,1,0:T(8,128)(2,1)S(1)}, u32[]{:S(2)}, u32[]{:S(2)}) collective-permute-start(bf16[2,8,16,256]{3,2,1,0:T(8,128)(2,1)S(1)} %get-tuple-element.27), channel_id=1, source_target_pairs={{0,128},{16,144},{32,160},{48,176},{64,192},{80,208},{96,224},{112... | collective-permute-start | bytes 393224 | tf_op jit(solution)/shard_map/ppermute | solution.py:483
  74.6 11.7 %collective-permute-start.6 = (bf16[2,8,16,256]{3,2,1,0:T(8,128)(2,1)S(1)}, bf16[2,8,16,256]{3,2,1,0:T(8,128)(2,1)S(1)}, u32[]{:S(2)}, u32[]{:S(2)}) collective-permute-start(bf16[2,8,16,256]{3,2,1,0:T(8,128)(2,1)S(1)} %get-tuple-element.28), channel_id=1, source_target_pairs={{0,64},{16,80},{32,96},{48,112},{64,128},{80,144},{96,160},{112,17... | collective-permute-start | bytes 393224 | tf_op jit(solution)/shard_map/ppermute | solution.py:483
  75.8 10.5 %collective-permute-start.8 = (bf16[2,8,16,256]{3,2,1,0:T(8,128)(2,1)S(1)}, bf16[2,8,16,256]{3,2,1,0:T(8,128)(2,1)S(1)}, u32[]{:S(2)}, u32[]{:S(2)}) collective-permute-start(bf16[2,8,16,256]{3,2,1,0:T(8,128)(2,1)S(1)} %get-tuple-element.29), channel_id=1, source_target_pairs={{0,192},{16,208},{32,224},{48,240},{64,0},{80,16},{96,32},{112,48}... | collective-permute-start | bytes 393224 | tf_op jit(solution)/shard_map/ppermute | solution.py:483
  76.7 9.6 %collective-permute-start.7 = (bf16[2,8,16,256]{3,2,1,0:T(8,128)(2,1)S(1)}, bf16[2,8,16,256]{3,2,1,0:T(8,128)(2,1)S(1)}, u32[]{:S(2)}, u32[]{:S(2)}) collective-permute-start(bf16[2,8,16,256]{3,2,1,0:T(8,128)(2,1)S(1)} %get-tuple-element.30), channel_id=1, source_target_pairs={{0,128},{16,144},{32,160},{48,176},{64,192},{80,208},{96,224},{112... | collective-permute-start | bytes 393224 | tf_op jit(solution)/shard_map/ppermute | solution.py:483
  81.7 9.0 %collective-permute-start.4 = (bf16[8,16,256]{2,1,0:T(8,128)(2,1)S(1)}, bf16[8,16,256]{2,1,0:T(8,128)(2,1)S(1)}, u32[]{:S(2)}, u32[]{:S(2)}) collective-permute-start(bf16[8,16,256]{2,1,0:T(8,128)(2,1)S(1)} %slice_bitcast_fusion.2), channel_id=1, source_target_pairs={{0,32},{16,48},{32,0},{48,16},{64,96},{80,112},{96,64},{112,80},{1... | collective-permute-start | bytes 196616 | tf_op jit(solution)/shard_map/ppermute | solution.py:483
  86.4 8.7 %collective-permute-start.9 = (bf16[8,16,256]{2,1,0:T(8,128)(2,1)S(1)}, bf16[8,16,256]{2,1,0:T(8,128)(2,1)S(1)}, u32[]{:S(2)}, u32[]{:S(2)}) collective-permute-start(bf16[8,16,256]{2,1,0:T(8,128)(2,1)S(1)} %slice_bitcast_fusion), channel_id=1, source_target_pairs={{0,32},{16,48},{32,0},{48,16},{64,96},{80,112},{96,64},{112,80},{1... | collective-permute-start | bytes 196616 | tf_op jit(solution)/shard_map/ppermute | solution.py:483

commit v7 on v6

--- a/solution.py
+++ b/solution.py
@@ -266,7 +266,7 @@
                 acc_ref[q, pl.ds(row, S), :] += block[:, q * 128 : (q + 1) * 128]
         return carry
 
-    lax.fori_loop(0, sources, per_source, 0, unroll=4)
+    lax.fori_loop(0, sources, per_source, 0, unroll=8)
 
 
 def grid_kernel(
@@ -385,7 +385,7 @@
                         ].astype(jnp.bfloat16)
         return carry
 
-    lax.fori_loop(0, U0 // 16, first_step, 0, unroll=2)
+    lax.fori_loop(0, U0 // 16, first_step, 0, unroll=4)
     load_table.wait()
     load_screen.wait()
     finish(place_ref, [table_ref], mid_ref, screen_ref, full_ref, keep_ref, send_ref)
@@ -488,7 +488,34 @@
         shifted(total[step], lambda i, step=step: (i + 4 * step) % planes) for step in (1, 2, 3)
     ]
     total = (total[0].astype(jnp.float32) + got[0] + got[1] + got[2]).astype(jnp.bfloat16)
-    return total[0].astype(jnp.float32) + shifted(total[1], lambda i: i ^ 2)
+    return total, lax.ppermute(total[1], "wa", [(i, i ^ 2) for i in range(planes)])
+
+
+def last_kernel(even_ref, even_got_ref, odd_ref, odd_got_ref, out_ref, rows_ref):
+    for half, (ref, got_ref) in enumerate(((even_ref, even_got_ref), (odd_ref, odd_got_ref))):
+        for k in range(L0 // 2):
+            value = ref[0, k].astype(jnp.float32) + got_ref[k].astype(jnp.float32)
+            for c in range(2):
+                rows_ref[c, pl.ds(2 * k + half, 16, stride=L0), :] = value[
+                    :, 128 * c : 128 * (c + 1)
+                ]
+    for c in range(2):
+        out_ref[:, 128 * c : 128 * (c + 1)] = rows_ref[c]
+
+
+def last_sum(even, odd):
+    vmem = pl.BlockSpec(memory_space=pltpu.VMEM)
+    return pl.pallas_call(
+        last_kernel,
+        out_shape=jax.ShapeDtypeStruct((L0 * 16, COLS), jnp.float32),
+        in_specs=[vmem] * 4,
+        out_specs=vmem,
+        scratch_shapes=[pltpu.VMEM((2, L0 * 16, 128), jnp.float32)],
+        compiler_params=pltpu.CompilerParams(vmem_limit_bytes=16 * MIB),
+        cost_estimate=pl.CostEstimate(
+            flops=10**8, bytes_accessed=MIB, transcendentals=0
+        ),
+    )(*even, *odd)
 
 
 def body(kernel_u, kernel_v, visibilities, vis_count, tile_route, block_offset, plane_w):
@@ -540,7 +567,7 @@
     if planes != 16:
         return halves
     even, odd = (sum_planes(keep, send, planes) for keep, send in halves)
-    return jnp.stack([even, odd], axis=1).transpose(2, 0, 1, 3).reshape(L0 * 16, COLS)
+    return last_sum(even, odd)
 
 
 def solution(mesh):

time: 96.6 us -> 95.8 us (level)
  local copies, waits for them, and re-layouts: 3.38 us -> 2.29 us
    ppermute x0 -> x2, starting transfers between devices: none -> 8.9 us  [sum_planes(): lax.ppermute(total[1], 'wa', [(i, i ^ 2) for i in range(planes)])]
    ppermute x10 -> x8, starting transfers between devices: 17.9 us -> 9.11 us  [shifted(): return lax.ppermute(values, 'wa', pairs).astype(jnp.float32)]
    ppermute x10 -> x8, waiting for transfers between devices: 7.39 us -> 2.98 us  [shifted(): return lax.ppermute(values, 'wa', pairs).astype(jnp.float32)]
    ppermute x0 -> x2, waiting for transfers between devices: none -> 4.38 us  [sum_planes(): lax.ppermute(total[1], 'wa', [(i, i ^ 2) for i in range(planes)])]
where the time goes in v7:
time: 95.8 us; the launch traced here: 95.4 us
  Pallas kernels  47.4 us (49%)
  starting transfers between devices  31.6 us (33%)
  waiting for transfers between devices  12.6 us (13%)
  local copies, waits for them, and re-layouts  2.29 us (2%)
  between operations  0.98 us (1%)
    pallas_call x1, Pallas kernels, make_image(): pl.pallas_call(functools.partial(even_kernel, size=size), out_shape=(piec...  14.8 us
    all_to_all x2, starting transfers between devices, body(): lax.all_to_all(coeffs, ('tv', 'tu'), split_axis=0, concat_axis=0, tiled=T...  13.6 us
    pallas_call x1, Pallas kernels, grid_chunk(): pl.pallas_call(functools.partial(grid_kernel, size=size), out_shape=jax.S...  11.1 us
    ppermute x8, starting transfers between devices, shifted(): return lax.ppermute(values, 'wa', pairs).astype(jnp.float32)  9.11 us
    pallas_call x1, Pallas kernels, make_screen(): pl.pallas_call(functools.partial(screen_kernel, scale=scale), out_shape=(...  9.06 us
    ppermute x2, starting transfers between devices, sum_planes(): lax.ppermute(total[1], 'wa', [(i, i ^ 2) for i in range(planes)])  8.9 us
    pallas_call x2, Pallas kernels, project_chunk(): pl.pallas_call(functools.partial(project_kernel, first=chunk * size, n_tv...  8.49 us
    all_to_all x2, waiting for transfers between devices, body(): lax.all_to_all(coeffs, ('tv', 'tu'), split_axis=0, concat_axis=0, tiled=T...  5.22 us
  transfers between devices with their start and end apart: 12, of which 4 were waited for; matrix products, arithmetic and copies ran while one was open for 3% of the time, Pallas kernels for 29%

profile of v7, /device:TPU:2, one launch (start us, length us, event | category | flops | bytes accessed | tf_op | source)
XLA Modules:
  0.0 95.4 jit_solution(14856175002567817451)
XLA Ops:
  0.0 4.3 %shard_map.190 = bf16[16,144,128]{2,1,0:T(8,128)(2,1)} custom-call(s32[16]{0:T(128)} %count_ref.3, s32[1,16]{1,0:T(1,128)} %bitcast.25, s32[2,16]{1,0:T(2,128)} %bitcast.23, bf16[16,256,128]{2,1,0:T(8,128)(2,1)} %ku_ref.3, bf16[16,256,128]{2,1,0:T(8,128)(2,1)} %kv_ref.3, bf16[16,2,256]{2,1,0:T(2,128)(2,1)} %vis_ref.3, ...), custom_call_target="tpu_custom_call" | custom-call | flops 402653184 | bytes 2097152 | tf_op jit(solution)/shard_map/pallas_call | solution.py:198
  4.3 8.6 %all-to-all-start = ((bf16[16,144,128]{2,1,0:T(8,128)(2,1)}), bf16[16,144,128]{2,1,0:T(8,128)(2,1)S(1)}, u32[]{:S(2)}, u32[]{:S(2)}) async-start(bf16[16,144,128]{2,1,0:T(8,128)(2,1)} %shard_map.190), calls=%async_computation | async-start | bytes 1179648 | tf_op jit(solution)/shard_map/all_to_all | solution.py:546
  13.6 9.1 %shard_map.192 = (bf16[32,2,256,256]{3,2,1,0:T(8,128)(2,1)}, bf16[8,2,256,256]{3,2,1,0:T(8,128)(2,1)}) custom-call(s32[1]{0:T(128)} %bitcast.3.base_ref, f32[1]{0:T(128)S(6)} %copy.45.w_ref), custom_call_target="tpu_custom_call" | custom-call | flops 41943040 | bytes 8388608 | tf_op jit(solution)/shard_map/pallas_call | solution.py:467
  22.7 4.2 %shard_map.191 = bf16[16,144,128]{2,1,0:T(8,128)(2,1)} custom-call(s32[16]{0:T(128)} %count_ref.3, s32[1,16]{1,0:T(1,128)} %bitcast.26, s32[2,16]{1,0:T(2,128)} %bitcast.24, bf16[16,256,128]{2,1,0:T(8,128)(2,1)} %ku_ref.3, bf16[16,256,128]{2,1,0:T(8,128)(2,1)} %kv_ref.3, bf16[16,2,256]{2,1,0:T(2,128)(2,1)} %vis_ref.3, ...), custom_call_target="tpu_custom_call" | custom-call | flops 402653184 | bytes 2097152 | tf_op jit(solution)/shard_map/pallas_call | solution.py:198
  26.9 2.6 %all-to-all-done.got_ref = bf16[16,144,128]{2,1,0:T(8,128)(2,1)S(1)} async-done(((bf16[16,144,128]{2,1,0:T(8,128)(2,1)}), bf16[16,144,128]{2,1,0:T(8,128)(2,1)S(1)}, u32[]{:S(2)}, u32[]{:S(2)}) %all-to-all-start) | async-done | bytes 589856 | tf_op jit(solution)/shard_map/all_to_all | solution.py:546
  29.5 4.9 %all-to-all-start.1 = ((bf16[16,144,128]{2,1,0:T(8,128)(2,1)}), bf16[16,144,128]{2,1,0:T(8,128)(2,1)S(1)}, u32[]{:S(2)}, u32[]{:S(2)}) async-start(bf16[16,144,128]{2,1,0:T(8,128)(2,1)} %shard_map.191), calls=%async_computation.1 | async-start | bytes 1179648 | tf_op jit(solution)/shard_map/all_to_all | solution.py:546
  35.1 0.6 reshape_squeeze.7.row_ref
  36.0 0.7 copy.35.phase_ref
  36.8 11.1 %shard_map.193.old_hbm = f32[4,4096,128]{2,1,0:T(8,128)} custom-call(s32[128]{0:T(128)} %reshape_squeeze.7.row_ref, bf16[16,144,128]{2,1,0:T(8,128)(2,1)} %copy-done.10, s32[128,2]{1,0:T(8,128)} %copy.35.phase_ref, f32[2,32,512]{2,1,0:T(8,128)} %constant.132.clone.expand_ref, bf16[256,1024]{1,0:T(8,128)(2,1)} %constant.133.clone.back_ref), custom_call_target="tpu_custom_call" | custom-call | flops 4294967296 | bytes 12582912 | tf_op jit(solution)/shard_map/pallas_call | solution.py:287
  47.9 2.6 %all-to-all-done.1.got_ref = bf16[16,144,128]{2,1,0:T(8,128)(2,1)S(1)} async-done(((bf16[16,144,128]{2,1,0:T(8,128)(2,1)}), bf16[16,144,128]{2,1,0:T(8,128)(2,1)S(1)}, u32[]{:S(2)}, u32[]{:S(2)}) %all-to-all-start.1) | async-done | bytes 589856 | tf_op jit(solution)/shard_map/all_to_all | solution.py:546
  50.5 14.8 %shard_map.194 = (bf16[8,8,16,256]{3,2,1,0:T(8,128)(2,1)S(1)}, bf16[8,8,16,256]{3,2,1,0:T(8,128)(2,1)S(1)}, bf16[8,1024,256]{2,1,0:T(8,128)(2,1)S(1)}) custom-call(s32[128]{0:T(128)S(1)} %reshape_squeeze.6.row_ref, s32[2,8]{1,0:T(2,128)S(1)} %pad_add_fusion.place_ref, bf16[16,144,128]{2,1,0:T(8,128)(2,1)S(1)} %all-to-all-done.1.got_ref, ...), custom_call_target="tpu_custom_call" | custom-call | flops 17179869184 | bytes 25165824 | tf_op jit(solution)/shard_map/pallas_call | solution.py:413
  65.8 3.2 %shard_map.195 = (bf16[8,8,16,256]{3,2,1,0:T(8,128)(2,1)S(1)}, bf16[8,8,16,256]{3,2,1,0:T(8,128)(2,1)S(1)}) custom-call(s32[2,8]{1,0:T(2,128)S(1)} %pad_add_fusion.place_ref, bf16[8,1024,256]{2,1,0:T(8,128)(2,1)S(1)} %get-tuple-element.21.mid_ref, bf16[8,2,256,256]{3,2,1,0:T(8,128)(2,1)S(1)} %copy-done.9, bf16[1,512,1024]{2,1,0:T(8,128)(2,1)S(1)} %copy-done.7, ...), custom_call_target="tpu_custom_call" | custom-call | flops 4294967296 | bytes 12582912 | tf_op jit(solution)/shard_map/pallas_call | solution.py:433
  68.9 0.6 collective-permute-start.5
  69.7 1.6 %collective-permute-start.1 = (bf16[2,8,16,256]{3,2,1,0:T(8,128)(2,1)S(1)}, bf16[2,8,16,256]{3,2,1,0:T(8,128)(2,1)S(1)}, u32[]{:S(2)}, u32[]{:S(2)}) collective-permute-start(bf16[2,8,16,256]{3,2,1,0:T(8,128)(2,1)S(1)} %get-tuple-element.28), channel_id=1, source_target_pairs={{0,64},{16,80},{32,96},{48,112},{64,128},{80,144},{96,160},{112,17... | collective-permute-start | bytes 393224 | tf_op jit(solution)/shard_map/ppermute | solution.py:483
  71.2 0.5 collective-permute-start.3
  71.8 2.1 %collective-permute-start.2 = (bf16[2,8,16,256]{3,2,1,0:T(8,128)(2,1)S(1)}, bf16[2,8,16,256]{3,2,1,0:T(8,128)(2,1)S(1)}, u32[]{:S(2)}, u32[]{:S(2)}) collective-permute-start(bf16[2,8,16,256]{3,2,1,0:T(8,128)(2,1)S(1)} %get-tuple-element.30), channel_id=1, source_target_pairs={{0,128},{16,144},{32,160},{48,176},{64,192},{80,208},{96,224},{112... | collective-permute-start | bytes 393224 | tf_op jit(solution)/shard_map/ppermute | solution.py:483
  74.1 1.2 %collective-permute-start.6 = (bf16[2,8,16,256]{3,2,1,0:T(8,128)(2,1)S(1)}, bf16[2,8,16,256]{3,2,1,0:T(8,128)(2,1)S(1)}, u32[]{:S(2)}, u32[]{:S(2)}) collective-permute-start(bf16[2,8,16,256]{3,2,1,0:T(8,128)(2,1)S(1)} %get-tuple-element.25), channel_id=1, source_target_pairs={{0,64},{16,80},{32,96},{48,112},{64,128},{80,144},{96,160},{112,17... | collective-permute-start | bytes 393224 | tf_op jit(solution)/shard_map/ppermute | solution.py:483
  75.3 0.9 collective-permute-start.8
  76.2 1.9 %collective-permute-start.7 = (bf16[2,8,16,256]{3,2,1,0:T(8,128)(2,1)S(1)}, bf16[2,8,16,256]{3,2,1,0:T(8,128)(2,1)S(1)}, u32[]{:S(2)}, u32[]{:S(2)}) collective-permute-start(bf16[2,8,16,256]{3,2,1,0:T(8,128)(2,1)S(1)} %get-tuple-element.27), channel_id=1, source_target_pairs={{0,128},{16,144},{32,160},{48,176},{64,192},{80,208},{96,224},{112... | collective-permute-start | bytes 393224 | tf_op jit(solution)/shard_map/ppermute | solution.py:483
  78.1 3.0 %collective-permute-done.2 = bf16[2,8,16,256]{3,2,1,0:T(8,128)(2,1)S(1)} collective-permute-done((bf16[2,8,16,256]{3,2,1,0:T(8,128)(2,1)S(1)}, bf16[2,8,16,256]{3,2,1,0:T(8,128)(2,1)S(1)}, u32[]{:S(2)}, u32[]{:S(2)}) %collective-permute-start.2) | collective-permute-done | bytes 131104 | tf_op jit(solution)/shard_map/ppermute | solution.py:483
  81.2 4.6 %collective-permute-start.4 = (bf16[8,16,256]{2,1,0:T(8,128)(2,1)S(1)}, bf16[8,16,256]{2,1,0:T(8,128)(2,1)S(1)}, u32[]{:S(2)}, u32[]{:S(2)}) collective-permute-start(bf16[8,16,256]{2,1,0:T(8,128)(2,1)S(1)} %slice_bitcast_fusion.1), channel_id=1, source_target_pairs={{0,32},{16,48},{32,0},{48,16},{64,96},{80,112},{96,64},{112,80},{1... | collective-permute-start | bytes 196616 | tf_op jit(solution)/shard_map/ppermute | solution.py:491
  85.9 4.3 %collective-permute-start.9 = (bf16[8,16,256]{2,1,0:T(8,128)(2,1)S(1)}, bf16[8,16,256]{2,1,0:T(8,128)(2,1)S(1)}, u32[]{:S(2)}, u32[]{:S(2)}) collective-permute-start(bf16[8,16,256]{2,1,0:T(8,128)(2,1)S(1)} %slice_bitcast_fusion), channel_id=1, source_target_pairs={{0,32},{16,48},{32,0},{48,16},{64,96},{80,112},{96,64},{112,80},{1... | collective-permute-start | bytes 196616 | tf_op jit(solution)/shard_map/ppermute | solution.py:491
  90.2 4.4 %collective-permute-done.9.odd_got_ref = bf16[8,16,256]{2,1,0:T(8,128)(2,1)S(1)} collective-permute-done((bf16[8,16,256]{2,1,0:T(8,128)(2,1)S(1)}, bf16[8,16,256]{2,1,0:T(8,128)(2,1)S(1)}, u32[]{:S(2)}, u32[]{:S(2)}) %collective-permute-start.9) | collective-permute-done | bytes 65568 | tf_op jit(solution)/shard_map/ppermute | solution.py:491
  94.6 0.8 shard_map.196
  (56 shorter events, 1.8 us)
Async XLA Ops:
  4.3 25.2 %all-to-all-start = ((bf16[16,144,128]{2,1,0:T(8,128)(2,1)}), bf16[16,144,128]{2,1,0:T(8,128)(2,1)S(1)}, u32[]{:S(2)}, u32[]{:S(2)}) async-start(bf16[16,144,128]{2,1,0:T(8,128)(2,1)} %shard_map.190), calls=%async_computation | async-start | bytes 1179648 | tf_op jit(solution)/shard_map/all_to_all | solution.py:546
  29.5 7.2 %copy-start.10 = (bf16[16,144,128]{2,1,0:T(8,128)(2,1)}, bf16[16,144,128]{2,1,0:T(8,128)(2,1)S(1)}, u32[]{:S(2)}) copy-start(bf16[16,144,128]{2,1,0:T(8,128)(2,1)S(1)} %all-to-all-done.got_ref) | copy-start | bytes 1769476
  29.5 21.0 %all-to-all-start.1 = ((bf16[16,144,128]{2,1,0:T(8,128)(2,1)}), bf16[16,144,128]{2,1,0:T(8,128)(2,1)S(1)}, u32[]{:S(2)}, u32[]{:S(2)}) async-start(bf16[16,144,128]{2,1,0:T(8,128)(2,1)} %shard_map.191), calls=%async_computation.1 | async-start | bytes 1179648 | tf_op jit(solution)/shard_map/all_to_all | solution.py:546
  34.5 16.0 %copy-start.8 = (f32[2,32,512]{2,1,0:T(8,128)S(1)}, f32[2,32,512]{2,1,0:T(8,128)}, u32[]{:S(2)}) copy-start(f32[2,32,512]{2,1,0:T(8,128)} %constant.132.clone.expand_ref) | copy-start | bytes 393220
  47.9 17.8 %copy-start = (bf16[1,512,1024]{2,1,0:T(8,128)(2,1)S(1)}, bf16[1,512,1024]{2,1,0:T(8,128)(2,1)}, u32[]{:S(2)}) copy-start(bf16[1,512,1024]{2,1,0:T(8,128)(2,1)} %constant.142.clone.refs_7_) | copy-start | bytes 3145732
  47.9 17.8 %copy-start.1 = (bf16[1,512,1024]{2,1,0:T(8,128)(2,1)S(1)}, bf16[1,512,1024]{2,1,0:T(8,128)(2,1)}, u32[]{:S(2)}) copy-start(bf16[1,512,1024]{2,1,0:T(8,128)(2,1)} %constant.141.clone.refs_6_) | copy-start | bytes 3145732
  50.5 15.2 %copy-start.2 = (bf16[1,512,1024]{2,1,0:T(8,128)(2,1)S(1)}, bf16[1,512,1024]{2,1,0:T(8,128)(2,1)}, u32[]{:S(2)}) copy-start(bf16[1,512,1024]{2,1,0:T(8,128)(2,1)} %constant.140.clone.refs_5_) | copy-start | bytes 3145732
  50.5 15.2 %copy-start.3 = (bf16[1,512,1024]{2,1,0:T(8,128)(2,1)S(1)}, bf16[1,512,1024]{2,1,0:T(8,128)(2,1)}, u32[]{:S(2)}) copy-start(bf16[1,512,1024]{2,1,0:T(8,128)(2,1)} %constant.139.clone.refs_4_) | copy-start | bytes 3145732
  50.5 15.2 %copy-start.4 = (bf16[1,512,1024]{2,1,0:T(8,128)(2,1)S(1)}, bf16[1,512,1024]{2,1,0:T(8,128)(2,1)}, u32[]{:S(2)}) copy-start(bf16[1,512,1024]{2,1,0:T(8,128)(2,1)} %constant.138.clone.refs_3_) | copy-start | bytes 3145732
  50.5 15.2 %copy-start.5 = (bf16[1,512,1024]{2,1,0:T(8,128)(2,1)S(1)}, bf16[1,512,1024]{2,1,0:T(8,128)(2,1)}, u32[]{:S(2)}) copy-start(bf16[1,512,1024]{2,1,0:T(8,128)(2,1)} %constant.137.clone.refs_2_) | copy-start | bytes 3145732
  50.5 15.2 %copy-start.6 = (bf16[1,512,1024]{2,1,0:T(8,128)(2,1)S(1)}, bf16[1,512,1024]{2,1,0:T(8,128)(2,1)}, u32[]{:S(2)}) copy-start(bf16[1,512,1024]{2,1,0:T(8,128)(2,1)} %constant.136.clone.refs_1_) | copy-start | bytes 3145732
  50.5 15.2 %copy-start.7 = (bf16[1,512,1024]{2,1,0:T(8,128)(2,1)S(1)}, bf16[1,512,1024]{2,1,0:T(8,128)(2,1)}, u32[]{:S(2)}) copy-start(bf16[1,512,1024]{2,1,0:T(8,128)(2,1)} %constant.135.clone.refs_0_) | copy-start | bytes 3145732
  50.5 15.2 %copy-start.9 = (bf16[8,2,256,256]{3,2,1,0:T(8,128)(2,1)S(1)}, bf16[8,2,256,256]{3,2,1,0:T(8,128)(2,1)}, u32[]{:S(2)}) copy-start(bf16[8,2,256,256]{3,2,1,0:T(8,128)(2,1)} %get-tuple-element.22.screen_ref) | copy-start | bytes 6291460
  65.4 4.1 %collective-permute-start = (bf16[8,8,16,256]{3,2,1,0:T(8,128)(2,1)S(1)}, bf16[8,8,16,256]{3,2,1,0:T(8,128)(2,1)S(1)}, u32[]{:S(2)}, u32[]{:S(2)}) collective-permute-start(bf16[8,8,16,256]{3,2,1,0:T(8,128)(2,1)S(1)} %get-tuple-element.20), channel_id=1, source_target_pairs={{0,16},{16,0},{32,48},{48,32},{64,80},{80,64},{96,112},{112,96},{1... | collective-permute-start | bytes 1572872 | tf_op jit(solution)/shard_map/ppermute | solution.py:483
  68.9 5.0 %collective-permute-start.5 = (bf16[8,8,16,256]{3,2,1,0:T(8,128)(2,1)S(1)}, bf16[8,8,16,256]{3,2,1,0:T(8,128)(2,1)S(1)}, u32[]{:S(2)}, u32[]{:S(2)}) collective-permute-start(bf16[8,8,16,256]{3,2,1,0:T(8,128)(2,1)S(1)} %get-tuple-element.24), channel_id=1, source_target_pairs={{0,16},{16,0},{32,48},{48,32},{64,80},{80,64},{96,112},{112,96},{1... | collective-permute-start | bytes 1572872 | tf_op jit(solution)/shard_map/ppermute | solution.py:483
  69.7 6.5 %collective-permute-start.1 = (bf16[2,8,16,256]{3,2,1,0:T(8,128)(2,1)S(1)}, bf16[2,8,16,256]{3,2,1,0:T(8,128)(2,1)S(1)}, u32[]{:S(2)}, u32[]{:S(2)}) collective-permute-start(bf16[2,8,16,256]{3,2,1,0:T(8,128)(2,1)S(1)} %get-tuple-element.28), channel_id=1, source_target_pairs={{0,64},{16,80},{32,96},{48,112},{64,128},{80,144},{96,160},{112,17... | collective-permute-start | bytes 393224 | tf_op jit(solution)/shard_map/ppermute | solution.py:483
  71.2 6.9 %collective-permute-start.3 = (bf16[2,8,16,256]{3,2,1,0:T(8,128)(2,1)S(1)}, bf16[2,8,16,256]{3,2,1,0:T(8,128)(2,1)S(1)}, u32[]{:S(2)}, u32[]{:S(2)}) collective-permute-start(bf16[2,8,16,256]{3,2,1,0:T(8,128)(2,1)S(1)} %get-tuple-element.29), channel_id=1, source_target_pairs={{0,192},{16,208},{32,224},{48,240},{64,0},{80,16},{96,32},{112,48}... | collective-permute-start | bytes 393224 | tf_op jit(solution)/shard_map/ppermute | solution.py:483
  71.8 9.3 %collective-permute-start.2 = (bf16[2,8,16,256]{3,2,1,0:T(8,128)(2,1)S(1)}, bf16[2,8,16,256]{3,2,1,0:T(8,128)(2,1)S(1)}, u32[]{:S(2)}, u32[]{:S(2)}) collective-permute-start(bf16[2,8,16,256]{3,2,1,0:T(8,128)(2,1)S(1)} %get-tuple-element.30), channel_id=1, source_target_pairs={{0,128},{16,144},{32,160},{48,176},{64,192},{80,208},{96,224},{112... | collective-permute-start | bytes 393224 | tf_op jit(solution)/shard_map/ppermute | solution.py:483
  74.1 11.7 %collective-permute-start.6 = (bf16[2,8,16,256]{3,2,1,0:T(8,128)(2,1)S(1)}, bf16[2,8,16,256]{3,2,1,0:T(8,128)(2,1)S(1)}, u32[]{:S(2)}, u32[]{:S(2)}) collective-permute-start(bf16[2,8,16,256]{3,2,1,0:T(8,128)(2,1)S(1)} %get-tuple-element.25), channel_id=1, source_target_pairs={{0,64},{16,80},{32,96},{48,112},{64,128},{80,144},{96,160},{112,17... | collective-permute-start | bytes 393224 | tf_op jit(solution)/shard_map/ppermute | solution.py:483
  75.3 10.5 %collective-permute-start.8 = (bf16[2,8,16,256]{3,2,1,0:T(8,128)(2,1)S(1)}, bf16[2,8,16,256]{3,2,1,0:T(8,128)(2,1)S(1)}, u32[]{:S(2)}, u32[]{:S(2)}) collective-permute-start(bf16[2,8,16,256]{3,2,1,0:T(8,128)(2,1)S(1)} %get-tuple-element.26), channel_id=1, source_target_pairs={{0,192},{16,208},{32,224},{48,240},{64,0},{80,16},{96,32},{112,48}... | collective-permute-start | bytes 393224 | tf_op jit(solution)/shard_map/ppermute | solution.py:483
  76.2 9.6 %collective-permute-start.7 = (bf16[2,8,16,256]{3,2,1,0:T(8,128)(2,1)S(1)}, bf16[2,8,16,256]{3,2,1,0:T(8,128)(2,1)S(1)}, u32[]{:S(2)}, u32[]{:S(2)}) collective-permute-start(bf16[2,8,16,256]{3,2,1,0:T(8,128)(2,1)S(1)} %get-tuple-element.27), channel_id=1, source_target_pairs={{0,128},{16,144},{32,160},{48,176},{64,192},{80,208},{96,224},{112... | collective-permute-start | bytes 393224 | tf_op jit(solution)/shard_map/ppermute | solution.py:483
  81.2 9.0 %collective-permute-start.4 = (bf16[8,16,256]{2,1,0:T(8,128)(2,1)S(1)}, bf16[8,16,256]{2,1,0:T(8,128)(2,1)S(1)}, u32[]{:S(2)}, u32[]{:S(2)}) collective-permute-start(bf16[8,16,256]{2,1,0:T(8,128)(2,1)S(1)} %slice_bitcast_fusion.1), channel_id=1, source_target_pairs={{0,32},{16,48},{32,0},{48,16},{64,96},{80,112},{96,64},{112,80},{1... | collective-permute-start | bytes 196616 | tf_op jit(solution)/shard_map/ppermute | solution.py:491
  85.9 8.7 %collective-permute-start.9 = (bf16[8,16,256]{2,1,0:T(8,128)(2,1)S(1)}, bf16[8,16,256]{2,1,0:T(8,128)(2,1)S(1)}, u32[]{:S(2)}, u32[]{:S(2)}) collective-permute-start(bf16[8,16,256]{2,1,0:T(8,128)(2,1)S(1)} %slice_bitcast_fusion), channel_id=1, source_target_pairs={{0,32},{16,48},{32,0},{48,16},{64,96},{80,112},{96,64},{112,80},{1... | collective-permute-start | bytes 196616 | tf_op jit(solution)/shard_map/ppermute | solution.py:491
